TPU v7x, 512 devices: a whole 4x8x8 slice. The times are simulated.
512 devices in a mesh: aperture: 64 (over y_hi, z, core), range: 8 (over y_lo, x).
Axes of the slice: x: 4, y: 8 (y_hi: 4, y_lo: 2; y = y_hi * 2 + y_lo), z: 8, core: 2. Of those that a mesh axis runs over, the one named last changes fastest.
Arguments:
- echoes: bfloat16 [2, 2048, 8192], P(None, 'aperture', 'range'), may hold values from -6 to 6
- transmit_chirp: bfloat16 [2, 512], replicated, may hold values from -0.1875 to 0.1875
- band_weights: float32 [4, 2, 2, 2048, 16], P(None, None, None, 'aperture'), may hold values from -0.75 to 0.75
- band_offsets: int32 [4, 2, 2048], P(None, None, 'aperture'), may hold values from -16 to 16
- band_widths: int32 [4, 2, 2048], P(None, None, 'aperture'), may hold values from 8 to 16
- child_rows: int32 [4, 2048], P(None, 'aperture'), may hold values from 0 to 15
Outputs:
- subimage: bfloat16 [2, 2048, 8192], P(None, 'aperture', 'range')
All inputs are finite; a program needn't handle non-finite values.
Results may differ from a plain program's by a relative error of at most 0.007.
Values may be sent and summed in bfloat16 or wider, within the bound.
No kernel may reach another device: no remote copies, remote signals or barrier semaphores. Data moves between devices by JAX's collectives and lax.ppermute only.
A program may use at most 128 MiB of HBM per device.

v0:
```python
import jax
import jax.numpy as jnp
from jax import lax
from jax.experimental import pallas as pl
from jax.experimental.pallas import tpu as pltpu
from jax.sharding import PartitionSpec as P

KERN = 16
SHIFT = 16
LEVELS = 4
TAPS = 512
HALF = 16
ROWS = 32
LANES = 128
BINS = 1024
RIM = 128
FRAME = BINS + 2 * RIM
HALO = RIM + TAPS // 2
SPAN = LANES + TAPS
COARSE = 6
FINE = 8
COLS = COARSE * 64
VMEM = 48 * 1024 * 1024


def column(row):
    lane = lax.broadcasted_iota(jnp.int32, (ROWS, ROWS), 1)
    sub = lax.broadcasted_iota(jnp.int32, (ROWS, ROWS), 0)
    wide = jnp.broadcast_to(row.astype(jnp.float32), (ROWS, ROWS))
    return jnp.sum(jnp.where(lane == sub, wide, 0.0), axis=1, keepdims=True)


def prepare_kernel(place, chirp, weights, offsets, widths, child, toeplitz, bank):
    device = place[0]

    taps = chirp[...].astype(jnp.float32)
    taps = jnp.concatenate([taps, jnp.zeros((2, SPAN - TAPS), jnp.float32)], axis=1)
    real = pltpu.roll(jnp.broadcast_to(taps[0:1], (LANES, SPAN)), 0, 1, stride=1, stride_axis=0)
    imag = pltpu.roll(jnp.broadcast_to(taps[1:2], (LANES, SPAN)), 0, 1, stride=1, stride_axis=0)
    toeplitz[0:LANES, 0:SPAN] = real.astype(jnp.bfloat16)
    toeplitz[0:LANES, SPAN : 2 * SPAN] = imag.astype(jnp.bfloat16)
    toeplitz[LANES : 2 * LANES, 0:SPAN] = (-imag).astype(jnp.bfloat16)
    toeplitz[LANES : 2 * LANES, SPAN : 2 * SPAN] = real.astype(jnp.bfloat16)

    lane = lax.broadcasted_iota(jnp.int32, (ROWS, LANES), 1)
    upper = lane >= 64
    shift_of = (lane & 63).astype(jnp.float32)
    col = lax.broadcasted_iota(jnp.int32, (256, COLS), 1)
    row = lax.broadcasted_iota(jnp.int32, (256, COLS), 0)
    wanted = row - (((col >> 4) & 3) * 64 + (col >> 6) * 8)
    child_of = (lax.broadcasted_iota(jnp.int32, (HALF, COLS), 1) & 15).astype(jnp.float32)

    stacks = []
    masks = []
    for level in range(LEVELS):
        side = (device >> level) & 1
        if level + 1 < LEVELS:
            first = ((device >> (level + 1)) & 1) == 1
        else:
            first = None

        def order(pair):
            if first is None:
                return pair
            low, high = pair[0:HALF], pair[HALF:ROWS]
            return jnp.concatenate(
                [jnp.where(first, high, low), jnp.where(first, low, high)], axis=0
            )

        spread = []
        for which in range(2):
            t = side if which == 0 else 1 - side
            offset = column(offsets[level, pl.ds(t, 1), :])
            width = column(widths[level, pl.ds(t, 1), :])
            wr = weights[level, t, 0]
            wi = weights[level, t, 1]
            tap = shift_of - (offset + float(SHIFT))
            tap = jnp.where(tap < width, tap, -1.0)
            total = jnp.zeros((ROWS, LANES), jnp.float32)
            for k in range(KERN):
                both = jnp.where(upper, wi[:, k : k + 1], wr[:, k : k + 1])
                total = jnp.where(tap == float(k), both, total)
            spread.append(total)
        to_real = order(
            jnp.concatenate([jnp.where(upper, -s, s) for s in spread], axis=1)
        )
        to_imag = order(jnp.concatenate([pltpu.roll(s, 64, 1) for s in spread], axis=1))
        both = jnp.concatenate([to_real, to_imag], axis=0)
        high = both.astype(jnp.bfloat16)
        low = (both - high.astype(jnp.float32)).astype(jnp.bfloat16)
        stacks += [high, low]
        chosen = order(jnp.broadcast_to(column(child[pl.ds(level, 1), :]), (ROWS, COLS)))
        mask = jnp.concatenate([chosen[0:HALF] == child_of, chosen[HALF:ROWS] == child_of], axis=0)
        masks.append(jnp.concatenate([mask, mask], axis=0))
    stack = jnp.concatenate(stacks, axis=0)
    for b in range(FINE):
        pick = (wanted == b).astype(jnp.float32).astype(jnp.bfloat16)
        out = jnp.dot(stack, pick, preferred_element_type=jnp.float32)
        for level in range(LEVELS):
            for part in range(2):
                piece = out[(level * 2 + part) * 64 : (level * 2 + part + 1) * 64]
                piece = jnp.where(masks[level], piece, 0.0).astype(jnp.bfloat16)
                bank[level, b * 64 : (b + 1) * 64, part * COLS : (part + 1) * COLS] = piece


def inside_mask(place, rows):
    position = place[1] * BINS - RIM
    bins = lax.broadcasted_iota(jnp.int32, (rows, FRAME), 1) + position
    return (bins >= 0) & (bins < place[2])


def compress_kernel(place, echoes, left, right, toeplitz, kept, sent, window):
    start = pl.multiple_of((place[0] & 1) * HALF, HALF)
    other = pl.multiple_of((1 - (place[0] & 1)) * HALF, HALF)
    blocks = FRAME // LANES
    tiles = SPAN // LANES
    first = HALO // LANES
    last = first + BINS // LANES
    for part in range(2):
        for half, at in enumerate((start, other)):
            for tile in range(blocks + tiles - 1):
                if tile < first:
                    piece = left[part, pl.ds(at, HALF), tile * LANES : (tile + 1) * LANES]
                elif tile < last:
                    spot = (tile - first) * LANES
                    piece = echoes[part, pl.ds(at, HALF), spot : spot + LANES]
                else:
                    spot = (tile - last) * LANES
                    piece = right[part, pl.ds(at, HALF), spot : spot + LANES]
                for block in range(max(0, tile - tiles + 1), min(blocks, tile + 1)):
                    spot = part * SPAN + (tile - block) * LANES
                    top = block * ROWS + half * HALF
                    window[top : top + HALF, spot : spot + LANES] = piece
    result = lax.dot_general(
        window[...], toeplitz[...], (((1,), (1,)), ((), ())), preferred_element_type=jnp.float32
    )
    position = place[1] * BINS - RIM
    for block in range(blocks):
        bins = lax.broadcasted_iota(jnp.int32, (ROWS, 2 * LANES), 1) & (LANES - 1)
        bins = bins + (position + block * LANES)
        inside = (bins >= 0) & (bins < place[2])
        piece = jnp.where(inside, result[block * ROWS : (block + 1) * ROWS], 0.0)
        piece = piece.astype(jnp.bfloat16)
        at = slice(block * LANES, (block + 1) * LANES)
        for part in range(2):
            lanes = slice(part * LANES, (part + 1) * LANES)
            kept[part * HALF : (part + 1) * HALF, at] = piece[0:HALF, lanes]
            sent[part * HALF : (part + 1) * HALF, at] = piece[HALF:ROWS, lanes]


def merged_beams(place, mine, theirs, bank, stack):
    source = jnp.concatenate([mine[...], theirs[...]], axis=0).astype(jnp.float32)
    for a in range(COARSE):
        shift = (24 - 8 * a) % FRAME
        moved = pltpu.roll(source, shift, 1) if shift else source
        moved = moved.astype(jnp.bfloat16)
        stack[a * 64 : (a + 1) * 64] = moved
        stack[COLS + a * 64 : COLS + (a + 1) * 64] = moved
    total = None
    product = jnp.dot(bank[0], stack[...], preferred_element_type=jnp.float32)
    for b in range(FINE):
        piece = product[b * 64 : (b + 1) * 64]
        if b:
            piece = pltpu.roll(piece, FRAME - b, 1)
        total = piece if total is None else total + piece
    return total


def level_kernel(place, mine, theirs, bank, kept, sent, stack):
    total = merged_beams(place, mine, theirs, bank, stack)
    total = jnp.where(inside_mask(place, 64), total, 0.0).astype(jnp.bfloat16)
    for part in range(2):
        kept[part * HALF : (part + 1) * HALF] = total[part * ROWS : part * ROWS + HALF]
        sent[part * HALF : (part + 1) * HALF] = total[part * ROWS + HALF : (part + 1) * ROWS]


def last_kernel(place, mine, theirs, bank, out, stack):
    total = merged_beams(place, mine, theirs, bank, stack)[:, RIM : RIM + BINS].astype(jnp.bfloat16)
    out[0] = total[0:ROWS]
    out[1] = total[ROWS : 2 * ROWS]


WHOLE = pl.BlockSpec(memory_space=pltpu.VMEM)
SCALARS = pl.BlockSpec(memory_space=pltpu.SMEM)
PARAMS = pltpu.CompilerParams(vmem_limit_bytes=VMEM)


def prepare(place, chirp, weights, offsets, widths, child):
    return pl.pallas_call(
        prepare_kernel,
        out_shape=(
            jax.ShapeDtypeStruct((2 * LANES, 2 * SPAN), jnp.bfloat16),
            jax.ShapeDtypeStruct((LEVELS, FINE * 64, 2 * COLS), jnp.bfloat16),
        ),
        in_specs=[SCALARS] + [WHOLE] * 5,
        out_specs=(WHOLE, WHOLE),
        compiler_params=PARAMS,
        cost_estimate=pl.CostEstimate(flops=4_000_000_000, bytes_accessed=4_000_000, transcendentals=0),
        name="prepare",
    )(place, chirp, weights, offsets, widths, child)


def compress(place, echoes, left, right, toeplitz):
    half = jax.ShapeDtypeStruct((2 * HALF, FRAME), jnp.bfloat16)
    return pl.pallas_call(
        compress_kernel,
        out_shape=(half, half),
        in_specs=[SCALARS] + [WHOLE] * 4,
        out_specs=(WHOLE, WHOLE),
        scratch_shapes=[pltpu.VMEM((FRAME // LANES * ROWS, 2 * SPAN), jnp.bfloat16)],
        compiler_params=PARAMS,
        name="compress",
    )(place, echoes, left, right, toeplitz)


def merge(place, mine, theirs, bank, level):
    half = jax.ShapeDtypeStruct((2 * HALF, FRAME), jnp.bfloat16)
    last = level + 1 == LEVELS
    return pl.pallas_call(
        last_kernel if last else level_kernel,
        grid=(1,),
        out_shape=jax.ShapeDtypeStruct((2, ROWS, BINS), jnp.bfloat16) if last else (half, half),
        in_specs=[
            SCALARS,
            WHOLE,
            WHOLE,
            pl.BlockSpec((1, FINE * 64, 2 * COLS), lambda i: (level, 0, 0)),
        ],
        out_specs=WHOLE if last else (WHOLE, WHOLE),
        scratch_shapes=[pltpu.VMEM((2 * COLS, FRAME), jnp.bfloat16)],
        compiler_params=PARAMS,
        name=f"merge_{level}",
    )(place, mine, theirs, bank)


def body(echoes, transmit_chirp, band_weights, band_offsets, band_widths, child_rows):
    count = lax.axis_size("range")
    right = lax.ppermute(echoes[:, :, :HALO], "range", [(i + 1, i) for i in range(count - 1)])
    left = lax.ppermute(echoes[:, :, BINS - HALO :], "range", [(i, i + 1) for i in range(count - 1)])
    place = jnp.stack(
        [lax.axis_index("aperture"), lax.axis_index("range"), jnp.int32(BINS * count)]
    ).astype(jnp.int32)
    toeplitz, bank = prepare(
        place, transmit_chirp, band_weights, band_offsets, band_widths, child_rows
    )
    kept, sent = compress(place, echoes, left, right, toeplitz)
    blocks = lax.axis_size("aperture")
    for level in range(LEVELS):
        theirs = lax.ppermute(sent, "aperture", [(i, i ^ (1 << level)) for i in range(blocks)])
        result = merge(place, kept, theirs, bank, level)
        if level + 1 < LEVELS:
            kept, sent = result
    return result


def solution(mesh):
    return jax.shard_map(
        body,
        mesh=mesh,
        in_specs=(
            P(None, "aperture", "range"),
            P(),
            P(None, None, None, "aperture", None),
            P(None, None, "aperture"),
            P(None, None, "aperture"),
            P(None, "aperture"),
        ),
        out_specs=P(None, "aperture", "range"),
        check_vma=False,
    )
```

profile of v0, /device:TPU:24, one launch (start us, length us, event | category | flops | bytes accessed | tf_op | source)
XLA Modules:
  0.0 57.5 jit_solution(2248984490658307538)
XLA Ops:
  0.0 0.8 %fusion = (bf16[2,32,384]{2,1,0:T(8,128)(2,1)S(1)}, bf16[2,32,384]{2,1,0:T(8,128)(2,1)S(1)}) fusion(bf16[2,32,1024]{2,1,0:T(8,128)(2,1)} %echoes.1), kind=kLoop, calls=%fused_computation.1 | loop fusion | bytes 196608 | tf_op jit(solution)/shard_map/slice | solution.py:238
  0.8 3.4 %collective-permute-start = (bf16[2,32,384]{2,1,0:T(8,128)(2,1)S(1)}, bf16[2,32,384]{2,1,0:T(8,128)(2,1)S(1)}, u32[]{:S(2)}, u32[]{:S(2)}) collective-permute-start(bf16[2,32,384]{2,1,0:T(8,128)(2,1)S(1)} %get-tuple-element.26), channel_id=1, source_target_pairs={{0,1},{1,2},{2,3},{3,4},{4,5},{5,6},{6,7},{8,9},{9,10},{10,11},{11... | collective-permute-start | bytes 147464 | tf_op jit(solution)/shard_map/ppermute | solution.py:239
  4.2 4.6 %collective-permute-start.1 = (bf16[2,32,384]{2,1,0:T(8,128)(2,1)S(1)}, bf16[2,32,384]{2,1,0:T(8,128)(2,1)S(1)}, u32[]{:S(2)}, u32[]{:S(2)}) collective-permute-start(bf16[2,32,384]{2,1,0:T(8,128)(2,1)S(1)} %get-tuple-element.25), channel_id=1, source_target_pairs={{1,0},{2,1},{3,2},{4,3},{5,4},{6,5},{7,6},{9,8},{10,9},{11,10},{12... | collective-permute-start | bytes 147464 | tf_op jit(solution)/shard_map/ppermute | solution.py:238
  8.8 1.0 %copy.7.weights = f32[4,2,2,32,16]{4,3,2,1,0:T(8,128)S(1)} copy(f32[4,2,2,32,16]{3,4,2,1,0:T(8,128)} %param.8) | data formatting | bytes 65536 | tf_op args[2]
  9.8 0.1 pad_add_fusion.place
  9.9 0.0 copy-start.1
  9.9 0.7 %copy-done.1 = s32[4,2,32]{2,1,0:T(2,128)S(1)} copy-done((s32[4,2,32]{2,1,0:T(2,128)S(1)}, s32[4,2,32]{2,1,0:T(2,128)}, u32[]{:S(2)}) %copy-start.1) | copy-done | bytes 1048
  10.6 0.0 copy-start.2
  10.6 0.7 %copy-done.2 = s32[4,2,32]{2,1,0:T(2,128)S(1)} copy-done((s32[4,2,32]{2,1,0:T(2,128)S(1)}, s32[4,2,32]{2,1,0:T(2,128)}, u32[]{:S(2)}) %copy-start.2) | copy-done | bytes 1048
  11.3 0.0 copy-start.3
  11.3 0.7 %copy-done.3 = bf16[2,512]{1,0:T(2,128)(2,1)S(1)} copy-done((bf16[2,512]{1,0:T(2,128)(2,1)S(1)}, bf16[2,512]{1,0:T(2,128)(2,1)}, u32[]{:S(2)}) %copy-start.3) | copy-done | bytes 2072
  12.0 0.0 copy-start.4
  12.0 0.7 %copy-done.4 = s32[4,32]{1,0:T(4,128)S(1)} copy-done((s32[4,32]{1,0:T(4,128)S(1)}, s32[4,32]{1,0:T(4,128)}, u32[]{:S(2)}) %copy-start.4) | copy-done | bytes 536
  12.7 0.0 copy-start
  12.7 3.7 %prepare.1 = (bf16[256,1280]{1,0:T(8,128)(2,1)S(1)}, bf16[4,512,768]{2,1,0:T(8,128)(2,1)S(1)}) custom-call(s32[3]{0:T(128)S(1)} %pad_add_fusion.place, bf16[2,512]{1,0:T(2,128)(2,1)S(1)} %copy-done.3, f32[4,2,2,32,16]{4,3,2,1,0:T(8,128)S(1)} %copy.7.weights, s32[4,2,32]{2,1,0:T(2,128)S(1)} %copy-done.1, s32[4,2,32]{2,1,0:T(2,128)S(1)} %copy-done.2, ...), custom_call_target="tpu_custom_call" | custom-call | flops 4000000000 | bytes 4000000 | tf_op jit(solution)/shard_map/prepare/pallas_call | solution.py:189
  16.4 0.0 collective-permute-done.left
  16.4 0.0 collective-permute-done.1.right
  16.4 0.0 copy-done
  16.4 1.0 %compress.1 = (bf16[32,1280]{1,0:T(8,128)(2,1)S(1)}, bf16[32,1280]{1,0:T(8,128)(2,1)S(1)}) custom-call(s32[3]{0:T(128)S(1)} %pad_add_fusion.place, bf16[2,32,1024]{2,1,0:T(8,128)(2,1)S(1)} %copy-done, bf16[2,32,384]{2,1,0:T(8,128)(2,1)S(1)} %collective-permute-done.left, bf16[2,32,384]{2,1,0:T(8,128)(2,1)S(1)} %collective-permute-done.1.right, ...), custom_call_target="tpu_custom_call" | custom-call | tf_op jit(solution)/shard_map/compress/pallas_call | solution.py:205
  17.4 1.9 %collective-permute-start.2 = (bf16[32,1280]{1,0:T(8,128)(2,1)S(1)}, bf16[32,1280]{1,0:T(8,128)(2,1)S(1)}, u32[]{:S(2)}, u32[]{:S(2)}) collective-permute-start(bf16[32,1280]{1,0:T(8,128)(2,1)S(1)} %get-tuple-element.17), channel_id=1, source_target_pairs={{0,8},{8,0},{16,24},{24,16},{32,40},{40,32},{48,56},{56,48},{64,72... | collective-permute-start | bytes 245768 | tf_op jit(solution)/shard_map/ppermute | solution.py:249
  19.3 1.2 %collective-permute-done.2.theirs = bf16[32,1280]{1,0:T(8,128)(2,1)S(1)} collective-permute-done((bf16[32,1280]{1,0:T(8,128)(2,1)S(1)}, bf16[32,1280]{1,0:T(8,128)(2,1)S(1)}, u32[]{:S(2)}, u32[]{:S(2)}) %collective-permute-start.2) | collective-permute-done | bytes 81952 | tf_op jit(solution)/shard_map/ppermute | solution.py:249
  20.6 2.1 %merge_0.1 = (bf16[32,1280]{1,0:T(8,128)(2,1)S(1)}, bf16[32,1280]{1,0:T(8,128)(2,1)S(1)}) custom-call(s32[3]{0:T(128)S(1)} %pad_add_fusion.place, bf16[32,1280]{1,0:T(8,128)(2,1)S(1)} %get-tuple-element.16.mine, bf16[32,1280]{1,0:T(8,128)(2,1)S(1)} %collective-permute-done.2.theirs, bf16[4,512,768]{2,1,0:T(8,128)(2,1)S(1)} %get-tuple-element.18.bank), custom_call_target="tpu_custom_call" | custom-call | tf_op jit(solution)/shard_map/merge_0/pallas_call | solution.py:219
  22.6 4.3 %collective-permute-start.3 = (bf16[32,1280]{1,0:T(8,128)(2,1)S(1)}, bf16[32,1280]{1,0:T(8,128)(2,1)S(1)}, u32[]{:S(2)}, u32[]{:S(2)}) collective-permute-start(bf16[32,1280]{1,0:T(8,128)(2,1)S(1)} %get-tuple-element.20), channel_id=1, source_target_pairs={{0,16},{8,24},{16,0},{24,8},{32,48},{40,56},{48,32},{56,40},{64,80... | collective-permute-start | bytes 245768 | tf_op jit(solution)/shard_map/ppermute | solution.py:249
  26.9 2.7 %collective-permute-done.3.theirs = bf16[32,1280]{1,0:T(8,128)(2,1)S(1)} collective-permute-done((bf16[32,1280]{1,0:T(8,128)(2,1)S(1)}, bf16[32,1280]{1,0:T(8,128)(2,1)S(1)}, u32[]{:S(2)}, u32[]{:S(2)}) %collective-permute-start.3) | collective-permute-done | bytes 81952 | tf_op jit(solution)/shard_map/ppermute | solution.py:249
  29.7 2.1 %merge_1.1 = (bf16[32,1280]{1,0:T(8,128)(2,1)S(1)}, bf16[32,1280]{1,0:T(8,128)(2,1)S(1)}) custom-call(s32[3]{0:T(128)S(1)} %pad_add_fusion.place, bf16[32,1280]{1,0:T(8,128)(2,1)S(1)} %get-tuple-element.19.mine, bf16[32,1280]{1,0:T(8,128)(2,1)S(1)} %collective-permute-done.3.theirs, bf16[4,512,768]{2,1,0:T(8,128)(2,1)S(1)} %get-tuple-element.18.bank), custom_call_target="tpu_custom_call" | custom-call | tf_op jit(solution)/shard_map/merge_1/pallas_call | solution.py:219
  31.7 6.1 %collective-permute-start.4 = (bf16[32,1280]{1,0:T(8,128)(2,1)S(1)}, bf16[32,1280]{1,0:T(8,128)(2,1)S(1)}, u32[]{:S(2)}, u32[]{:S(2)}) collective-permute-start(bf16[32,1280]{1,0:T(8,128)(2,1)S(1)} %get-tuple-element.22), channel_id=1, source_target_pairs={{0,32},{8,40},{16,48},{24,56},{32,0},{40,8},{48,16},{56,24},{64,96... | collective-permute-start | bytes 245768 | tf_op jit(solution)/shard_map/ppermute | solution.py:249
  37.8 4.0 %collective-permute-done.4.theirs = bf16[32,1280]{1,0:T(8,128)(2,1)S(1)} collective-permute-done((bf16[32,1280]{1,0:T(8,128)(2,1)S(1)}, bf16[32,1280]{1,0:T(8,128)(2,1)S(1)}, u32[]{:S(2)}, u32[]{:S(2)}) %collective-permute-start.4) | collective-permute-done | bytes 81952 | tf_op jit(solution)/shard_map/ppermute | solution.py:249
  41.8 2.1 %merge_2.1 = (bf16[32,1280]{1,0:T(8,128)(2,1)S(1)}, bf16[32,1280]{1,0:T(8,128)(2,1)S(1)}) custom-call(s32[3]{0:T(128)S(1)} %pad_add_fusion.place, bf16[32,1280]{1,0:T(8,128)(2,1)S(1)} %get-tuple-element.21.mine, bf16[32,1280]{1,0:T(8,128)(2,1)S(1)} %collective-permute-done.4.theirs, bf16[4,512,768]{2,1,0:T(8,128)(2,1)S(1)} %get-tuple-element.18.bank), custom_call_target="tpu_custom_call" | custom-call | tf_op jit(solution)/shard_map/merge_2/pallas_call | solution.py:219
  43.9 8.5 %collective-permute-start.5 = (bf16[32,1280]{1,0:T(8,128)(2,1)S(1)}, bf16[32,1280]{1,0:T(8,128)(2,1)S(1)}, u32[]{:S(2)}, u32[]{:S(2)}) collective-permute-start(bf16[32,1280]{1,0:T(8,128)(2,1)S(1)} %get-tuple-element.24), channel_id=1, source_target_pairs={{0,64},{8,72},{16,80},{24,88},{32,96},{40,104},{48,112},{56,120},{... | collective-permute-start | bytes 245768 | tf_op jit(solution)/shard_map/ppermute | solution.py:249
  52.4 2.4 %collective-permute-done.5.theirs = bf16[32,1280]{1,0:T(8,128)(2,1)S(1)} collective-permute-done((bf16[32,1280]{1,0:T(8,128)(2,1)S(1)}, bf16[32,1280]{1,0:T(8,128)(2,1)S(1)}, u32[]{:S(2)}, u32[]{:S(2)}) %collective-permute-start.5) | collective-permute-done | bytes 81952 | tf_op jit(solution)/shard_map/ppermute | solution.py:249
  54.8 2.7 %merge_3.1 = bf16[2,32,1024]{2,1,0:T(8,128)(2,1)} custom-call(s32[3]{0:T(128)S(1)} %pad_add_fusion.place, bf16[32,1280]{1,0:T(8,128)(2,1)S(1)} %get-tuple-element.23.mine, bf16[32,1280]{1,0:T(8,128)(2,1)S(1)} %collective-permute-done.5.theirs, bf16[4,512,768]{2,1,0:T(8,128)(2,1)S(1)} %get-tuple-element.18.bank), custom_call_target="tpu_custom_call" | custom-call | tf_op jit(solution)/shard_map/merge_3/pallas_call | solution.py:219
Async XLA Ops:
  0.8 15.6 %collective-permute-start = (bf16[2,32,384]{2,1,0:T(8,128)(2,1)S(1)}, bf16[2,32,384]{2,1,0:T(8,128)(2,1)S(1)}, u32[]{:S(2)}, u32[]{:S(2)}) collective-permute-start(bf16[2,32,384]{2,1,0:T(8,128)(2,1)S(1)} %get-tuple-element.26), channel_id=1, source_target_pairs={{0,1},{1,2},{2,3},{3,4},{4,5},{5,6},{6,7},{8,9},{9,10},{10,11},{11... | collective-permute-start | bytes 147464 | tf_op jit(solution)/shard_map/ppermute | solution.py:239
  4.2 12.2 %collective-permute-start.1 = (bf16[2,32,384]{2,1,0:T(8,128)(2,1)S(1)}, bf16[2,32,384]{2,1,0:T(8,128)(2,1)S(1)}, u32[]{:S(2)}, u32[]{:S(2)}) collective-permute-start(bf16[2,32,384]{2,1,0:T(8,128)(2,1)S(1)} %get-tuple-element.25), channel_id=1, source_target_pairs={{1,0},{2,1},{3,2},{4,3},{5,4},{6,5},{7,6},{9,8},{10,9},{11,10},{12... | collective-permute-start | bytes 147464 | tf_op jit(solution)/shard_map/ppermute | solution.py:238
  9.9 0.7 %copy-start.1 = (s32[4,2,32]{2,1,0:T(2,128)S(1)}, s32[4,2,32]{2,1,0:T(2,128)}, u32[]{:S(2)}) copy-start(s32[4,2,32]{2,1,0:T(2,128)} %offsets.1) | copy-start | bytes 3076
  10.6 0.7 %copy-start.2 = (s32[4,2,32]{2,1,0:T(2,128)S(1)}, s32[4,2,32]{2,1,0:T(2,128)}, u32[]{:S(2)}) copy-start(s32[4,2,32]{2,1,0:T(2,128)} %widths.1) | copy-start | bytes 3076
  11.3 0.7 %copy-start.3 = (bf16[2,512]{1,0:T(2,128)(2,1)S(1)}, bf16[2,512]{1,0:T(2,128)(2,1)}, u32[]{:S(2)}) copy-start(bf16[2,512]{1,0:T(2,128)(2,1)} %chirp.1) | copy-start | bytes 6148
  12.0 0.7 %copy-start.4 = (s32[4,32]{1,0:T(4,128)S(1)}, s32[4,32]{1,0:T(4,128)}, u32[]{:S(2)}) copy-start(s32[4,32]{1,0:T(4,128)} %child.1) | copy-start | bytes 1540
  12.7 3.8 %copy-start = (bf16[2,32,1024]{2,1,0:T(8,128)(2,1)S(1)}, bf16[2,32,1024]{2,1,0:T(8,128)(2,1)}, u32[]{:S(2)}) copy-start(bf16[2,32,1024]{2,1,0:T(8,128)(2,1)} %echoes.1) | copy-start | bytes 393220
  17.4 3.2 %collective-permute-start.2 = (bf16[32,1280]{1,0:T(8,128)(2,1)S(1)}, bf16[32,1280]{1,0:T(8,128)(2,1)S(1)}, u32[]{:S(2)}, u32[]{:S(2)}) collective-permute-start(bf16[32,1280]{1,0:T(8,128)(2,1)S(1)} %get-tuple-element.17), channel_id=1, source_target_pairs={{0,8},{8,0},{16,24},{24,16},{32,40},{40,32},{48,56},{56,48},{64,72... | collective-permute-start | bytes 245768 | tf_op jit(solution)/shard_map/ppermute | solution.py:249
  22.6 7.0 %collective-permute-start.3 = (bf16[32,1280]{1,0:T(8,128)(2,1)S(1)}, bf16[32,1280]{1,0:T(8,128)(2,1)S(1)}, u32[]{:S(2)}, u32[]{:S(2)}) collective-permute-start(bf16[32,1280]{1,0:T(8,128)(2,1)S(1)} %get-tuple-element.20), channel_id=1, source_target_pairs={{0,16},{8,24},{16,0},{24,8},{32,48},{40,56},{48,32},{56,40},{64,80... | collective-permute-start | bytes 245768 | tf_op jit(solution)/shard_map/ppermute | solution.py:249
  31.7 10.1 %collective-permute-start.4 = (bf16[32,1280]{1,0:T(8,128)(2,1)S(1)}, bf16[32,1280]{1,0:T(8,128)(2,1)S(1)}, u32[]{:S(2)}, u32[]{:S(2)}) collective-permute-start(bf16[32,1280]{1,0:T(8,128)(2,1)S(1)} %get-tuple-element.22), channel_id=1, source_target_pairs={{0,32},{8,40},{16,48},{24,56},{32,0},{40,8},{48,16},{56,24},{64,96... | collective-permute-start | bytes 245768 | tf_op jit(solution)/shard_map/ppermute | solution.py:249
  43.9 10.9 %collective-permute-start.5 = (bf16[32,1280]{1,0:T(8,128)(2,1)S(1)}, bf16[32,1280]{1,0:T(8,128)(2,1)S(1)}, u32[]{:S(2)}, u32[]{:S(2)}) collective-permute-start(bf16[32,1280]{1,0:T(8,128)(2,1)S(1)} %get-tuple-element.24), channel_id=1, source_target_pairs={{0,64},{8,72},{16,80},{24,88},{32,96},{40,104},{48,112},{56,120},{... | collective-permute-start | bytes 245768 | tf_op jit(solution)/shard_map/ppermute | solution.py:249
where the time goes:
time: 57.9 us; the launch traced here: 57.5 us
  starting transfers between devices  28.7 us (50%)
  Pallas kernels  13.6 us (23%)
  waiting for transfers between devices  10.4 us (18%)
  local copies, waits for them, and re-layouts  4.6 us (8%)
    ppermute x4, starting transfers between devices, body(): lax.ppermute(sent, 'aperture', [(i, i ^ 1 << level) for i in range(blocks)])  20.7 us
    ppermute x4, waiting for transfers between devices, body(): lax.ppermute(sent, 'aperture', [(i, i ^ 1 << level) for i in range(blocks)])  10.4 us
    pallas_call x4, Pallas kernels, merge(): pl.pallas_call(last_kernel if last else level_kernel, grid=(1,), out_shap...  8.9 us
    ppermute x1, starting transfers between devices, body(): lax.ppermute(echoes[:, :, :HALO], 'range', [(i + 1, i) for i in range(cou...  4.55 us
    unnamed x11, local copies, waits for them, and re-layouts  3.77 us
    pallas_call x1, Pallas kernels, prepare(): pl.pallas_call(prepare_kernel, out_shape=(jax.ShapeDtypeStruct((2 * LANES...  3.72 us
    ppermute x1, starting transfers between devices, body(): lax.ppermute(echoes[:, :, BINS - HALO:], 'range', [(i, i + 1) for i in ra...  3.4 us
  transfers between devices with their start and end apart: 6, of which 4 were waited for; matrix products, arithmetic and copies ran while one was open for 2% of the time, Pallas kernels for 6%

commit v1 on v0

v1 whole, which is shorter than its diff:
```python
import jax
import jax.numpy as jnp
from jax import lax
from jax.experimental import pallas as pl
from jax.experimental.pallas import tpu as pltpu
from jax.sharding import PartitionSpec as P

KERN = 16
SHIFT = 16
LEVELS = 4
TAPS = 512
HALF = 16
ROWS = 32
LANES = 128
BINS = 1024
RIM = 128
FRAME = BINS + 2 * RIM
RIM_LATE = 64
FRAME_LATE = BINS + 2 * RIM_LATE
HALO = RIM + TAPS // 2
SPAN = LANES + TAPS
COARSE = 6
FINE = 8
COLS = 2 * COARSE * 32
OUTS = FINE * 32
PART = 64
VMEM = 48 * 1024 * 1024
BF16 = jnp.bfloat16
F32 = jnp.float32


def build_bank(bank, weights, numbers):
    lane = lax.broadcasted_iota(jnp.int32, (HALF, LANES), 1)
    imag = ((lane >> 4) & 1) == 1
    swapped = jnp.where(imag, pltpu.roll(weights, 16, 1), pltpu.roll(weights, LANES - 16, 1))
    sources = (jnp.where(imag, -weights, weights), swapped)
    numbers = numbers.astype(jnp.int32)
    column = [jnp.broadcast_to(numbers[:, i : i + 1], (HALF, LANES)) for i in range(5)]
    for tile in range(COLS // LANES):
        spot = lane + tile * LANES
        upper = spot >= COLS // 2
        spot = jnp.where(upper, spot - COLS // 2, spot)
        base = jnp.where(upper, 32, 0) + ((spot >> 4) & 1) * KERN
        first = (spot >> 5) * FINE - SHIFT - jnp.where(upper, column[1], column[0])
        width = jnp.where(upper, column[3], column[2])
        width = jnp.where((spot & 15) == column[4], width, 0)
        at = slice(tile * LANES, (tile + 1) * LANES)
        rest_at = slice(COLS + tile * LANES, COLS + (tile + 1) * LANES)
        for b in range(FINE):
            tap = first + b
            live = (tap >= 0) & (tap < width)
            index = base | (tap & (KERN - 1))
            for part in range(2):
                value = jnp.take_along_axis(
                    sources[part], index, axis=1, mode="promise_in_bounds"
                )
                value = jnp.where(live, value, 0.0)
                high = value.astype(BF16)
                rows = slice(b * 32 + part * HALF, b * 32 + (part + 1) * HALF)
                bank[rows, at] = high
                bank[rows, rest_at] = (value - high.astype(F32)).astype(BF16)


def level_params(weights, numbers, level, rows):
    tile = weights[rows, (level // 2) * LANES : (level // 2 + 1) * LANES]
    if level % 2:
        tile = pltpu.roll(tile, LANES - PART, 1)
    own = numbers[rows, :]
    picks = (2 * level, 2 * level + 1, 8 + 2 * level, 9 + 2 * level, 16 + level)
    return tile, jnp.concatenate([own[:, i : i + 1] for i in picks], axis=1)


def prepare_kernel(
    place, chirp_hbm, weights_hbm, offsets_hbm, widths_hbm, child_hbm,
    toeplitz, bank, weights, numbers,
    chirp, wide, offsets, widths, child, table, sems,
):
    copies = [
        pltpu.make_async_copy(source, target, sems.at[i])
        for i, (source, target) in enumerate(
            (
                (chirp_hbm, chirp),
                (weights_hbm, wide),
                (offsets_hbm, offsets),
                (widths_hbm, widths),
                (child_hbm, child),
            )
        )
    ]
    for copy in copies:
        copy.start()
    for copy in copies:
        copy.wait()

    taps = chirp[...].astype(F32)
    taps = jnp.concatenate([taps, jnp.zeros((2, SPAN - TAPS), F32)], axis=1)
    real = pltpu.roll(jnp.broadcast_to(taps[0:1], (LANES, SPAN)), 0, 1, stride=1, stride_axis=0)
    imag = pltpu.roll(jnp.broadcast_to(taps[1:2], (LANES, SPAN)), 0, 1, stride=1, stride_axis=0)
    toeplitz[0:LANES, 0:SPAN] = real.astype(BF16)
    toeplitz[0:LANES, SPAN : 2 * SPAN] = imag.astype(BF16)
    toeplitz[LANES : 2 * LANES, 0:SPAN] = (-imag).astype(BF16)
    toeplitz[LANES : 2 * LANES, SPAN : 2 * SPAN] = real.astype(BF16)

    weights[...] = wide[...].T
    table[...] = jnp.zeros((ROWS, LANES), F32)
    for level in range(LEVELS):
        table[2 * level : 2 * level + 2, 0:ROWS] = offsets[level].astype(F32)
        table[8 + 2 * level : 10 + 2 * level, 0:ROWS] = widths[level].astype(F32)
    table[16:20, 0:ROWS] = child[...].astype(F32)
    numbers[:, 0:ROWS] = table[...].T[0:ROWS]

    first = pl.multiple_of(((place[0] >> 1) & 1) * HALF, HALF)
    other = pl.multiple_of((1 - ((place[0] >> 1) & 1)) * HALF, HALF)
    for half, start in enumerate((first, other)):
        build_bank(bank.at[half], *level_params(weights, numbers, 0, pl.ds(start, HALF)))


def prepare_late_kernel(after, weights, numbers, bank, bank_last, payload):
    for half in range(2):
        rows = slice(half * HALF, (half + 1) * HALF)
        build_bank(bank.at[half], *level_params(weights, numbers, 1, rows))
        build_bank(bank_last.at[half], *level_params(weights, numbers, 3, rows))
        tile, own = level_params(weights, numbers, 2, rows)
        lane = lax.broadcasted_iota(jnp.int32, (HALF, LANES), 1)
        high = tile.astype(BF16).astype(F32)
        rest = pltpu.roll(tile - high, PART, 1)
        payload[half, 0:HALF] = jnp.where(lane < PART, high, rest).astype(BF16)
        own = jnp.concatenate([own, jnp.zeros((HALF, LANES - 5), F32)], axis=1)
        payload[half, HALF:ROWS] = own.astype(BF16)


def inside_mask(place, rows, length, rim):
    bins = lax.broadcasted_iota(jnp.int32, (rows, length), 1) + (place[1] * BINS - rim)
    return (bins >= 0) & (bins < place[2])


def compress_kernel(place, echoes, left, right, toeplitz, kept, sent, window):
    start = pl.multiple_of((place[0] & 1) * HALF, HALF)
    other = pl.multiple_of((1 - (place[0] & 1)) * HALF, HALF)
    blocks = FRAME // LANES
    tiles = SPAN // LANES
    first = HALO // LANES
    last = first + BINS // LANES
    for part in range(2):
        for half, at in enumerate((start, other)):
            for tile in range(blocks + tiles - 1):
                if tile < first:
                    piece = left[part, pl.ds(at, HALF), tile * LANES : (tile + 1) * LANES]
                elif tile < last:
                    spot = (tile - first) * LANES
                    piece = echoes[part, pl.ds(at, HALF), spot : spot + LANES]
                else:
                    spot = (tile - last) * LANES
                    piece = right[part, pl.ds(at, HALF), spot : spot + LANES]
                for block in range(max(0, tile - tiles + 1), min(blocks, tile + 1)):
                    spot = part * SPAN + (tile - block) * LANES
                    top = block * ROWS + half * HALF
                    window[top : top + HALF, spot : spot + LANES] = piece
    result = lax.dot_general(
        window[...], toeplitz[...], (((1,), (1,)), ((), ())), preferred_element_type=jnp.float32
    )
    position = place[1] * BINS - RIM
    for block in range(blocks):
        bins = lax.broadcasted_iota(jnp.int32, (ROWS, 2 * LANES), 1) & (LANES - 1)
        bins = bins + (position + block * LANES)
        inside = (bins >= 0) & (bins < place[2])
        piece = jnp.where(inside, result[block * ROWS : (block + 1) * ROWS], 0.0)
        piece = piece.astype(jnp.bfloat16)
        at = slice(block * LANES, (block + 1) * LANES)
        for part in range(2):
            lanes = slice(part * LANES, (part + 1) * LANES)
            kept[part * HALF : (part + 1) * HALF, at] = piece[0:HALF, lanes]
            sent[part * HALF : (part + 1) * HALF, at] = piece[HALF:ROWS, lanes]


def fill_stack(stack, t, source):
    length = source.shape[1]
    source = source.astype(F32)
    for a in range(COARSE):
        shift = (24 - 8 * a) % length
        moved = (pltpu.roll(source, shift, 1) if shift else source).astype(BF16)
        top = t * (COLS // 2) + a * 32
        stack[top : top + 32] = moved
        stack[COLS + top : COLS + top + 32] = moved


def fine_sum(product, trim):
    length = product.shape[1]
    total = None
    for b in range(FINE):
        piece = product[b * 32 : (b + 1) * 32]
        if b + trim:
            piece = pltpu.roll(piece, length - b - trim, 1)
        total = piece if total is None else total + piece
    return total


def merge_first_kernel(place, mine, theirs, bank, kept, sent, stack):
    lower = (place[0] & 1) == 0
    fill_stack(stack, 0, jnp.where(lower, mine[...], theirs[...]))
    fill_stack(stack, 1, jnp.where(lower, theirs[...], mine[...]))
    inside = inside_mask(place, 32, FRAME, RIM)
    for half, out in enumerate((kept, sent)):
        product = jnp.dot(bank[half], stack[...], preferred_element_type=F32)
        out[...] = jnp.where(inside, fine_sum(product, 0), 0.0).astype(BF16)


def merge_second_kernel(place, mine, theirs, bank, payload, out, stack):
    lower = ((place[0] >> 1) & 1) == 0
    fill_stack(stack, 0, jnp.where(lower, mine[...], theirs[...]))
    fill_stack(stack, 1, jnp.where(lower, theirs[...], mine[...]))
    inside = inside_mask(place, 32, FRAME_LATE, RIM_LATE)
    for half in range(2):
        product = jnp.dot(bank[half], stack[...], preferred_element_type=F32)
        total = fine_sum(product, RIM - RIM_LATE)[:, 0:FRAME_LATE]
        total = jnp.where(inside, total, 0.0).astype(BF16)
        for q in (half, half + 2):
            out[q, :, 0:FRAME_LATE] = total
            out[q, :, FRAME_LATE:FRAME] = payload[q >> 1]


def merge_late_kernel(place, parts, bank_last, out, bank, stacks):
    inside = inside_mask(place, 32, FRAME_LATE, RIM_LATE)
    side = (place[0] >> 2) & 1
    for beta in range(2):
        packed = parts[2 * beta + side, :, FRAME_LATE:FRAME].astype(F32)
        weights = packed[0:HALF] + pltpu.roll(packed[0:HALF], LANES - PART, 1)
        build_bank(bank.at[beta], weights, packed[HALF:ROWS])
        for t in range(2):
            fill_stack(stacks.at[beta], t, parts[2 * beta + t, :, 0:FRAME_LATE])
    for beta in range(2):
        product = jnp.dot(bank[beta], stacks[beta], preferred_element_type=F32)
        total = jnp.where(inside, fine_sum(product, 0), 0.0).astype(BF16)
        fill_stack(stacks.at[2], beta, total)
    for half in range(2):
        product = jnp.dot(bank_last[half], stacks[2], preferred_element_type=F32)
        total = fine_sum(product, RIM_LATE)[:, 0:BINS].astype(BF16)
        for part in range(2):
            out[part, half * HALF : (half + 1) * HALF] = total[part * HALF : (part + 1) * HALF]


WHOLE = pl.BlockSpec(memory_space=pltpu.VMEM)
SCALARS = pl.BlockSpec(memory_space=pltpu.SMEM)
FAR = pl.BlockSpec(memory_space=pltpu.HBM)
PARAMS = pltpu.CompilerParams(vmem_limit_bytes=VMEM)
BANK = jax.ShapeDtypeStruct((2, OUTS, 2 * COLS), BF16)
MESSAGE = jax.ShapeDtypeStruct((2 * HALF, FRAME), BF16)


def prepare(place, chirp, weights, offsets, widths, child):
    return pl.pallas_call(
        prepare_kernel,
        out_shape=(
            jax.ShapeDtypeStruct((2 * LANES, 2 * SPAN), BF16),
            BANK,
            jax.ShapeDtypeStruct((ROWS, 4 * PART), F32),
            jax.ShapeDtypeStruct((ROWS, LANES), F32),
        ),
        in_specs=[SCALARS] + [FAR] * 5,
        out_specs=(WHOLE,) * 4,
        scratch_shapes=[
            pltpu.VMEM(chirp.shape, chirp.dtype),
            pltpu.VMEM(weights.shape, weights.dtype),
            pltpu.VMEM(offsets.shape, offsets.dtype),
            pltpu.VMEM(widths.shape, widths.dtype),
            pltpu.VMEM(child.shape, child.dtype),
            pltpu.VMEM((ROWS, LANES), F32),
            pltpu.SemaphoreType.DMA((5,)),
        ],
        compiler_params=PARAMS,
        cost_estimate=pl.CostEstimate(flops=1_000_000_000, bytes_accessed=2_000_000, transcendentals=0),
        name="prepare",
    )(place, chirp, weights, offsets, widths, child)


def prepare_late(after, weights, numbers):
    return pl.pallas_call(
        prepare_late_kernel,
        out_shape=(BANK, BANK, jax.ShapeDtypeStruct((2, ROWS, LANES), BF16)),
        in_specs=[pl.BlockSpec(memory_space=pl.ANY), WHOLE, WHOLE],
        out_specs=(WHOLE,) * 3,
        compiler_params=PARAMS,
        cost_estimate=pl.CostEstimate(flops=2_000_000_000, bytes_accessed=4_000_000, transcendentals=0),
        name="prepare_late",
    )(after, weights, numbers)


def compress(place, echoes, left, right, toeplitz):
    return pl.pallas_call(
        compress_kernel,
        out_shape=(MESSAGE, MESSAGE),
        in_specs=[SCALARS] + [WHOLE] * 4,
        out_specs=(WHOLE, WHOLE),
        scratch_shapes=[pltpu.VMEM((FRAME // LANES * ROWS, 2 * SPAN), BF16)],
        compiler_params=PARAMS,
        name="compress",
    )(place, echoes, left, right, toeplitz)


def merge_first(place, mine, theirs, bank):
    return pl.pallas_call(
        merge_first_kernel,
        out_shape=(MESSAGE, MESSAGE),
        in_specs=[SCALARS] + [WHOLE] * 3,
        out_specs=(WHOLE, WHOLE),
        scratch_shapes=[pltpu.VMEM((2 * COLS, FRAME), BF16)],
        compiler_params=PARAMS,
        name="merge_first",
    )(place, mine, theirs, bank)


def merge_second(place, mine, theirs, bank, payload):
    return pl.pallas_call(
        merge_second_kernel,
        out_shape=jax.ShapeDtypeStruct((4, 2 * HALF, FRAME), BF16),
        in_specs=[SCALARS] + [WHOLE] * 4,
        out_specs=WHOLE,
        scratch_shapes=[pltpu.VMEM((2 * COLS, FRAME), BF16)],
        compiler_params=PARAMS,
        name="merge_second",
    )(place, mine, theirs, bank, payload)


def merge_late(place, parts, bank_last):
    return pl.pallas_call(
        merge_late_kernel,
        out_shape=jax.ShapeDtypeStruct((2, ROWS, BINS), BF16),
        in_specs=[SCALARS] + [WHOLE] * 2,
        out_specs=WHOLE,
        scratch_shapes=[
            pltpu.VMEM((2, OUTS, 2 * COLS), BF16),
            pltpu.VMEM((3, 2 * COLS, FRAME_LATE), BF16),
        ],
        compiler_params=PARAMS,
        name="merge_late",
    )(place, parts, bank_last)


def body(echoes, transmit_chirp, band_weights, band_offsets, band_widths, child_rows):
    count = lax.axis_size("range")
    right = lax.ppermute(echoes[:, :, :HALO], "range", [(i + 1, i) for i in range(count - 1)])
    left = lax.ppermute(echoes[:, :, BINS - HALO :], "range", [(i, i + 1) for i in range(count - 1)])
    place = jnp.stack(
        [lax.axis_index("aperture"), lax.axis_index("range"), jnp.int32(BINS * count)]
    ).astype(jnp.int32)
    taps_first = jnp.swapaxes(band_weights, 3, 4).reshape(LEVELS * PART, ROWS)
    toeplitz, bank, weights, numbers = prepare(
        place, transmit_chirp, taps_first, band_offsets, band_widths, child_rows
    )
    kept, sent = compress(place, echoes, left, right, toeplitz)
    blocks = lax.axis_size("aperture")
    theirs = lax.ppermute(sent, "aperture", [(i, i ^ 1) for i in range(blocks)])
    kept, sent = merge_first(place, kept, theirs, bank)
    theirs = lax.ppermute(sent, "aperture", [(i, i ^ 2) for i in range(blocks)])
    bank, bank_last, payload = prepare_late(kept, weights, numbers)
    parts = merge_second(place, kept, theirs, bank, payload)
    groups = [[i, i + 4, i + 8, i + 12] for i in range(blocks) if not i & 12]
    parts = lax.all_to_all(parts, "aperture", 0, 0, axis_index_groups=groups, tiled=True)
    return merge_late(place, parts, bank_last)


def solution(mesh):
    return jax.shard_map(
        body,
        mesh=mesh,
        in_specs=(
            P(None, "aperture", "range"),
            P(),
            P(None, None, None, "aperture", None),
            P(None, None, "aperture"),
            P(None, None, "aperture"),
            P(None, "aperture"),
        ),
        out_specs=P(None, "aperture", "range"),
        check_vma=False,
    )
```

time: 57.9 us -> 56.5 us (0.976)
  the two profiles are of different devices: /device:TPU:24 before, /device:TPU:40 now
where the time goes in v1:
time: 56.5 us; the launch traced here: 56.2 us
  blocking collectives  22 us (39%)
  starting transfers between devices  13.6 us (24%)
  Pallas kernels  13.2 us (23%)
  waiting for transfers between devices  5.63 us (10%)
  local copies, waits for them, and re-layouts  1.5 us (3%)
    all_to_all x1, blocking collectives, body(): lax.all_to_all(parts, 'aperture', 0, 0, axis_index_groups=groups, tiled=T...  22 us
    ppermute x1, starting transfers between devices, body(): lax.ppermute(echoes[:, :, :HALO], 'range', [(i + 1, i) for i in range(cou...  5.45 us
    pallas_call x1, Pallas kernels, merge_late(): pl.pallas_call(merge_late_kernel, out_shape=jax.ShapeDtypeStruct((2, ROWS...  4.5 us
    ppermute x1, starting transfers between devices, body(): theirs = lax.ppermute(sent, 'aperture', [(i, i ^ 2) for i in range(blocks)])  4.28 us
    ppermute x1, waiting for transfers between devices, body(): lax.ppermute(echoes[:, :, BINS - HALO:], 'range', [(i, i + 1) for i in ra...  3.52 us
    pallas_call x1, Pallas kernels, merge_first(): pl.pallas_call(merge_first_kernel, out_shape=(MESSAGE, MESSAGE), in_specs...  2.03 us
    pallas_call x1, Pallas kernels, merge_second(): pl.pallas_call(merge_second_kernel, out_shape=jax.ShapeDtypeStruct((4, 2...  2 us
    ppermute x1, starting transfers between devices, body(): theirs = lax.ppermute(sent, 'aperture', [(i, i ^ 1) for i in range(blocks)])  1.92 us
  transfers between devices with their start and end apart: 4, of which 3 were waited for; matrix products, arithmetic and copies ran while one was open for 0% of the time, Pallas kernels for 7%

profile of v1, /device:TPU:40, one launch (start us, length us, event | category | flops | bytes accessed | tf_op | source)
XLA Modules:
  0.0 56.2 jit_solution(10137533246549006808)
XLA Ops:
  0.0 0.0 copy-start.1
  0.0 0.9 %fusion = (bf16[2,32,384]{2,1,0:T(8,128)(2,1)S(1)}, bf16[2,32,384]{2,1,0:T(8,128)(2,1)S(1)}) fusion(bf16[2,32,1024]{2,1,0:T(8,128)(2,1)} %echoes.1), kind=kLoop, calls=%fused_computation.1 | loop fusion | bytes 196608 | tf_op jit(solution)/shard_map/slice | solution.py:341
  0.9 5.5 %collective-permute-start.1 = (bf16[2,32,384]{2,1,0:T(8,128)(2,1)S(1)}, bf16[2,32,384]{2,1,0:T(8,128)(2,1)S(1)}, u32[]{:S(2)}, u32[]{:S(2)}) collective-permute-start(bf16[2,32,384]{2,1,0:T(8,128)(2,1)S(1)} %get-tuple-element.27), channel_id=1, source_target_pairs={{1,0},{2,1},{3,2},{4,3},{5,4},{6,5},{7,6},{9,8},{10,9},{11,10},{12... | collective-permute-start | bytes 147464 | tf_op jit(solution)/shard_map/ppermute | solution.py:341
  6.3 1.9 %collective-permute-start = (bf16[2,32,384]{2,1,0:T(8,128)(2,1)S(1)}, bf16[2,32,384]{2,1,0:T(8,128)(2,1)S(1)}, u32[]{:S(2)}, u32[]{:S(2)}) collective-permute-start(bf16[2,32,384]{2,1,0:T(8,128)(2,1)S(1)} %get-tuple-element.28), channel_id=1, source_target_pairs={{0,1},{1,2},{2,3},{3,4},{4,5},{5,6},{6,7},{8,9},{9,10},{10,11},{11... | collective-permute-start | bytes 147464 | tf_op jit(solution)/shard_map/ppermute | solution.py:342
  8.3 0.0 copy-start.5
  8.3 0.0 copy-start.4
  8.3 0.0 copy-start.3
  8.3 0.0 copy-start.2
  8.3 0.1 pad_add_fusion.place
  8.4 0.0 copy-done.1
  8.4 0.6 copy-done.5
  9.0 0.0 copy-done.4
  9.0 0.0 copy-done.3
  9.0 0.0 copy-done.2
  9.0 0.0 copy-start
  9.0 1.9 %prepare.1 = (bf16[256,1280]{1,0:T(8,128)(2,1)S(1)}, bf16[2,256,768]{2,1,0:T(8,128)(2,1)S(1)}, f32[32,256]{1,0:T(8,128)S(1)}, f32[32,128]{1,0:T(8,128)S(1)}) custom-call(s32[3]{0:T(128)S(1)} %pad_add_fusion.place, bf16[2,512]{1,0:T(2,128)(2,1)S(1)} %copy-done.4, f32[256,32]{1,0:T(8,128)S(1)} %bitcast.5, s32[4,2,32]{2,1,0:T(2,128)S(1)} %copy-done.2, ...), custom_call_target="tpu_custom_call" | custom-call | flops 1000000000 | bytes 2000000 | tf_op jit(solution)/shard_map/prepare/pallas_call | solution.py:251
  10.9 0.0 collective-permute-done.1.right
  10.9 3.5 %collective-permute-done.left = bf16[2,32,384]{2,1,0:T(8,128)(2,1)S(1)} collective-permute-done((bf16[2,32,384]{2,1,0:T(8,128)(2,1)S(1)}, bf16[2,32,384]{2,1,0:T(8,128)(2,1)S(1)}, u32[]{:S(2)}, u32[]{:S(2)}) %collective-permute-start) | collective-permute-done | bytes 49184 | tf_op jit(solution)/shard_map/ppermute | solution.py:342
  14.4 0.0 copy-done
  14.4 1.0 %compress.1 = (bf16[32,1280]{1,0:T(8,128)(2,1)S(1)}, bf16[32,1280]{1,0:T(8,128)(2,1)S(1)}) custom-call(s32[3]{0:T(128)S(1)} %pad_add_fusion.place, bf16[2,32,1024]{2,1,0:T(8,128)(2,1)S(1)} %copy-done, bf16[2,32,384]{2,1,0:T(8,128)(2,1)S(1)} %collective-permute-done.left, bf16[2,32,384]{2,1,0:T(8,128)(2,1)S(1)} %collective-permute-done.1.right, ...), custom_call_target="tpu_custom_call" | custom-call | tf_op jit(solution)/shard_map/compress/pallas_call | solution.py:289
  15.4 1.9 %collective-permute-start.2 = (bf16[32,1280]{1,0:T(8,128)(2,1)S(1)}, bf16[32,1280]{1,0:T(8,128)(2,1)S(1)}, u32[]{:S(2)}, u32[]{:S(2)}) collective-permute-start(bf16[32,1280]{1,0:T(8,128)(2,1)S(1)} %get-tuple-element.18), channel_id=1, source_target_pairs={{0,8},{8,0},{16,24},{24,16},{32,40},{40,32},{48,56},{56,48},{64,72... | collective-permute-start | bytes 245768 | tf_op jit(solution)/shard_map/ppermute | solution.py:352
  17.3 1.2 %collective-permute-done.2.theirs = bf16[32,1280]{1,0:T(8,128)(2,1)S(1)} collective-permute-done((bf16[32,1280]{1,0:T(8,128)(2,1)S(1)}, bf16[32,1280]{1,0:T(8,128)(2,1)S(1)}, u32[]{:S(2)}, u32[]{:S(2)}) %collective-permute-start.2) | collective-permute-done | bytes 81952 | tf_op jit(solution)/shard_map/ppermute | solution.py:352
  18.6 2.0 %merge_first.1 = (bf16[32,1280]{1,0:T(8,128)(2,1)S(1)}, bf16[32,1280]{1,0:T(8,128)(2,1)S(1)}) custom-call(s32[3]{0:T(128)S(1)} %pad_add_fusion.place, bf16[32,1280]{1,0:T(8,128)(2,1)S(1)} %get-tuple-element.17.mine, bf16[32,1280]{1,0:T(8,128)(2,1)S(1)} %collective-permute-done.2.theirs, bf16[2,256,768]{2,1,0:T(8,128)(2,1)S(1)} %get-tuple-element.19.bank), custom_call_target="tpu_custom_call" | custom-call | tf_op jit(solution)/shard_map/merge_first/pallas_call | solution.py:301
  20.6 4.3 %collective-permute-start.3 = (bf16[32,1280]{1,0:T(8,128)(2,1)S(1)}, bf16[32,1280]{1,0:T(8,128)(2,1)S(1)}, u32[]{:S(2)}, u32[]{:S(2)}) collective-permute-start(bf16[32,1280]{1,0:T(8,128)(2,1)S(1)} %get-tuple-element.21), channel_id=1, source_target_pairs={{0,16},{8,24},{16,0},{24,8},{32,48},{40,56},{48,32},{56,40},{64,80... | collective-permute-start | bytes 245768 | tf_op jit(solution)/shard_map/ppermute | solution.py:354
  24.9 1.9 %prepare_late.1 = (bf16[2,256,768]{2,1,0:T(8,128)(2,1)S(1)}, bf16[2,256,768]{2,1,0:T(8,128)(2,1)S(1)}, bf16[2,32,128]{2,1,0:T(8,128)(2,1)S(1)}) custom-call(bf16[32,1280]{1,0:T(8,128)(2,1)S(1)} %get-tuple-element.20.after.mine, f32[32,256]{1,0:T(8,128)S(1)} %get-tuple-element.22.weights, f32[32,128]{1,0:T(8,128)S(1)} %get-tuple-element.23.numbers), custom_call_target="tpu_custom_call" | custom-call | flops 2000000000 | bytes 4000000 | tf_op jit(solution)/shard_map/prepare_late/pallas_call | solution.py:277
  26.8 0.9 %collective-permute-done.3.theirs = bf16[32,1280]{1,0:T(8,128)(2,1)S(1)} collective-permute-done((bf16[32,1280]{1,0:T(8,128)(2,1)S(1)}, bf16[32,1280]{1,0:T(8,128)(2,1)S(1)}, u32[]{:S(2)}, u32[]{:S(2)}) %collective-permute-start.3) | collective-permute-done | bytes 81952 | tf_op jit(solution)/shard_map/ppermute | solution.py:354
  27.6 2.0 %merge_second.1 = bf16[4,32,1280]{2,1,0:T(8,128)(2,1)S(1)} custom-call(s32[3]{0:T(128)S(1)} %pad_add_fusion.place, bf16[32,1280]{1,0:T(8,128)(2,1)S(1)} %get-tuple-element.20.after.mine, bf16[32,1280]{1,0:T(8,128)(2,1)S(1)} %collective-permute-done.3.theirs, bf16[2,256,768]{2,1,0:T(8,128)(2,1)S(1)} %get-tuple-element.24.bank, ...), custom_call_target="tpu_custom_call" | custom-call | tf_op jit(solution)/shard_map/merge_second/pallas_call | solution.py:313
  29.7 22.0 %all_to_all.5.parts = bf16[4,32,1280]{2,1,0:T(8,128)(2,1)S(1)} all-to-all(bf16[4,32,1280]{2,1,0:T(8,128)(2,1)S(1)} %merge_second.1), channel_id=1, replica_groups={{0,32,64,96},{8,40,72,104},{16,48,80,112},{24,56,88,120},{128,160,192,2..., dimensions={0} | all-to-all | bytes 655360 | tf_op jit(solution)/shard_map/all_to_all | solution.py:358
  51.7 4.5 %merge_late.1 = bf16[2,32,1024]{2,1,0:T(8,128)(2,1)} custom-call(s32[3]{0:T(128)S(1)} %pad_add_fusion.place, bf16[4,32,1280]{2,1,0:T(8,128)(2,1)S(1)} %all_to_all.5.parts, bf16[2,256,768]{2,1,0:T(8,128)(2,1)S(1)} %get-tuple-element.26.bank_last), custom_call_target="tpu_custom_call" | custom-call | tf_op jit(solution)/shard_map/merge_late/pallas_call | solution.py:325
Async XLA Ops:
  0.0 8.4 %copy-start.1 = (f32[4,2,2,32,16]{3,4,2,1,0:T(8,128)S(1)}, f32[4,2,2,32,16]{3,4,2,1,0:T(8,128)}, u32[]{:S(2)}) copy-start(f32[4,2,2,32,16]{3,4,2,1,0:T(8,128)} %param.8) | copy-start | bytes 98308
  0.9 10.0 %collective-permute-start.1 = (bf16[2,32,384]{2,1,0:T(8,128)(2,1)S(1)}, bf16[2,32,384]{2,1,0:T(8,128)(2,1)S(1)}, u32[]{:S(2)}, u32[]{:S(2)}) collective-permute-start(bf16[2,32,384]{2,1,0:T(8,128)(2,1)S(1)} %get-tuple-element.27), channel_id=1, source_target_pairs={{1,0},{2,1},{3,2},{4,3},{5,4},{6,5},{7,6},{9,8},{10,9},{11,10},{12... | collective-permute-start | bytes 147464 | tf_op jit(solution)/shard_map/ppermute | solution.py:341
  6.3 8.1 %collective-permute-start = (bf16[2,32,384]{2,1,0:T(8,128)(2,1)S(1)}, bf16[2,32,384]{2,1,0:T(8,128)(2,1)S(1)}, u32[]{:S(2)}, u32[]{:S(2)}) collective-permute-start(bf16[2,32,384]{2,1,0:T(8,128)(2,1)S(1)} %get-tuple-element.28), channel_id=1, source_target_pairs={{0,1},{1,2},{2,3},{3,4},{4,5},{5,6},{6,7},{8,9},{9,10},{10,11},{11... | collective-permute-start | bytes 147464 | tf_op jit(solution)/shard_map/ppermute | solution.py:342
  8.3 0.7 %copy-start.5 = (s32[4,32]{1,0:T(4,128)S(1)}, s32[4,32]{1,0:T(4,128)}, u32[]{:S(2)}) copy-start(s32[4,32]{1,0:T(4,128)} %child_hbm.1) | copy-start | bytes 1540
  8.3 0.7 %copy-start.4 = (bf16[2,512]{1,0:T(2,128)(2,1)S(1)}, bf16[2,512]{1,0:T(2,128)(2,1)}, u32[]{:S(2)}) copy-start(bf16[2,512]{1,0:T(2,128)(2,1)} %chirp_hbm.1) | copy-start | bytes 6148
  8.3 0.7 %copy-start.3 = (s32[4,2,32]{2,1,0:T(2,128)S(1)}, s32[4,2,32]{2,1,0:T(2,128)}, u32[]{:S(2)}) copy-start(s32[4,2,32]{2,1,0:T(2,128)} %widths_hbm.1) | copy-start | bytes 3076
  8.3 0.7 %copy-start.2 = (s32[4,2,32]{2,1,0:T(2,128)S(1)}, s32[4,2,32]{2,1,0:T(2,128)}, u32[]{:S(2)}) copy-start(s32[4,2,32]{2,1,0:T(2,128)} %offsets_hbm.1) | copy-start | bytes 3076
  9.0 5.4 %copy-start = (bf16[2,32,1024]{2,1,0:T(8,128)(2,1)S(1)}, bf16[2,32,1024]{2,1,0:T(8,128)(2,1)}, u32[]{:S(2)}) copy-start(bf16[2,32,1024]{2,1,0:T(8,128)(2,1)} %echoes.1) | copy-start | bytes 393220
  15.4 3.2 %collective-permute-start.2 = (bf16[32,1280]{1,0:T(8,128)(2,1)S(1)}, bf16[32,1280]{1,0:T(8,128)(2,1)S(1)}, u32[]{:S(2)}, u32[]{:S(2)}) collective-permute-start(bf16[32,1280]{1,0:T(8,128)(2,1)S(1)} %get-tuple-element.18), channel_id=1, source_target_pairs={{0,8},{8,0},{16,24},{24,16},{32,40},{40,32},{48,56},{56,48},{64,72... | collective-permute-start | bytes 245768 | tf_op jit(solution)/shard_map/ppermute | solution.py:352
  20.6 7.0 %collective-permute-start.3 = (bf16[32,1280]{1,0:T(8,128)(2,1)S(1)}, bf16[32,1280]{1,0:T(8,128)(2,1)S(1)}, u32[]{:S(2)}, u32[]{:S(2)}) collective-permute-start(bf16[32,1280]{1,0:T(8,128)(2,1)S(1)} %get-tuple-element.21), channel_id=1, source_target_pairs={{0,16},{8,24},{16,0},{24,8},{32,48},{40,56},{48,32},{56,40},{64,80... | collective-permute-start | bytes 245768 | tf_op jit(solution)/shard_map/ppermute | solution.py:354

commit v2 on v1

v2 whole, which is shorter than its diff:
```python
import functools

import jax
import jax.numpy as jnp
from jax import lax
from jax.experimental import pallas as pl
from jax.experimental.pallas import tpu as pltpu
from jax.sharding import PartitionSpec as P

KERN = 16
SHIFT = 16
LEVELS = 4
TAPS = 512
HALF = 16
ROWS = 32
LANES = 128
BINS = 1024
RIM = 128
FRAME = BINS + 2 * RIM
RIM_LATE = 64
FRAME_LATE = BINS + 2 * RIM_LATE
HALO = RIM + TAPS // 2
SPAN = LANES + TAPS
COARSE = 6
FINE = 8
COLS = 2 * COARSE * 32
OUTS = FINE * 32
PART = 64
VMEM = 48 * 1024 * 1024
BF16 = jnp.bfloat16
F32 = jnp.float32


def build_bank(bank, weights, numbers):
    lane = lax.broadcasted_iota(jnp.int32, (HALF, LANES), 1)
    imag = ((lane >> 4) & 1) == 1
    swapped = jnp.where(imag, pltpu.roll(weights, 16, 1), pltpu.roll(weights, LANES - 16, 1))
    sources = (jnp.where(imag, -weights, weights), swapped)
    numbers = numbers.astype(jnp.int32)
    column = [jnp.broadcast_to(numbers[:, i : i + 1], (HALF, LANES)) for i in range(5)]
    for tile in range(COLS // LANES):
        spot = lane + tile * LANES
        upper = spot >= COLS // 2
        spot = jnp.where(upper, spot - COLS // 2, spot)
        base = jnp.where(upper, 32, 0) + ((spot >> 4) & 1) * KERN
        first = (spot >> 5) * FINE - SHIFT - jnp.where(upper, column[1], column[0])
        width = jnp.where(upper, column[3], column[2])
        width = jnp.where((spot & 15) == column[4], width, 0)
        at = slice(tile * LANES, (tile + 1) * LANES)
        rest_at = slice(COLS + tile * LANES, COLS + (tile + 1) * LANES)
        for b in range(FINE):
            tap = first + b
            live = (tap >= 0) & (tap < width)
            index = base | (tap & (KERN - 1))
            for part in range(2):
                value = jnp.take_along_axis(
                    sources[part], index, axis=1, mode="promise_in_bounds"
                )
                value = jnp.where(live, value, 0.0)
                high = value.astype(BF16)
                rows = slice(b * 32 + part * HALF, b * 32 + (part + 1) * HALF)
                bank[rows, at] = high
                bank[rows, rest_at] = (value - high.astype(F32)).astype(BF16)


def level_params(weights, numbers, level, rows):
    swap = ((lax.axis_index("aperture") >> level) & 1) == 1
    tile = weights[rows, (level // 2) * LANES : (level // 2 + 1) * LANES]
    if level % 2:
        tile = pltpu.roll(tile, LANES - PART, 1)
    lane = lax.broadcasted_iota(jnp.int32, (HALF, LANES), 1)
    turned = jnp.where(lane < 32, pltpu.roll(tile, LANES - 32, 1), pltpu.roll(tile, 32, 1))
    own = numbers[rows, :]
    off, wide = 2 * level, 8 + 2 * level
    picks = [own[:, k : k + 1] for k in (off, off + 1, wide, wide + 1, 16 + level)]
    for k in (0, 2):
        pair = picks[k], picks[k + 1]
        picks[k] = jnp.where(swap, pair[1], pair[0])
        picks[k + 1] = jnp.where(swap, pair[0], pair[1])
    return jnp.where(swap, turned, tile), jnp.concatenate(picks, axis=1)


def build_level(bank, weights, numbers, level):
    first = 0
    if level + 1 < LEVELS:
        first = (lax.axis_index("aperture") >> (level + 1)) & 1
    for half in range(2):
        side = half ^ first
        start = side * HALF if isinstance(side, int) else pl.multiple_of(side * HALF, HALF)
        build_bank(bank.at[half], *level_params(weights, numbers, level, pl.ds(start, HALF)))


def prepare_kernel(chirp, taps_in, numbers_in, toeplitz, bank, weights, numbers, table):
    taps = chirp[...].astype(F32)
    taps = jnp.concatenate([taps, jnp.zeros((2, SPAN - TAPS), F32)], axis=1)
    real = pltpu.roll(jnp.broadcast_to(taps[0:1], (LANES, SPAN)), 0, 1, stride=1, stride_axis=0)
    imag = pltpu.roll(jnp.broadcast_to(taps[1:2], (LANES, SPAN)), 0, 1, stride=1, stride_axis=0)
    toeplitz[0:LANES, 0:SPAN] = real.astype(BF16)
    toeplitz[0:LANES, SPAN : 2 * SPAN] = imag.astype(BF16)
    toeplitz[LANES : 2 * LANES, 0:SPAN] = (-imag).astype(BF16)
    toeplitz[LANES : 2 * LANES, SPAN : 2 * SPAN] = real.astype(BF16)

    table[...] = jnp.zeros((ROWS, LANES), F32)
    for level in range(LEVELS):
        weights[:, level * PART : (level + 1) * PART] = taps_in[level].T
        own = numbers_in[level].astype(F32)
        table[2 * level : 2 * level + 2, 0:ROWS] = own[0:2]
        table[8 + 2 * level : 10 + 2 * level, 0:ROWS] = own[2:4]
        table[16 + level : 17 + level, 0:ROWS] = own[4:5]
    numbers[:, 0:ROWS] = table[...].T[0:ROWS]
    build_level(bank, weights, numbers, 0)


def prepare_late_kernel(level, after, weights, numbers, bank):
    build_level(bank, weights, numbers, level)


def inside_mask(rows, length, rim):
    bins = lax.broadcasted_iota(jnp.int32, (rows, length), 1) + (lax.axis_index("range") * BINS - rim)
    return (bins >= 0) & (bins < (BINS * lax.axis_size("range")))


def compress_kernel(sent, echoes, even, odd, toeplitz, out, window, rows=None):
    side = (lax.axis_index("aperture") & 1) ^ 1 if sent else lax.axis_index("aperture") & 1
    at = pl.multiple_of(side * HALF, HALF)
    is_odd = (lax.axis_index("range") & 1) == 1
    blocks = FRAME // LANES
    tiles = SPAN // LANES
    first = HALO // LANES
    last = first + BINS // LANES
    for part in range(2):
        for tile in range(blocks + tiles - 1):
            if first <= tile < last:
                spot = (tile - first) * LANES
                piece = echoes[part, pl.ds(at, HALF), spot : spot + LANES]
            else:
                spot = (tile if tile < first else tile - last) * LANES
                ours = even[part, pl.ds(at, HALF), spot : spot + LANES]
                other = odd[part, pl.ds(at, HALF), spot : spot + LANES]
                if tile < first:
                    piece = jnp.where(is_odd, ours, other)
                else:
                    piece = jnp.where(is_odd, other, ours)
            for block in range(max(0, tile - tiles + 1), min(blocks, tile + 1)):
                spot = part * SPAN + (tile - block) * LANES
                window[block * HALF : (block + 1) * HALF, spot : spot + LANES] = piece
    result = lax.dot_general(
        window[...], toeplitz[...], (((1,), (1,)), ((), ())), preferred_element_type=F32
    )
    position = lax.axis_index("range") * BINS - RIM
    target = out if sent else rows
    for block in range(blocks):
        bins = lax.broadcasted_iota(jnp.int32, (HALF, 2 * LANES), 1) & (LANES - 1)
        bins = bins + (position + block * LANES)
        inside = (bins >= 0) & (bins < BINS * lax.axis_size("range"))
        piece = jnp.where(inside, result[block * HALF : (block + 1) * HALF], 0.0).astype(BF16)
        at = slice(block * LANES, (block + 1) * LANES)
        for part in range(2):
            target[part * HALF : (part + 1) * HALF, at] = piece[:, part * LANES : (part + 1) * LANES]
    if not sent:
        fill_stack(out, rows[...])


def fill_stack(stack, source):
    length = source.shape[1]
    source = source.astype(F32)
    for a in range(COARSE):
        shift = (24 - 8 * a) % length
        moved = pltpu.roll(source, shift, 1) if shift else source
        stack[a * 32 : (a + 1) * 32] = moved.astype(BF16)


def fine_sum(product, trim):
    length = product.shape[1]
    total = None
    for b in range(FINE):
        piece = product[b * 32 : (b + 1) * 32]
        if b + trim:
            piece = pltpu.roll(piece, length - b - trim, 1)
        total = piece if total is None else total + piece
    return total


def product_of(bank, own, partner, trim):
    both = jnp.concatenate([own[...], partner[...]] * 2, axis=0)
    return fine_sum(jnp.dot(bank, both, preferred_element_type=F32), trim)


def rounded(total, rim):
    total = total[:, 0 : BINS + 2 * rim]
    return jnp.where(inside_mask(*total.shape, rim), total, 0.0).astype(BF16)


def merge_sent_kernel(trim, rim, own, theirs, bank, sent, partner):
    fill_stack(partner, theirs[...])
    sent[...] = rounded(product_of(bank[1], own, partner, trim), rim)


def merge_kept_kernel(trim, rim, own, partner, bank, after):
    fill_stack(after, rounded(product_of(bank[0], own, partner, trim), rim))


def merge_last_kernel(own, theirs, bank, out, partner):
    fill_stack(partner, theirs[...])
    for half in range(2):
        total = product_of(bank[half], own, partner, RIM_LATE)[:, 0:BINS].astype(BF16)
        for part in range(2):
            out[part, half * HALF : (half + 1) * HALF] = total[part * HALF : (part + 1) * HALF]


WHOLE = pl.BlockSpec(memory_space=pltpu.VMEM)
PARAMS = pltpu.CompilerParams(vmem_limit_bytes=VMEM)
BANK = jax.ShapeDtypeStruct((2, OUTS, 2 * COLS), BF16)
FRAMES = (FRAME, FRAME, FRAME_LATE, FRAME_LATE)
RIMS = (RIM, RIM, RIM_LATE, RIM_LATE)


def message(length):
    return jax.ShapeDtypeStruct((2 * HALF, length), BF16)


def shifted(length):
    return jax.ShapeDtypeStruct((COLS // 2, length), BF16)


def small_cost():
    return pl.CostEstimate(flops=1000, bytes_accessed=1000, transcendentals=0)


def prepare(chirp, taps, numbers):
    return pl.pallas_call(
        prepare_kernel,
        out_shape=(
            jax.ShapeDtypeStruct((2 * LANES, 2 * SPAN), BF16),
            BANK,
            jax.ShapeDtypeStruct((ROWS, 4 * PART), F32),
            jax.ShapeDtypeStruct((ROWS, LANES), F32),
        ),
        in_specs=[WHOLE] * 3,
        out_specs=(WHOLE,) * 4,
        scratch_shapes=[pltpu.VMEM((ROWS, LANES), F32)],
        compiler_params=PARAMS,
        cost_estimate=pl.CostEstimate(flops=1_000_000_000, bytes_accessed=2_000_000, transcendentals=0),
        name="prepare",
    )(chirp, taps, numbers)


def prepare_late(level, after, weights, numbers):
    return pl.pallas_call(
        functools.partial(prepare_late_kernel, level),
        out_shape=BANK,
        in_specs=[pl.BlockSpec(memory_space=pl.ANY), WHOLE, WHOLE],
        out_specs=WHOLE,
        compiler_params=PARAMS,
        cost_estimate=small_cost(),
        name=f"prepare_{level}",
    )(after, weights, numbers)


def compress(sent, echoes, even, odd, toeplitz):
    scratch = [pltpu.VMEM((FRAME // LANES * HALF, 2 * SPAN), BF16)]
    if not sent:
        scratch.append(pltpu.VMEM((2 * HALF, FRAME), BF16))
    return pl.pallas_call(
        functools.partial(compress_kernel, sent),
        out_shape=message(FRAME) if sent else shifted(FRAME),
        in_specs=[WHOLE] * 4,
        out_specs=WHOLE,
        scratch_shapes=scratch,
        compiler_params=PARAMS,
        cost_estimate=pl.CostEstimate(flops=200_000_000, bytes_accessed=1_000_000, transcendentals=0),
        name="compress_sent" if sent else "compress_kept",
    )(echoes, even, odd, toeplitz)


def merge_sent(level, own, theirs, bank):
    rim = RIMS[level + 1]
    return pl.pallas_call(
        functools.partial(merge_sent_kernel, RIMS[level] - rim, rim),
        out_shape=(message(FRAMES[level + 1]), shifted(FRAMES[level])),
        in_specs=[WHOLE] * 3,
        out_specs=(WHOLE, WHOLE),
        compiler_params=PARAMS,
        name=f"merge_{level}_sent",
    )(own, theirs, bank)


def merge_kept(level, own, partner, bank):
    rim = RIMS[level + 1]
    return pl.pallas_call(
        functools.partial(merge_kept_kernel, RIMS[level] - rim, rim),
        out_shape=shifted(FRAMES[level + 1]),
        in_specs=[WHOLE] * 3,
        out_specs=WHOLE,
        compiler_params=PARAMS,
        cost_estimate=small_cost(),
        name=f"merge_{level}_kept",
    )(own, partner, bank)


def merge_last(own, theirs, bank):
    return pl.pallas_call(
        merge_last_kernel,
        out_shape=jax.ShapeDtypeStruct((2, ROWS, BINS), BF16),
        in_specs=[WHOLE] * 3,
        out_specs=WHOLE,
        scratch_shapes=[pltpu.VMEM((COLS // 2, FRAMES[LEVELS - 1]), BF16)],
        compiler_params=PARAMS,
        name="merge_last",
    )(own, theirs, bank)


def body(echoes, transmit_chirp, band_weights, band_offsets, band_widths, child_rows):
    count = lax.axis_size("range")
    is_odd = lax.axis_index("range") % 2 == 1
    head = echoes[:, :, :HALO]
    tail = echoes[:, :, BINS - HALO :]
    pairs = [(i, i + 1) for i in range(1, count - 1, 2)]
    odd = lax.ppermute(jnp.where(is_odd, tail, head), "range", pairs + [(j, i) for i, j in pairs])
    pairs = [(i, i + 1) for i in range(0, count - 1, 2)]
    even = lax.ppermute(jnp.where(is_odd, head, tail), "range", pairs + [(j, i) for i, j in pairs])
    taps = jnp.swapaxes(band_weights, 3, 4).reshape(LEVELS, PART, ROWS)
    numbers = jnp.concatenate([band_offsets, band_widths, child_rows[:, None]], axis=1)
    toeplitz, bank, weights, numbers = prepare(transmit_chirp, taps, numbers)
    sent = compress(True, echoes, even, odd, toeplitz)
    blocks = lax.axis_size("aperture")
    own = None
    for level in range(LEVELS):
        theirs = lax.ppermute(sent, "aperture", [(i, i ^ (1 << level)) for i in range(blocks)])
        if level == 0:
            own = compress(False, echoes, even, odd, toeplitz)
        else:
            own = merge_kept(level - 1, own, partner, bank)
            bank = prepare_late(level, own, weights, numbers)
        if level + 1 < LEVELS:
            sent, partner = merge_sent(level, own, theirs, bank)
    return merge_last(own, theirs, bank)


def solution(mesh):
    return jax.shard_map(
        body,
        mesh=mesh,
        in_specs=(
            P(None, "aperture", "range"),
            P(),
            P(None, None, None, "aperture", None),
            P(None, None, "aperture"),
            P(None, None, "aperture"),
            P(None, "aperture"),
        ),
        out_specs=P(None, "aperture", "range"),
        check_vma=False,
    )
```

time: 56.5 us -> 47.9 us (0.85)
  blocking collectives: 22 us -> 0 us
  starting transfers between devices: 13.6 us -> 27.3 us
  Pallas kernels: 13.2 us -> 12 us
  waiting for transfers between devices: 5.63 us -> 6.51 us
  local copies, waits for them, and re-layouts: 1.5 us -> 0.67 us
  other arithmetic: 0.08 us -> 0.89 us
    all_to_all x1 -> x0, blocking collectives: 22 us -> none  [body(): lax.all_to_all(parts, 'aperture', 0, 0, axis_index_groups=groups, tiled=T...]
    ppermute x4 -> x6, starting transfers between devices: 13.6 us -> 27.3 us  [the longest x4 20 us: body(): lax.ppermute(sent, 'aperture', [(i, i ^ 1 << level) for i in range(blocks)])]
    ppermute x4 -> x6, waiting for transfers between devices: 5.63 us -> 6.51 us  [the longest x4 4.52 us: body(): lax.ppermute(sent, 'aperture', [(i, i ^ 1 << level) for i in range(blocks)])]
    select_n x0 -> x1, other arithmetic: none -> 0.88 us  [body(): jnp.where(is_odd, tail, head)]
    slice x1 -> x0, local copies, waits for them, and re-layouts: 0.87 us -> none  [body(): echoes[:, :, :HALO]]
    pallas_call x5 -> x12, Pallas kernels: 11.4 us -> 10.7 us  [the longest x3 2.78 us: merge_kept(): pl.pallas_call(functools.partial(merge_kept_kernel, RIMS[level] - rim, ri...]
  transfers between devices with their start and end apart: 4 -> 6, of which waited for: 3 -> 5; matrix products, arithmetic and copies ran while one was open for 0% -> 0% of each run, Pallas kernels for 7% -> 15%
where the time goes in v2:
time: 47.9 us; the launch traced here: 47.6 us
  starting transfers between devices  27.3 us (57%)
  Pallas kernels  12 us (25%)
  waiting for transfers between devices  6.51 us (14%)
  other arithmetic  0.89 us (2%)
  local copies, waits for them, and re-layouts  0.67 us (1%)
    ppermute x4, starting transfers between devices, body(): lax.ppermute(sent, 'aperture', [(i, i ^ 1 << level) for i in range(blocks)])  20 us
    ppermute x1, starting transfers between devices, body(): lax.ppermute(jnp.where(is_odd, tail, head), 'range', pairs + [(j, i) for...  5.45 us
    ppermute x4, waiting for transfers between devices, body(): lax.ppermute(sent, 'aperture', [(i, i ^ 1 << level) for i in range(blocks)])  4.52 us
    pallas_call x3, Pallas kernels, merge_kept(): pl.pallas_call(functools.partial(merge_kept_kernel, RIMS[level] - rim, ri...  2.78 us
    pallas_call x3, Pallas kernels, merge_sent(): pl.pallas_call(functools.partial(merge_sent_kernel, RIMS[level] - rim, ri...  2.59 us
    pallas_call x3, Pallas kernels, prepare_late(): pl.pallas_call(functools.partial(prepare_late_kernel, level), out_shape=B...  2.36 us
    pallas_call x1, Pallas kernels, merge_last(): pl.pallas_call(merge_last_kernel, out_shape=jax.ShapeDtypeStruct((2, ROWS...  1.99 us
    ppermute x1, waiting for transfers between devices, body(): lax.ppermute(jnp.where(is_odd, head, tail), 'range', pairs + [(j, i) for...  1.98 us
  transfers between devices with their start and end apart: 6, of which 5 were waited for; matrix products, arithmetic and copies ran while one was open for 0% of the time, Pallas kernels for 15%

profile of v2, /device:TPU:40, one launch (start us, length us, event | category | flops | bytes accessed | tf_op | source)
XLA Modules:
  0.0 47.6 jit_solution(17089675043912159295)
XLA Ops:
  0.0 0.9 %broadcast_select_fusion = (bf16[2,32,384]{2,1,0:T(8,128)(2,1)S(1)}, bf16[2,32,384]{2,1,0:T(8,128)(2,1)S(1)}) fusion(pred[]{:T(512)S(6)} %eq.5, bf16[2,32,1024]{2,1,0:T(8,128)(2,1)} %echoes.3), kind=kLoop, calls=%fused_computation | loop fusion | flops 49152 | bytes 196609 | tf_op jit(solution)/shard_map/jit(_where)/select_n | solution.py:319
  0.9 0.0 copy-start.3
  0.9 5.5 %collective-permute-start.1 = (bf16[2,32,384]{2,1,0:T(8,128)(2,1)S(1)}, bf16[2,32,384]{2,1,0:T(8,128)(2,1)S(1)}, u32[]{:S(2)}, u32[]{:S(2)}) collective-permute-start(bf16[2,32,384]{2,1,0:T(8,128)(2,1)S(1)} %get-tuple-element.25), channel_id=1, source_target_pairs={{1,2},{3,4},{5,6},{2,1},{4,3},{6,5},{9,10},{11,12},{13,14},{10,9},... | collective-permute-start | bytes 147464 | tf_op jit(solution)/shard_map/ppermute | solution.py:319
  6.4 1.9 %collective-permute-start = (bf16[2,32,384]{2,1,0:T(8,128)(2,1)S(1)}, bf16[2,32,384]{2,1,0:T(8,128)(2,1)S(1)}, u32[]{:S(2)}, u32[]{:S(2)}) collective-permute-start(bf16[2,32,384]{2,1,0:T(8,128)(2,1)S(1)} %get-tuple-element.26), channel_id=1, source_target_pairs={{0,1},{2,3},{4,5},{6,7},{1,0},{3,2},{5,4},{7,6},{8,9},{10,11},{12,... | collective-permute-start | bytes 147464 | tf_op jit(solution)/shard_map/ppermute | solution.py:321
  8.3 0.0 copy-done.4
  8.3 0.0 copy-done.5
  8.3 0.0 copy-done.3
  8.3 0.0 copy-start.2
  8.4 0.6 %copy-done.2 = bf16[2,512]{1,0:T(2,128)(2,1)S(1)} copy-done((bf16[2,512]{1,0:T(2,128)(2,1)S(1)}, bf16[2,512]{1,0:T(2,128)(2,1)}, u32[]{:S(2)}) %copy-start.2) | copy-done | bytes 2072
  9.0 1.3 %prepare.1 = (bf16[256,1280]{1,0:T(8,128)(2,1)S(1)}, bf16[2,256,768]{2,1,0:T(8,128)(2,1)S(1)}, f32[32,256]{1,0:T(8,128)S(1)}, f32[32,128]{1,0:T(8,128)S(1)}) custom-call(bf16[2,512]{1,0:T(2,128)(2,1)S(1)} %copy-done.2, f32[4,64,32]{2,1,0:T(8,128)S(1)} %bitcast.6, s32[4,5,32]{2,1,0:T(8,128)S(1)} %pad_add_fusion.numbers_in), custom_call_target="tpu_custom_call" | custom-call | flops 1000000000 | bytes 2000000 | tf_op jit(solution)/shard_map/prepare/pallas_call | solution.py:231
  10.3 0.0 collective-permute-done.1.odd
  10.4 2.0 %collective-permute-done.even = bf16[2,32,384]{2,1,0:T(8,128)(2,1)S(1)} collective-permute-done((bf16[2,32,384]{2,1,0:T(8,128)(2,1)S(1)}, bf16[2,32,384]{2,1,0:T(8,128)(2,1)S(1)}, u32[]{:S(2)}, u32[]{:S(2)}) %collective-permute-start) | collective-permute-done | bytes 49184 | tf_op jit(solution)/shard_map/ppermute | solution.py:321
  12.3 0.4 compress_sent.1
  12.7 1.9 %collective-permute-start.2 = (bf16[32,1280]{1,0:T(8,128)(2,1)S(1)}, bf16[32,1280]{1,0:T(8,128)(2,1)S(1)}, u32[]{:S(2)}, u32[]{:S(2)}) collective-permute-start(bf16[32,1280]{1,0:T(8,128)(2,1)S(1)} %compress_sent.1), channel_id=1, source_target_pairs={{0,8},{8,0},{16,24},{24,16},{32,40},{40,32},{48,56},{56,48},{64,72... | collective-permute-start | bytes 245768 | tf_op jit(solution)/shard_map/ppermute | solution.py:329
  14.7 0.6 %compress_kept.1.own = bf16[192,1280]{1,0:T(8,128)(2,1)S(1)} custom-call(bf16[2,32,1024]{2,1,0:T(8,128)(2,1)S(1)} %copy-done, bf16[2,32,384]{2,1,0:T(8,128)(2,1)S(1)} %collective-permute-done.even, bf16[2,32,384]{2,1,0:T(8,128)(2,1)S(1)} %collective-permute-done.1.odd, bf16[256,1280]{1,0:T(8,128)(2,1)S(1)} %get-tuple-element.15.toeplitz), custom_call_target="tpu_custom_call" | custom-call | flops 200000000 | bytes 1000000 | tf_op jit(solution)/shard_map/compress_kept/pallas_call | solution.py:264
  15.2 0.7 %collective-permute-done.2.theirs = bf16[32,1280]{1,0:T(8,128)(2,1)S(1)} collective-permute-done((bf16[32,1280]{1,0:T(8,128)(2,1)S(1)}, bf16[32,1280]{1,0:T(8,128)(2,1)S(1)}, u32[]{:S(2)}, u32[]{:S(2)}) %collective-permute-start.2) | collective-permute-done | bytes 81952 | tf_op jit(solution)/shard_map/ppermute | solution.py:329
  15.9 0.9 %merge_0_sent.1 = (bf16[32,1280]{1,0:T(8,128)(2,1)S(1)}, bf16[192,1280]{1,0:T(8,128)(2,1)S(1)}) custom-call(bf16[192,1280]{1,0:T(8,128)(2,1)S(1)} %compress_kept.1.own, bf16[32,1280]{1,0:T(8,128)(2,1)S(1)} %collective-permute-done.2.theirs, bf16[2,256,768]{2,1,0:T(8,128)(2,1)S(1)} %get-tuple-element.16.bank), custom_call_target="tpu_custom_call" | custom-call | tf_op jit(solution)/shard_map/merge_0_sent/pallas_call | solution.py:278
  16.8 4.3 %collective-permute-start.3 = (bf16[32,1280]{1,0:T(8,128)(2,1)S(1)}, bf16[32,1280]{1,0:T(8,128)(2,1)S(1)}, u32[]{:S(2)}, u32[]{:S(2)}) collective-permute-start(bf16[32,1280]{1,0:T(8,128)(2,1)S(1)} %get-tuple-element.18), channel_id=1, source_target_pairs={{0,16},{8,24},{16,0},{24,8},{32,48},{40,56},{48,32},{56,40},{64,80... | collective-permute-start | bytes 245768 | tf_op jit(solution)/shard_map/ppermute | solution.py:329
  21.1 1.0 %merge_0_kept.1.after.own = bf16[192,1280]{1,0:T(8,128)(2,1)S(1)} custom-call(bf16[192,1280]{1,0:T(8,128)(2,1)S(1)} %compress_kept.1.own, bf16[192,1280]{1,0:T(8,128)(2,1)S(1)} %get-tuple-element.17.partner, bf16[2,256,768]{2,1,0:T(8,128)(2,1)S(1)} %get-tuple-element.16.bank), custom_call_target="tpu_custom_call" | custom-call | flops 1000 | bytes 1000 | tf_op jit(solution)/shard_map/merge_0_kept/pallas_call | solution.py:290
  22.0 0.8 %prepare_1.1.bank = bf16[2,256,768]{2,1,0:T(8,128)(2,1)S(1)} custom-call(bf16[192,1280]{1,0:T(8,128)(2,1)S(1)} %merge_0_kept.1.after.own, f32[32,256]{1,0:T(8,128)S(1)} %get-tuple-element.19.weights, f32[32,128]{1,0:T(8,128)S(1)} %get-tuple-element.20.numbers), custom_call_target="tpu_custom_call" | custom-call | flops 1000 | bytes 1000 | tf_op jit(solution)/shard_map/prepare_1/pallas_call | solution.py:249
  22.8 1.0 %collective-permute-done.3.theirs = bf16[32,1280]{1,0:T(8,128)(2,1)S(1)} collective-permute-done((bf16[32,1280]{1,0:T(8,128)(2,1)S(1)}, bf16[32,1280]{1,0:T(8,128)(2,1)S(1)}, u32[]{:S(2)}, u32[]{:S(2)}) %collective-permute-start.3) | collective-permute-done | bytes 81952 | tf_op jit(solution)/shard_map/ppermute | solution.py:329
  23.8 0.9 %merge_1_sent.1 = (bf16[32,1152]{1,0:T(8,128)(2,1)S(1)}, bf16[192,1280]{1,0:T(8,128)(2,1)S(1)}) custom-call(bf16[192,1280]{1,0:T(8,128)(2,1)S(1)} %merge_0_kept.1.after.own, bf16[32,1280]{1,0:T(8,128)(2,1)S(1)} %collective-permute-done.3.theirs, bf16[2,256,768]{2,1,0:T(8,128)(2,1)S(1)} %prepare_1.1.bank), custom_call_target="tpu_custom_call" | custom-call | tf_op jit(solution)/shard_map/merge_1_sent/pallas_call | solution.py:278
  24.7 6.1 %collective-permute-start.4 = (bf16[32,1152]{1,0:T(8,128)(2,1)S(1)}, bf16[32,1152]{1,0:T(8,128)(2,1)S(1)}, u32[]{:S(2)}, u32[]{:S(2)}) collective-permute-start(bf16[32,1152]{1,0:T(8,128)(2,1)S(1)} %get-tuple-element.22), channel_id=1, source_target_pairs={{0,32},{8,40},{16,48},{24,56},{32,0},{40,8},{48,16},{56,24},{64,96... | collective-permute-start | bytes 221192 | tf_op jit(solution)/shard_map/ppermute | solution.py:329
  30.8 1.0 %merge_1_kept.1.after.own = bf16[192,1152]{1,0:T(8,128)(2,1)S(1)} custom-call(bf16[192,1280]{1,0:T(8,128)(2,1)S(1)} %merge_0_kept.1.after.own, bf16[192,1280]{1,0:T(8,128)(2,1)S(1)} %get-tuple-element.21.partner, bf16[2,256,768]{2,1,0:T(8,128)(2,1)S(1)} %prepare_1.1.bank), custom_call_target="tpu_custom_call" | custom-call | flops 1000 | bytes 1000 | tf_op jit(solution)/shard_map/merge_1_kept/pallas_call | solution.py:290
  31.8 0.8 %prepare_2.1.bank = bf16[2,256,768]{2,1,0:T(8,128)(2,1)S(1)} custom-call(bf16[192,1152]{1,0:T(8,128)(2,1)S(1)} %merge_1_kept.1.after.own, f32[32,256]{1,0:T(8,128)S(1)} %get-tuple-element.19.weights, f32[32,128]{1,0:T(8,128)S(1)} %get-tuple-element.20.numbers), custom_call_target="tpu_custom_call" | custom-call | flops 1000 | bytes 1000 | tf_op jit(solution)/shard_map/prepare_2/pallas_call | solution.py:249
  32.6 1.9 %collective-permute-done.4.theirs = bf16[32,1152]{1,0:T(8,128)(2,1)S(1)} collective-permute-done((bf16[32,1152]{1,0:T(8,128)(2,1)S(1)}, bf16[32,1152]{1,0:T(8,128)(2,1)S(1)}, u32[]{:S(2)}, u32[]{:S(2)}) %collective-permute-start.4) | collective-permute-done | bytes 73760 | tf_op jit(solution)/shard_map/ppermute | solution.py:329
  34.5 0.8 %merge_2_sent.1 = (bf16[32,1152]{1,0:T(8,128)(2,1)S(1)}, bf16[192,1152]{1,0:T(8,128)(2,1)S(1)}) custom-call(bf16[192,1152]{1,0:T(8,128)(2,1)S(1)} %merge_1_kept.1.after.own, bf16[32,1152]{1,0:T(8,128)(2,1)S(1)} %collective-permute-done.4.theirs, bf16[2,256,768]{2,1,0:T(8,128)(2,1)S(1)} %prepare_2.1.bank), custom_call_target="tpu_custom_call" | custom-call | tf_op jit(solution)/shard_map/merge_2_sent/pallas_call | solution.py:278
  35.3 7.7 %collective-permute-start.5 = (bf16[32,1152]{1,0:T(8,128)(2,1)S(1)}, bf16[32,1152]{1,0:T(8,128)(2,1)S(1)}, u32[]{:S(2)}, u32[]{:S(2)}) collective-permute-start(bf16[32,1152]{1,0:T(8,128)(2,1)S(1)} %get-tuple-element.24), channel_id=1, source_target_pairs={{0,64},{8,72},{16,80},{24,88},{32,96},{40,104},{48,112},{56,120},{... | collective-permute-start | bytes 221192 | tf_op jit(solution)/shard_map/ppermute | solution.py:329
  43.0 0.9 %merge_2_kept.1.after.own = bf16[192,1152]{1,0:T(8,128)(2,1)S(1)} custom-call(bf16[192,1152]{1,0:T(8,128)(2,1)S(1)} %merge_1_kept.1.after.own, bf16[192,1152]{1,0:T(8,128)(2,1)S(1)} %get-tuple-element.23.partner, bf16[2,256,768]{2,1,0:T(8,128)(2,1)S(1)} %prepare_2.1.bank), custom_call_target="tpu_custom_call" | custom-call | flops 1000 | bytes 1000 | tf_op jit(solution)/shard_map/merge_2_kept/pallas_call | solution.py:290
  43.9 0.8 %prepare_3.1.bank = bf16[2,256,768]{2,1,0:T(8,128)(2,1)S(1)} custom-call(bf16[192,1152]{1,0:T(8,128)(2,1)S(1)} %merge_2_kept.1.after.own, f32[32,256]{1,0:T(8,128)S(1)} %get-tuple-element.19.weights, f32[32,128]{1,0:T(8,128)S(1)} %get-tuple-element.20.numbers), custom_call_target="tpu_custom_call" | custom-call | flops 1000 | bytes 1000 | tf_op jit(solution)/shard_map/prepare_3/pallas_call | solution.py:249
  44.7 0.9 %collective-permute-done.5.theirs = bf16[32,1152]{1,0:T(8,128)(2,1)S(1)} collective-permute-done((bf16[32,1152]{1,0:T(8,128)(2,1)S(1)}, bf16[32,1152]{1,0:T(8,128)(2,1)S(1)}, u32[]{:S(2)}, u32[]{:S(2)}) %collective-permute-start.5) | collective-permute-done | bytes 73760 | tf_op jit(solution)/shard_map/ppermute | solution.py:329
  45.6 2.0 %merge_last.1 = bf16[2,32,1024]{2,1,0:T(8,128)(2,1)} custom-call(bf16[192,1152]{1,0:T(8,128)(2,1)S(1)} %merge_2_kept.1.after.own, bf16[32,1152]{1,0:T(8,128)(2,1)S(1)} %collective-permute-done.5.theirs, bf16[2,256,768]{2,1,0:T(8,128)(2,1)S(1)} %prepare_3.1.bank), custom_call_target="tpu_custom_call" | custom-call | tf_op jit(solution)/shard_map/merge_last/pallas_call | solution.py:302
  (7 shorter events, 0.0 us)
Async XLA Ops:
  0.0 8.4 %copy-start.1 = (f32[4,2,2,32,16]{3,4,2,1,0:T(8,128)S(1)}, f32[4,2,2,32,16]{3,4,2,1,0:T(8,128)}, u32[]{:S(2)}) copy-start(f32[4,2,2,32,16]{3,4,2,1,0:T(8,128)} %param.8) | copy-start | bytes 98308
  0.0 8.3 %copy-start.4 = (s32[4,2,32]{2,1,0:T(2,128)S(1)}, s32[4,2,32]{2,1,0:T(2,128)}, u32[]{:S(2)}) copy-start(s32[4,2,32]{2,1,0:T(2,128)} %param.9) | copy-start | bytes 3076
  0.0 8.3 %copy-start.5 = (s32[4,32]{1,0:T(4,128)S(1)}, s32[4,32]{1,0:T(4,128)}, u32[]{:S(2)}) copy-start(s32[4,32]{1,0:T(4,128)} %param.11) | copy-start | bytes 1540
  0.9 7.4 %copy-start.3 = (s32[4,2,32]{2,1,0:T(2,128)S(1)}, s32[4,2,32]{2,1,0:T(2,128)}, u32[]{:S(2)}) copy-start(s32[4,2,32]{2,1,0:T(2,128)} %param.10) | copy-start | bytes 3076
  0.9 9.5 %collective-permute-start.1 = (bf16[2,32,384]{2,1,0:T(8,128)(2,1)S(1)}, bf16[2,32,384]{2,1,0:T(8,128)(2,1)S(1)}, u32[]{:S(2)}, u32[]{:S(2)}) collective-permute-start(bf16[2,32,384]{2,1,0:T(8,128)(2,1)S(1)} %get-tuple-element.25), channel_id=1, source_target_pairs={{1,2},{3,4},{5,6},{2,1},{4,3},{6,5},{9,10},{11,12},{13,14},{10,9},... | collective-permute-start | bytes 147464 | tf_op jit(solution)/shard_map/ppermute | solution.py:319
  6.4 6.0 %collective-permute-start = (bf16[2,32,384]{2,1,0:T(8,128)(2,1)S(1)}, bf16[2,32,384]{2,1,0:T(8,128)(2,1)S(1)}, u32[]{:S(2)}, u32[]{:S(2)}) collective-permute-start(bf16[2,32,384]{2,1,0:T(8,128)(2,1)S(1)} %get-tuple-element.26), channel_id=1, source_target_pairs={{0,1},{2,3},{4,5},{6,7},{1,0},{3,2},{5,4},{7,6},{8,9},{10,11},{12,... | collective-permute-start | bytes 147464 | tf_op jit(solution)/shard_map/ppermute | solution.py:321
  8.3 0.7 %copy-start.2 = (bf16[2,512]{1,0:T(2,128)(2,1)S(1)}, bf16[2,512]{1,0:T(2,128)(2,1)}, u32[]{:S(2)}) copy-start(bf16[2,512]{1,0:T(2,128)(2,1)} %chirp.1) | copy-start | bytes 6148
  9.0 3.3 %copy-start = (bf16[2,32,1024]{2,1,0:T(8,128)(2,1)S(1)}, bf16[2,32,1024]{2,1,0:T(8,128)(2,1)}, u32[]{:S(2)}) copy-start(bf16[2,32,1024]{2,1,0:T(8,128)(2,1)} %echoes.3) | copy-start | bytes 393220
  12.7 3.2 %collective-permute-start.2 = (bf16[32,1280]{1,0:T(8,128)(2,1)S(1)}, bf16[32,1280]{1,0:T(8,128)(2,1)S(1)}, u32[]{:S(2)}, u32[]{:S(2)}) collective-permute-start(bf16[32,1280]{1,0:T(8,128)(2,1)S(1)} %compress_sent.1), channel_id=1, source_target_pairs={{0,8},{8,0},{16,24},{24,16},{32,40},{40,32},{48,56},{56,48},{64,72... | collective-permute-start | bytes 245768 | tf_op jit(solution)/shard_map/ppermute | solution.py:329
  16.8 7.0 %collective-permute-start.3 = (bf16[32,1280]{1,0:T(8,128)(2,1)S(1)}, bf16[32,1280]{1,0:T(8,128)(2,1)S(1)}, u32[]{:S(2)}, u32[]{:S(2)}) collective-permute-start(bf16[32,1280]{1,0:T(8,128)(2,1)S(1)} %get-tuple-element.18), channel_id=1, source_target_pairs={{0,16},{8,24},{16,0},{24,8},{32,48},{40,56},{48,32},{56,40},{64,80... | collective-permute-start | bytes 245768 | tf_op jit(solution)/shard_map/ppermute | solution.py:329
  24.7 9.8 %collective-permute-start.4 = (bf16[32,1152]{1,0:T(8,128)(2,1)S(1)}, bf16[32,1152]{1,0:T(8,128)(2,1)S(1)}, u32[]{:S(2)}, u32[]{:S(2)}) collective-permute-start(bf16[32,1152]{1,0:T(8,128)(2,1)S(1)} %get-tuple-element.22), channel_id=1, source_target_pairs={{0,32},{8,40},{16,48},{24,56},{32,0},{40,8},{48,16},{56,24},{64,96... | collective-permute-start | bytes 221192 | tf_op jit(solution)/shard_map/ppermute | solution.py:329
  35.3 10.3 %collective-permute-start.5 = (bf16[32,1152]{1,0:T(8,128)(2,1)S(1)}, bf16[32,1152]{1,0:T(8,128)(2,1)S(1)}, u32[]{:S(2)}, u32[]{:S(2)}) collective-permute-start(bf16[32,1152]{1,0:T(8,128)(2,1)S(1)} %get-tuple-element.24), channel_id=1, source_target_pairs={{0,64},{8,72},{16,80},{24,88},{32,96},{40,104},{48,112},{56,120},{... | collective-permute-start | bytes 221192 | tf_op jit(solution)/shard_map/ppermute | solution.py:329

commit v3 on v2

--- a/solution.py
+++ b/solution.py
@@ -120,10 +120,15 @@
     return (bins >= 0) & (bins < (BINS * lax.axis_size("range")))
 
 
-def compress_kernel(sent, echoes, even, odd, toeplitz, out, window, rows=None):
+def takes_early(place):
+    return place == lax.axis_size("range") // 2
+
+
+def compress_kernel(sent, echoes, odd, late, early, toeplitz, out, window, rows=None):
     side = (lax.axis_index("aperture") & 1) ^ 1 if sent else lax.axis_index("aperture") & 1
     at = pl.multiple_of(side * HALF, HALF)
     is_odd = (lax.axis_index("range") & 1) == 1
+    is_early = takes_early(lax.axis_index("range"))
     blocks = FRAME // LANES
     tiles = SPAN // LANES
     first = HALO // LANES
@@ -135,7 +140,11 @@
                 piece = echoes[part, pl.ds(at, HALF), spot : spot + LANES]
             else:
                 spot = (tile if tile < first else tile - last) * LANES
-                ours = even[part, pl.ds(at, HALF), spot : spot + LANES]
+                ours = jnp.where(
+                    is_early,
+                    early[part, pl.ds(at, HALF), spot : spot + LANES],
+                    late[part, pl.ds(at, HALF), spot : spot + LANES],
+                )
                 other = odd[part, pl.ds(at, HALF), spot : spot + LANES]
                 if tile < first:
                     piece = jnp.where(is_odd, ours, other)
@@ -257,20 +266,20 @@
     )(after, weights, numbers)
 
 
-def compress(sent, echoes, even, odd, toeplitz):
+def compress(sent, echoes, odd, late, early, toeplitz):
     scratch = [pltpu.VMEM((FRAME // LANES * HALF, 2 * SPAN), BF16)]
     if not sent:
         scratch.append(pltpu.VMEM((2 * HALF, FRAME), BF16))
     return pl.pallas_call(
         functools.partial(compress_kernel, sent),
         out_shape=message(FRAME) if sent else shifted(FRAME),
-        in_specs=[WHOLE] * 4,
+        in_specs=[WHOLE] * 5,
         out_specs=WHOLE,
         scratch_shapes=scratch,
         compiler_params=PARAMS,
         cost_estimate=pl.CostEstimate(flops=200_000_000, bytes_accessed=1_000_000, transcendentals=0),
         name="compress_sent" if sent else "compress_kept",
-    )(echoes, even, odd, toeplitz)
+    )(echoes, odd, late, early, toeplitz)
 
 
 def merge_sent(level, own, theirs, bank):
@@ -315,20 +324,23 @@
     is_odd = lax.axis_index("range") % 2 == 1
     head = echoes[:, :, :HALO]
     tail = echoes[:, :, BINS - HALO :]
+    between = jnp.where(lax.axis_index("range") % 2 == 0, head, tail)
+    within = jnp.where(is_odd, head, tail)
+    within_late = jnp.where(lax.axis_index("range") % 2 != 1, tail, head)
     pairs = [(i, i + 1) for i in range(1, count - 1, 2)]
-    odd = lax.ppermute(jnp.where(is_odd, tail, head), "range", pairs + [(j, i) for i, j in pairs])
-    pairs = [(i, i + 1) for i in range(0, count - 1, 2)]
-    even = lax.ppermute(jnp.where(is_odd, head, tail), "range", pairs + [(j, i) for i, j in pairs])
+    early = lax.ppermute(within, "range", [(i ^ 1, i) for i in range(count) if takes_early(i)])
+    odd = lax.ppermute(between, "range", pairs + [(j, i) for i, j in pairs])
+    late = lax.ppermute(within_late, "range", [(i ^ 1, i) for i in range(count) if not takes_early(i)])
     taps = jnp.swapaxes(band_weights, 3, 4).reshape(LEVELS, PART, ROWS)
     numbers = jnp.concatenate([band_offsets, band_widths, child_rows[:, None]], axis=1)
     toeplitz, bank, weights, numbers = prepare(transmit_chirp, taps, numbers)
-    sent = compress(True, echoes, even, odd, toeplitz)
+    sent = compress(True, echoes, odd, late, early, toeplitz)
     blocks = lax.axis_size("aperture")
     own = None
     for level in range(LEVELS):
         theirs = lax.ppermute(sent, "aperture", [(i, i ^ (1 << level)) for i in range(blocks)])
         if level == 0:
-            own = compress(False, echoes, even, odd, toeplitz)
+            own = compress(False, echoes, odd, late, early, toeplitz)
         else:
             own = merge_kept(level - 1, own, partner, bank)
             bank = prepare_late(level, own, weights, numbers)

time: 47.9 us -> 47.4 us (0.990)
  the two profiles are of different devices: /device:TPU:40 before, /device:TPU:28 now
where the time goes in v3:
time: 47.4 us; the launch traced here: 47 us
  starting transfers between devices  26.8 us (57%)
  Pallas kernels  12 us (25%)
  waiting for transfers between devices  6.5 us (14%)
  other arithmetic  0.89 us (2%)
  local copies, waits for them, and re-layouts  0.67 us (1%)
    ppermute x4, starting transfers between devices, body(): lax.ppermute(sent, 'aperture', [(i, i ^ 1 << level) for i in range(blocks)])  20 us
    ppermute x4, waiting for transfers between devices, body(): lax.ppermute(sent, 'aperture', [(i, i ^ 1 << level) for i in range(blocks)])  4.52 us
    ppermute x1, starting transfers between devices, body(): odd = lax.ppermute(between, 'range', pairs + [(j, i) for i, j in pairs])  4.22 us
    pallas_call x3, Pallas kernels, merge_kept(): pl.pallas_call(functools.partial(merge_kept_kernel, RIMS[level] - rim, ri...  2.78 us
    pallas_call x3, Pallas kernels, merge_sent(): pl.pallas_call(functools.partial(merge_sent_kernel, RIMS[level] - rim, ri...  2.58 us
    pallas_call x3, Pallas kernels, prepare_late(): pl.pallas_call(functools.partial(prepare_late_kernel, level), out_shape=B...  2.36 us
    pallas_call x1, Pallas kernels, merge_last(): pl.pallas_call(merge_last_kernel, out_shape=jax.ShapeDtypeStruct((2, ROWS...  1.99 us
    ppermute x1, waiting for transfers between devices, body(): lax.ppermute(within_late, 'range', [(i ^ 1, i) for i in range(count) if n...  1.97 us
  transfers between devices with their start and end apart: 7, of which 5 were waited for; matrix products, arithmetic and copies ran while one was open for 0% of the time, Pallas kernels for 15%

profile of v3, /device:TPU:28, one launch (start us, length us, event | category | flops | bytes accessed | tf_op | source)
XLA Modules:
  0.0 47.0 jit_solution(14886843345724139010)
XLA Ops:
  0.0 0.9 %broadcast_select_fusion = (bf16[2,32,384]{2,1,0:T(8,128)(2,1)S(1)}, bf16[2,32,384]{2,1,0:T(8,128)(2,1)S(1)}, bf16[2,32,384]{2,1,0:T(8,128)(2,1)S(1)}) fusion(pred[]{:T(512)S(6)} %eq.11, bf16[2,32,1024]{2,1,0:T(8,128)(2,1)} %echoes.3, pred[]{:T(512)S(6)} %eq.10, pred[]{:T(512)S(6)} %ne.14), kind=kLoop, calls=%fused_computation | loop fusion | flops 73728 | bytes 245763 | tf_op jit(solution)/shard_map/jit(_where)/select_n | solution.py:328
  0.9 0.0 copy-start.3
  0.9 0.7 %collective-permute-start.2 = (bf16[2,32,384]{2,1,0:T(8,128)(2,1)S(1)}, bf16[2,32,384]{2,1,0:T(8,128)(2,1)S(1)}, u32[]{:S(2)}, u32[]{:S(2)}) collective-permute-start(bf16[2,32,384]{2,1,0:T(8,128)(2,1)S(1)} %get-tuple-element.25), channel_id=1, source_target_pairs={{5,4},{13,12},{21,20},{29,28},{37,36},{45,44},{53,52},{61,60},{69,... | collective-permute-start | bytes 147464 | tf_op jit(solution)/shard_map/ppermute | solution.py:331
  1.6 0.0 copy-start.5
  1.6 4.2 %collective-permute-start = (bf16[2,32,384]{2,1,0:T(8,128)(2,1)S(1)}, bf16[2,32,384]{2,1,0:T(8,128)(2,1)S(1)}, u32[]{:S(2)}, u32[]{:S(2)}) collective-permute-start(bf16[2,32,384]{2,1,0:T(8,128)(2,1)S(1)} %get-tuple-element.26), channel_id=1, source_target_pairs={{1,2},{3,4},{5,6},{2,1},{4,3},{6,5},{9,10},{11,12},{13,14},{10,9},... | collective-permute-start | bytes 147464 | tf_op jit(solution)/shard_map/ppermute | solution.py:332
  5.8 1.9 %collective-permute-start.1 = (bf16[2,32,384]{2,1,0:T(8,128)(2,1)S(1)}, bf16[2,32,384]{2,1,0:T(8,128)(2,1)S(1)}, u32[]{:S(2)}, u32[]{:S(2)}) collective-permute-start(bf16[2,32,384]{2,1,0:T(8,128)(2,1)S(1)} %get-tuple-element.27), channel_id=1, source_target_pairs={{1,0},{0,1},{3,2},{2,3},{4,5},{7,6},{6,7},{9,8},{8,9},{11,10},{10,... | collective-permute-start | bytes 147464 | tf_op jit(solution)/shard_map/ppermute | solution.py:333
  7.8 0.0 copy-start.2
  7.8 0.6 %copy-done.2 = bf16[2,512]{1,0:T(2,128)(2,1)S(1)} copy-done((bf16[2,512]{1,0:T(2,128)(2,1)S(1)}, bf16[2,512]{1,0:T(2,128)(2,1)}, u32[]{:S(2)}) %copy-start.2) | copy-done | bytes 2072
  8.5 1.3 %prepare.1 = (bf16[256,1280]{1,0:T(8,128)(2,1)S(1)}, bf16[2,256,768]{2,1,0:T(8,128)(2,1)S(1)}, f32[32,256]{1,0:T(8,128)S(1)}, f32[32,128]{1,0:T(8,128)S(1)}) custom-call(bf16[2,512]{1,0:T(2,128)(2,1)S(1)} %copy-done.2, f32[4,64,32]{2,1,0:T(8,128)S(1)} %bitcast.6, s32[4,5,32]{2,1,0:T(8,128)S(1)} %pad_add_fusion.numbers_in), custom_call_target="tpu_custom_call" | custom-call | flops 1000000000 | bytes 2000000 | tf_op jit(solution)/shard_map/prepare/pallas_call | solution.py:240
  9.8 0.0 collective-permute-done.2.early
  9.8 0.0 collective-permute-done.odd
  9.8 2.0 %collective-permute-done.1.late = bf16[2,32,384]{2,1,0:T(8,128)(2,1)S(1)} collective-permute-done((bf16[2,32,384]{2,1,0:T(8,128)(2,1)S(1)}, bf16[2,32,384]{2,1,0:T(8,128)(2,1)S(1)}, u32[]{:S(2)}, u32[]{:S(2)}) %collective-permute-start.1) | collective-permute-done | bytes 49184 | tf_op jit(solution)/shard_map/ppermute | solution.py:333
  11.8 0.4 compress_sent.1
  12.2 1.9 %collective-permute-start.3 = (bf16[32,1280]{1,0:T(8,128)(2,1)S(1)}, bf16[32,1280]{1,0:T(8,128)(2,1)S(1)}, u32[]{:S(2)}, u32[]{:S(2)}) collective-permute-start(bf16[32,1280]{1,0:T(8,128)(2,1)S(1)} %compress_sent.1), channel_id=1, source_target_pairs={{0,8},{8,0},{16,24},{24,16},{32,40},{40,32},{48,56},{56,48},{64,72... | collective-permute-start | bytes 245768 | tf_op jit(solution)/shard_map/ppermute | solution.py:341
  14.1 0.6 %compress_kept.1.own = bf16[192,1280]{1,0:T(8,128)(2,1)S(1)} custom-call(bf16[2,32,1024]{2,1,0:T(8,128)(2,1)S(1)} %copy-done, bf16[2,32,384]{2,1,0:T(8,128)(2,1)S(1)} %collective-permute-done.odd, bf16[2,32,384]{2,1,0:T(8,128)(2,1)S(1)} %collective-permute-done.1.late, bf16[2,32,384]{2,1,0:T(8,128)(2,1)S(1)} %collective-permute-done.2.early, ...), custom_call_target="tpu_custom_call" | custom-call | flops 200000000 | bytes 1000000 | tf_op jit(solution)/shard_map/compress_kept/pallas_call | solution.py:273
  14.7 0.7 %collective-permute-done.3.theirs = bf16[32,1280]{1,0:T(8,128)(2,1)S(1)} collective-permute-done((bf16[32,1280]{1,0:T(8,128)(2,1)S(1)}, bf16[32,1280]{1,0:T(8,128)(2,1)S(1)}, u32[]{:S(2)}, u32[]{:S(2)}) %collective-permute-start.3) | collective-permute-done | bytes 81952 | tf_op jit(solution)/shard_map/ppermute | solution.py:341
  15.4 0.9 %merge_0_sent.1 = (bf16[32,1280]{1,0:T(8,128)(2,1)S(1)}, bf16[192,1280]{1,0:T(8,128)(2,1)S(1)}) custom-call(bf16[192,1280]{1,0:T(8,128)(2,1)S(1)} %compress_kept.1.own, bf16[32,1280]{1,0:T(8,128)(2,1)S(1)} %collective-permute-done.3.theirs, bf16[2,256,768]{2,1,0:T(8,128)(2,1)S(1)} %get-tuple-element.16.bank), custom_call_target="tpu_custom_call" | custom-call | tf_op jit(solution)/shard_map/merge_0_sent/pallas_call | solution.py:287
  16.2 4.3 %collective-permute-start.4 = (bf16[32,1280]{1,0:T(8,128)(2,1)S(1)}, bf16[32,1280]{1,0:T(8,128)(2,1)S(1)}, u32[]{:S(2)}, u32[]{:S(2)}) collective-permute-start(bf16[32,1280]{1,0:T(8,128)(2,1)S(1)} %get-tuple-element.18), channel_id=1, source_target_pairs={{0,16},{8,24},{16,0},{24,8},{32,48},{40,56},{48,32},{56,40},{64,80... | collective-permute-start | bytes 245768 | tf_op jit(solution)/shard_map/ppermute | solution.py:341
  20.5 1.0 %merge_0_kept.1.after.own = bf16[192,1280]{1,0:T(8,128)(2,1)S(1)} custom-call(bf16[192,1280]{1,0:T(8,128)(2,1)S(1)} %compress_kept.1.own, bf16[192,1280]{1,0:T(8,128)(2,1)S(1)} %get-tuple-element.17.partner, bf16[2,256,768]{2,1,0:T(8,128)(2,1)S(1)} %get-tuple-element.16.bank), custom_call_target="tpu_custom_call" | custom-call | flops 1000 | bytes 1000 | tf_op jit(solution)/shard_map/merge_0_kept/pallas_call | solution.py:299
  21.5 0.8 %prepare_1.1.bank = bf16[2,256,768]{2,1,0:T(8,128)(2,1)S(1)} custom-call(bf16[192,1280]{1,0:T(8,128)(2,1)S(1)} %merge_0_kept.1.after.own, f32[32,256]{1,0:T(8,128)S(1)} %get-tuple-element.19.weights, f32[32,128]{1,0:T(8,128)S(1)} %get-tuple-element.20.numbers), custom_call_target="tpu_custom_call" | custom-call | flops 1000 | bytes 1000 | tf_op jit(solution)/shard_map/prepare_1/pallas_call | solution.py:258
  22.3 1.0 %collective-permute-done.4.theirs = bf16[32,1280]{1,0:T(8,128)(2,1)S(1)} collective-permute-done((bf16[32,1280]{1,0:T(8,128)(2,1)S(1)}, bf16[32,1280]{1,0:T(8,128)(2,1)S(1)}, u32[]{:S(2)}, u32[]{:S(2)}) %collective-permute-start.4) | collective-permute-done | bytes 81952 | tf_op jit(solution)/shard_map/ppermute | solution.py:341
  23.3 0.9 %merge_1_sent.1 = (bf16[32,1152]{1,0:T(8,128)(2,1)S(1)}, bf16[192,1280]{1,0:T(8,128)(2,1)S(1)}) custom-call(bf16[192,1280]{1,0:T(8,128)(2,1)S(1)} %merge_0_kept.1.after.own, bf16[32,1280]{1,0:T(8,128)(2,1)S(1)} %collective-permute-done.4.theirs, bf16[2,256,768]{2,1,0:T(8,128)(2,1)S(1)} %prepare_1.1.bank), custom_call_target="tpu_custom_call" | custom-call | tf_op jit(solution)/shard_map/merge_1_sent/pallas_call | solution.py:287
  24.2 6.1 %collective-permute-start.5 = (bf16[32,1152]{1,0:T(8,128)(2,1)S(1)}, bf16[32,1152]{1,0:T(8,128)(2,1)S(1)}, u32[]{:S(2)}, u32[]{:S(2)}) collective-permute-start(bf16[32,1152]{1,0:T(8,128)(2,1)S(1)} %get-tuple-element.22), channel_id=1, source_target_pairs={{0,32},{8,40},{16,48},{24,56},{32,0},{40,8},{48,16},{56,24},{64,96... | collective-permute-start | bytes 221192 | tf_op jit(solution)/shard_map/ppermute | solution.py:341
  30.3 1.0 %merge_1_kept.1.after.own = bf16[192,1152]{1,0:T(8,128)(2,1)S(1)} custom-call(bf16[192,1280]{1,0:T(8,128)(2,1)S(1)} %merge_0_kept.1.after.own, bf16[192,1280]{1,0:T(8,128)(2,1)S(1)} %get-tuple-element.21.partner, bf16[2,256,768]{2,1,0:T(8,128)(2,1)S(1)} %prepare_1.1.bank), custom_call_target="tpu_custom_call" | custom-call | flops 1000 | bytes 1000 | tf_op jit(solution)/shard_map/merge_1_kept/pallas_call | solution.py:299
  31.3 0.8 %prepare_2.1.bank = bf16[2,256,768]{2,1,0:T(8,128)(2,1)S(1)} custom-call(bf16[192,1152]{1,0:T(8,128)(2,1)S(1)} %merge_1_kept.1.after.own, f32[32,256]{1,0:T(8,128)S(1)} %get-tuple-element.19.weights, f32[32,128]{1,0:T(8,128)S(1)} %get-tuple-element.20.numbers), custom_call_target="tpu_custom_call" | custom-call | flops 1000 | bytes 1000 | tf_op jit(solution)/shard_map/prepare_2/pallas_call | solution.py:258
  32.0 1.9 %collective-permute-done.5.theirs = bf16[32,1152]{1,0:T(8,128)(2,1)S(1)} collective-permute-done((bf16[32,1152]{1,0:T(8,128)(2,1)S(1)}, bf16[32,1152]{1,0:T(8,128)(2,1)S(1)}, u32[]{:S(2)}, u32[]{:S(2)}) %collective-permute-start.5) | collective-permute-done | bytes 73760 | tf_op jit(solution)/shard_map/ppermute | solution.py:341
  34.0 0.8 %merge_2_sent.1 = (bf16[32,1152]{1,0:T(8,128)(2,1)S(1)}, bf16[192,1152]{1,0:T(8,128)(2,1)S(1)}) custom-call(bf16[192,1152]{1,0:T(8,128)(2,1)S(1)} %merge_1_kept.1.after.own, bf16[32,1152]{1,0:T(8,128)(2,1)S(1)} %collective-permute-done.5.theirs, bf16[2,256,768]{2,1,0:T(8,128)(2,1)S(1)} %prepare_2.1.bank), custom_call_target="tpu_custom_call" | custom-call | tf_op jit(solution)/shard_map/merge_2_sent/pallas_call | solution.py:287
  34.8 7.7 %collective-permute-start.6 = (bf16[32,1152]{1,0:T(8,128)(2,1)S(1)}, bf16[32,1152]{1,0:T(8,128)(2,1)S(1)}, u32[]{:S(2)}, u32[]{:S(2)}) collective-permute-start(bf16[32,1152]{1,0:T(8,128)(2,1)S(1)} %get-tuple-element.24), channel_id=1, source_target_pairs={{0,64},{8,72},{16,80},{24,88},{32,96},{40,104},{48,112},{56,120},{... | collective-permute-start | bytes 221192 | tf_op jit(solution)/shard_map/ppermute | solution.py:341
  42.5 0.9 %merge_2_kept.1.after.own = bf16[192,1152]{1,0:T(8,128)(2,1)S(1)} custom-call(bf16[192,1152]{1,0:T(8,128)(2,1)S(1)} %merge_1_kept.1.after.own, bf16[192,1152]{1,0:T(8,128)(2,1)S(1)} %get-tuple-element.23.partner, bf16[2,256,768]{2,1,0:T(8,128)(2,1)S(1)} %prepare_2.1.bank), custom_call_target="tpu_custom_call" | custom-call | flops 1000 | bytes 1000 | tf_op jit(solution)/shard_map/merge_2_kept/pallas_call | solution.py:299
  43.3 0.8 %prepare_3.1.bank = bf16[2,256,768]{2,1,0:T(8,128)(2,1)S(1)} custom-call(bf16[192,1152]{1,0:T(8,128)(2,1)S(1)} %merge_2_kept.1.after.own, f32[32,256]{1,0:T(8,128)S(1)} %get-tuple-element.19.weights, f32[32,128]{1,0:T(8,128)S(1)} %get-tuple-element.20.numbers), custom_call_target="tpu_custom_call" | custom-call | flops 1000 | bytes 1000 | tf_op jit(solution)/shard_map/prepare_3/pallas_call | solution.py:258
  44.1 0.9 %collective-permute-done.6.theirs = bf16[32,1152]{1,0:T(8,128)(2,1)S(1)} collective-permute-done((bf16[32,1152]{1,0:T(8,128)(2,1)S(1)}, bf16[32,1152]{1,0:T(8,128)(2,1)S(1)}, u32[]{:S(2)}, u32[]{:S(2)}) %collective-permute-start.6) | collective-permute-done | bytes 73760 | tf_op jit(solution)/shard_map/ppermute | solution.py:341
  45.1 2.0 %merge_last.1 = bf16[2,32,1024]{2,1,0:T(8,128)(2,1)} custom-call(bf16[192,1152]{1,0:T(8,128)(2,1)S(1)} %merge_2_kept.1.after.own, bf16[32,1152]{1,0:T(8,128)(2,1)S(1)} %collective-permute-done.6.theirs, bf16[2,256,768]{2,1,0:T(8,128)(2,1)S(1)} %prepare_3.1.bank), custom_call_target="tpu_custom_call" | custom-call | tf_op jit(solution)/shard_map/merge_last/pallas_call | solution.py:311
  (9 shorter events, 0.0 us)
Async XLA Ops:
  0.0 7.7 %copy-start.4 = (s32[4,2,32]{2,1,0:T(2,128)S(1)}, s32[4,2,32]{2,1,0:T(2,128)}, u32[]{:S(2)}) copy-start(s32[4,2,32]{2,1,0:T(2,128)} %param.9) | copy-start | bytes 3076
  0.0 7.8 %copy-start.1 = (f32[4,2,2,32,16]{3,4,2,1,0:T(8,128)S(1)}, f32[4,2,2,32,16]{3,4,2,1,0:T(8,128)}, u32[]{:S(2)}) copy-start(f32[4,2,2,32,16]{3,4,2,1,0:T(8,128)} %param.8) | copy-start | bytes 98308
  0.9 6.9 %copy-start.3 = (s32[4,2,32]{2,1,0:T(2,128)S(1)}, s32[4,2,32]{2,1,0:T(2,128)}, u32[]{:S(2)}) copy-start(s32[4,2,32]{2,1,0:T(2,128)} %param.10) | copy-start | bytes 3076
  0.9 8.9 %collective-permute-start.2 = (bf16[2,32,384]{2,1,0:T(8,128)(2,1)S(1)}, bf16[2,32,384]{2,1,0:T(8,128)(2,1)S(1)}, u32[]{:S(2)}, u32[]{:S(2)}) collective-permute-start(bf16[2,32,384]{2,1,0:T(8,128)(2,1)S(1)} %get-tuple-element.25), channel_id=1, source_target_pairs={{5,4},{13,12},{21,20},{29,28},{37,36},{45,44},{53,52},{61,60},{69,... | collective-permute-start | bytes 147464 | tf_op jit(solution)/shard_map/ppermute | solution.py:331
  1.6 6.2 %copy-start.5 = (s32[4,32]{1,0:T(4,128)S(1)}, s32[4,32]{1,0:T(4,128)}, u32[]{:S(2)}) copy-start(s32[4,32]{1,0:T(4,128)} %param.11) | copy-start | bytes 1540
  1.6 8.2 %collective-permute-start = (bf16[2,32,384]{2,1,0:T(8,128)(2,1)S(1)}, bf16[2,32,384]{2,1,0:T(8,128)(2,1)S(1)}, u32[]{:S(2)}, u32[]{:S(2)}) collective-permute-start(bf16[2,32,384]{2,1,0:T(8,128)(2,1)S(1)} %get-tuple-element.26), channel_id=1, source_target_pairs={{1,2},{3,4},{5,6},{2,1},{4,3},{6,5},{9,10},{11,12},{13,14},{10,9},... | collective-permute-start | bytes 147464 | tf_op jit(solution)/shard_map/ppermute | solution.py:332
  5.8 6.0 %collective-permute-start.1 = (bf16[2,32,384]{2,1,0:T(8,128)(2,1)S(1)}, bf16[2,32,384]{2,1,0:T(8,128)(2,1)S(1)}, u32[]{:S(2)}, u32[]{:S(2)}) collective-permute-start(bf16[2,32,384]{2,1,0:T(8,128)(2,1)S(1)} %get-tuple-element.27), channel_id=1, source_target_pairs={{1,0},{0,1},{3,2},{2,3},{4,5},{7,6},{6,7},{9,8},{8,9},{11,10},{10,... | collective-permute-start | bytes 147464 | tf_op jit(solution)/shard_map/ppermute | solution.py:333
  7.8 0.7 %copy-start.2 = (bf16[2,512]{1,0:T(2,128)(2,1)S(1)}, bf16[2,512]{1,0:T(2,128)(2,1)}, u32[]{:S(2)}) copy-start(bf16[2,512]{1,0:T(2,128)(2,1)} %chirp.1) | copy-start | bytes 6148
  8.5 3.3 %copy-start = (bf16[2,32,1024]{2,1,0:T(8,128)(2,1)S(1)}, bf16[2,32,1024]{2,1,0:T(8,128)(2,1)}, u32[]{:S(2)}) copy-start(bf16[2,32,1024]{2,1,0:T(8,128)(2,1)} %echoes.3) | copy-start | bytes 393220
  12.2 3.2 %collective-permute-start.3 = (bf16[32,1280]{1,0:T(8,128)(2,1)S(1)}, bf16[32,1280]{1,0:T(8,128)(2,1)S(1)}, u32[]{:S(2)}, u32[]{:S(2)}) collective-permute-start(bf16[32,1280]{1,0:T(8,128)(2,1)S(1)} %compress_sent.1), channel_id=1, source_target_pairs={{0,8},{8,0},{16,24},{24,16},{32,40},{40,32},{48,56},{56,48},{64,72... | collective-permute-start | bytes 245768 | tf_op jit(solution)/shard_map/ppermute | solution.py:341
  16.2 7.0 %collective-permute-start.4 = (bf16[32,1280]{1,0:T(8,128)(2,1)S(1)}, bf16[32,1280]{1,0:T(8,128)(2,1)S(1)}, u32[]{:S(2)}, u32[]{:S(2)}) collective-permute-start(bf16[32,1280]{1,0:T(8,128)(2,1)S(1)} %get-tuple-element.18), channel_id=1, source_target_pairs={{0,16},{8,24},{16,0},{24,8},{32,48},{40,56},{48,32},{56,40},{64,80... | collective-permute-start | bytes 245768 | tf_op jit(solution)/shard_map/ppermute | solution.py:341
  24.2 9.8 %collective-permute-start.5 = (bf16[32,1152]{1,0:T(8,128)(2,1)S(1)}, bf16[32,1152]{1,0:T(8,128)(2,1)S(1)}, u32[]{:S(2)}, u32[]{:S(2)}) collective-permute-start(bf16[32,1152]{1,0:T(8,128)(2,1)S(1)} %get-tuple-element.22), channel_id=1, source_target_pairs={{0,32},{8,40},{16,48},{24,56},{32,0},{40,8},{48,16},{56,24},{64,96... | collective-permute-start | bytes 221192 | tf_op jit(solution)/shard_map/ppermute | solution.py:341
  34.8 10.3 %collective-permute-start.6 = (bf16[32,1152]{1,0:T(8,128)(2,1)S(1)}, bf16[32,1152]{1,0:T(8,128)(2,1)S(1)}, u32[]{:S(2)}, u32[]{:S(2)}) collective-permute-start(bf16[32,1152]{1,0:T(8,128)(2,1)S(1)} %get-tuple-element.24), channel_id=1, source_target_pairs={{0,64},{8,72},{16,80},{24,88},{32,96},{40,104},{48,112},{56,120},{... | collective-permute-start | bytes 221192 | tf_op jit(solution)/shard_map/ppermute | solution.py:341

commit v4 on v3

--- a/solution.py
+++ b/solution.py
@@ -36,31 +36,45 @@
     imag = ((lane >> 4) & 1) == 1
     swapped = jnp.where(imag, pltpu.roll(weights, 16, 1), pltpu.roll(weights, LANES - 16, 1))
     sources = (jnp.where(imag, -weights, weights), swapped)
-    numbers = numbers.astype(jnp.int32)
-    column = [jnp.broadcast_to(numbers[:, i : i + 1], (HALF, LANES)) for i in range(5)]
-    for tile in range(COLS // LANES):
-        spot = lane + tile * LANES
-        upper = spot >= COLS // 2
-        spot = jnp.where(upper, spot - COLS // 2, spot)
-        base = jnp.where(upper, 32, 0) + ((spot >> 4) & 1) * KERN
-        first = (spot >> 5) * FINE - SHIFT - jnp.where(upper, column[1], column[0])
-        width = jnp.where(upper, column[3], column[2])
-        width = jnp.where((spot & 15) == column[4], width, 0)
-        at = slice(tile * LANES, (tile + 1) * LANES)
-        rest_at = slice(COLS + tile * LANES, COLS + (tile + 1) * LANES)
-        for b in range(FINE):
-            tap = first + b
-            live = (tap >= 0) & (tap < width)
-            index = base | (tap & (KERN - 1))
-            for part in range(2):
-                value = jnp.take_along_axis(
-                    sources[part], index, axis=1, mode="promise_in_bounds"
-                )
-                value = jnp.where(live, value, 0.0)
-                high = value.astype(BF16)
-                rows = slice(b * 32 + part * HALF, b * 32 + (part + 1) * HALF)
-                bank[rows, at] = high
-                bank[rows, rest_at] = (value - high.astype(F32)).astype(BF16)
+    column = [jnp.broadcast_to(number, (HALF, LANES)).astype(jnp.int32) for number in numbers]
+    for t in range(2):
+        width = jnp.where((lane & 15) == column[4], column[2 + t], 0)
+        base = t * 32 + ((lane >> 4) & 1) * KERN
+        for tile in range(2):
+            coarse = (lane >> 5) if tile == 0 else 4 + ((lane >> 5) & 1)
+            first = coarse * FINE - SHIFT - column[t]
+            for b in range(FINE):
+                tap = first + b
+                live = (tap >= 0) & (tap < width)
+                index = base | (tap & (KERN - 1))
+                for part in range(2):
+                    value = jnp.take_along_axis(
+                        sources[part], index, axis=1, mode="promise_in_bounds"
+                    )
+                    value = jnp.where(live, value, 0.0)
+                    high = value.astype(BF16).astype(F32)
+                    rows = slice(b * 32 + part * HALF, b * 32 + (part + 1) * HALF)
+                    at = t * COLS + tile * LANES
+                    if tile == 0:
+                        bank[rows, at : at + LANES] = high.astype(BF16)
+                        bank[rows, at + 2 * LANES : at + 3 * LANES] = (value - high).astype(BF16)
+                    else:
+                        both = jnp.where(lane < LANES // 2, high, value - high)
+                        bank[rows, at : at + LANES] = both.astype(BF16)
+
+
+def child_rows_of(stack):
+    return [stack[0:LANES], stack[LANES:], stack[LANES:], stack[0:LANES]]
+
+
+def child_product(bank, t, stack):
+    rows = jnp.concatenate(child_rows_of(stack), axis=0)
+    return jnp.dot(bank[:, t * COLS : (t + 1) * COLS], rows, preferred_element_type=F32)
+
+
+def both_products(bank, own, partner):
+    rows = jnp.concatenate(child_rows_of(own) + child_rows_of(partner), axis=0)
+    return jnp.dot(bank[...], rows, preferred_element_type=F32)
 
 
 def level_params(weights, numbers, level, rows):
@@ -77,7 +91,7 @@
         pair = picks[k], picks[k + 1]
         picks[k] = jnp.where(swap, pair[1], pair[0])
         picks[k + 1] = jnp.where(swap, pair[0], pair[1])
-    return jnp.where(swap, turned, tile), jnp.concatenate(picks, axis=1)
+    return jnp.where(swap, turned, tile), picks
 
 
 def build_level(bank, weights, numbers, level):
@@ -87,10 +101,12 @@
     for half in range(2):
         side = half ^ first
         start = side * HALF if isinstance(side, int) else pl.multiple_of(side * HALF, HALF)
-        build_bank(bank.at[half], *level_params(weights, numbers, level, pl.ds(start, HALF)))
-
-
-def prepare_kernel(chirp, taps_in, numbers_in, toeplitz, bank, weights, numbers, table):
+        build_bank(bank.at[half * OUTS : (half + 1) * OUTS], *level_params(weights, numbers, level, pl.ds(start, HALF)))
+
+
+def prepare_kernel(
+    chirp, taps_in, numbers_in, toeplitz, bank, bank_last, weights, numbers, table
+):
     taps = chirp[...].astype(F32)
     taps = jnp.concatenate([taps, jnp.zeros((2, SPAN - TAPS), F32)], axis=1)
     real = pltpu.roll(jnp.broadcast_to(taps[0:1], (LANES, SPAN)), 0, 1, stride=1, stride_axis=0)
@@ -109,10 +125,23 @@
         table[16 + level : 17 + level, 0:ROWS] = own[4:5]
     numbers[:, 0:ROWS] = table[...].T[0:ROWS]
     build_level(bank, weights, numbers, 0)
-
-
-def prepare_late_kernel(level, after, weights, numbers, bank):
+    build_level(bank_last, weights, numbers, LEVELS - 1)
+
+
+def banks_kernel(levels, after, weights, numbers, *banks):
+    for level, bank in zip(levels, banks):
+        build_level(bank, weights, numbers, level)
+
+
+def bank_and_part_kernel(level, trim, own, weights, numbers, bank, part):
     build_level(bank, weights, numbers, level)
+    part[...] = fine_sum(child_product(bank.at[OUTS : 2 * OUTS], 0, own), trim)
+
+
+def parts_kernel(trim, own, bank, parts):
+    product = child_product(bank, 0, own)
+    for half in range(2):
+        parts[half] = fine_sum(product[half * OUTS : (half + 1) * OUTS], trim)
 
 
 def inside_mask(rows, length, rim):
@@ -190,11 +219,6 @@
     return total
 
 
-def product_of(bank, own, partner, trim):
-    both = jnp.concatenate([own[...], partner[...]] * 2, axis=0)
-    return fine_sum(jnp.dot(bank, both, preferred_element_type=F32), trim)
-
-
 def rounded(total, rim):
     total = total[:, 0 : BINS + 2 * rim]
     return jnp.where(inside_mask(*total.shape, rim), total, 0.0).astype(BF16)
@@ -202,24 +226,34 @@
 
 def merge_sent_kernel(trim, rim, own, theirs, bank, sent, partner):
     fill_stack(partner, theirs[...])
-    sent[...] = rounded(product_of(bank[1], own, partner, trim), rim)
+    product = both_products(bank.at[OUTS : 2 * OUTS], own, partner)
+    sent[...] = rounded(fine_sum(product, trim), rim)
+
+
+def merge_sent_part_kernel(trim, rim, part, theirs, bank, sent, partner):
+    fill_stack(partner, theirs[...])
+    product = child_product(bank.at[OUTS : 2 * OUTS], 1, partner)
+    sent[...] = rounded(part[...] + fine_sum(product, trim), rim)
 
 
 def merge_kept_kernel(trim, rim, own, partner, bank, after):
-    fill_stack(after, rounded(product_of(bank[0], own, partner, trim), rim))
-
-
-def merge_last_kernel(own, theirs, bank, out, partner):
+    product = both_products(bank.at[0:OUTS], own, partner)
+    fill_stack(after, rounded(fine_sum(product, trim), rim))
+
+
+def merge_last_kernel(parts, theirs, bank, out, partner):
     fill_stack(partner, theirs[...])
+    product = child_product(bank, 1, partner)
     for half in range(2):
-        total = product_of(bank[half], own, partner, RIM_LATE)[:, 0:BINS].astype(BF16)
+        total = parts[half] + fine_sum(product[half * OUTS : (half + 1) * OUTS], RIM_LATE)
+        total = total[:, 0:BINS].astype(BF16)
         for part in range(2):
             out[part, half * HALF : (half + 1) * HALF] = total[part * HALF : (part + 1) * HALF]
 
 
 WHOLE = pl.BlockSpec(memory_space=pltpu.VMEM)
 PARAMS = pltpu.CompilerParams(vmem_limit_bytes=VMEM)
-BANK = jax.ShapeDtypeStruct((2, OUTS, 2 * COLS), BF16)
+BANK = jax.ShapeDtypeStruct((2 * OUTS, 2 * COLS), BF16)
 FRAMES = (FRAME, FRAME, FRAME_LATE, FRAME_LATE)
 RIMS = (RIM, RIM, RIM_LATE, RIM_LATE)
 
@@ -241,12 +275,13 @@
         prepare_kernel,
         out_shape=(
             jax.ShapeDtypeStruct((2 * LANES, 2 * SPAN), BF16),
+            BANK,
             BANK,
             jax.ShapeDtypeStruct((ROWS, 4 * PART), F32),
             jax.ShapeDtypeStruct((ROWS, LANES), F32),
         ),
         in_specs=[WHOLE] * 3,
-        out_specs=(WHOLE,) * 4,
+        out_specs=(WHOLE,) * 5,
         scratch_shapes=[pltpu.VMEM((ROWS, LANES), F32)],
         compiler_params=PARAMS,
         cost_estimate=pl.CostEstimate(flops=1_000_000_000, bytes_accessed=2_000_000, transcendentals=0),
@@ -254,16 +289,44 @@
     )(chirp, taps, numbers)
 
 
-def prepare_late(level, after, weights, numbers):
-    return pl.pallas_call(
-        functools.partial(prepare_late_kernel, level),
-        out_shape=BANK,
+def make_banks(levels, after, weights, numbers):
+    return pl.pallas_call(
+        functools.partial(banks_kernel, levels),
+        out_shape=(BANK,) * len(levels),
         in_specs=[pl.BlockSpec(memory_space=pl.ANY), WHOLE, WHOLE],
+        out_specs=(WHOLE,) * len(levels),
+        compiler_params=PARAMS,
+        cost_estimate=small_cost(),
+        name="bank_" + "_".join(map(str, levels)),
+    )(after, weights, numbers)
+
+
+def bank_and_part(level, own, weights, numbers):
+    return pl.pallas_call(
+        functools.partial(bank_and_part_kernel, level, trim_of(level)),
+        out_shape=(BANK, jax.ShapeDtypeStruct((2 * HALF, FRAMES[level]), F32)),
+        in_specs=[WHOLE] * 3,
+        out_specs=(WHOLE, WHOLE),
+        compiler_params=PARAMS,
+        cost_estimate=small_cost(),
+        name=f"bank_and_part_{level}",
+    )(own, weights, numbers)
+
+
+def own_parts(level, own, bank):
+    return pl.pallas_call(
+        functools.partial(parts_kernel, trim_of(level)),
+        out_shape=jax.ShapeDtypeStruct((2, 2 * HALF, FRAMES[level]), F32),
+        in_specs=[WHOLE] * 2,
         out_specs=WHOLE,
         compiler_params=PARAMS,
         cost_estimate=small_cost(),
-        name=f"prepare_{level}",
-    )(after, weights, numbers)
+        name=f"own_parts_{level}",
+    )(own, bank)
+
+
+def trim_of(level):
+    return RIMS[level] - RIMS[level + 1] if level + 1 < LEVELS else RIMS[level]
 
 
 def compress(sent, echoes, odd, late, early, toeplitz):
@@ -282,10 +345,10 @@
     )(echoes, odd, late, early, toeplitz)
 
 
-def merge_sent(level, own, theirs, bank):
-    rim = RIMS[level + 1]
-    return pl.pallas_call(
-        functools.partial(merge_sent_kernel, RIMS[level] - rim, rim),
+def merge_sent(level, own, theirs, bank, has_part=False):
+    kernel = merge_sent_part_kernel if has_part else merge_sent_kernel
+    return pl.pallas_call(
+        functools.partial(kernel, trim_of(level), RIMS[level + 1]),
         out_shape=(message(FRAMES[level + 1]), shifted(FRAMES[level])),
         in_specs=[WHOLE] * 3,
         out_specs=(WHOLE, WHOLE),
@@ -295,9 +358,8 @@
 
 
 def merge_kept(level, own, partner, bank):
-    rim = RIMS[level + 1]
-    return pl.pallas_call(
-        functools.partial(merge_kept_kernel, RIMS[level] - rim, rim),
+    return pl.pallas_call(
+        functools.partial(merge_kept_kernel, trim_of(level), RIMS[level + 1]),
         out_shape=shifted(FRAMES[level + 1]),
         in_specs=[WHOLE] * 3,
         out_specs=WHOLE,
@@ -307,7 +369,7 @@
     )(own, partner, bank)
 
 
-def merge_last(own, theirs, bank):
+def merge_last(parts, theirs, bank):
     return pl.pallas_call(
         merge_last_kernel,
         out_shape=jax.ShapeDtypeStruct((2, ROWS, BINS), BF16),
@@ -316,7 +378,7 @@
         scratch_shapes=[pltpu.VMEM((COLS // 2, FRAMES[LEVELS - 1]), BF16)],
         compiler_params=PARAMS,
         name="merge_last",
-    )(own, theirs, bank)
+    )(parts, theirs, bank)
 
 
 def body(echoes, transmit_chirp, band_weights, band_offsets, band_widths, child_rows):
@@ -333,20 +395,28 @@
     late = lax.ppermute(within_late, "range", [(i ^ 1, i) for i in range(count) if not takes_early(i)])
     taps = jnp.swapaxes(band_weights, 3, 4).reshape(LEVELS, PART, ROWS)
     numbers = jnp.concatenate([band_offsets, band_widths, child_rows[:, None]], axis=1)
-    toeplitz, bank, weights, numbers = prepare(transmit_chirp, taps, numbers)
+    toeplitz, bank, bank_last, weights, numbers = prepare(transmit_chirp, taps, numbers)
     sent = compress(True, echoes, odd, late, early, toeplitz)
     blocks = lax.axis_size("aperture")
-    own = None
-    for level in range(LEVELS):
-        theirs = lax.ppermute(sent, "aperture", [(i, i ^ (1 << level)) for i in range(blocks)])
-        if level == 0:
-            own = compress(False, echoes, odd, late, early, toeplitz)
-        else:
-            own = merge_kept(level - 1, own, partner, bank)
-            bank = prepare_late(level, own, weights, numbers)
-        if level + 1 < LEVELS:
-            sent, partner = merge_sent(level, own, theirs, bank)
-    return merge_last(own, theirs, bank)
+
+    def trade(message, level):
+        return lax.ppermute(message, "aperture", [(i, i ^ (1 << level)) for i in range(blocks)])
+
+    theirs = trade(sent, 0)
+    own = compress(False, echoes, odd, late, early, toeplitz)
+    sent, partner = merge_sent(0, own, theirs, bank)
+    theirs = trade(sent, 1)
+    own = merge_kept(0, own, partner, bank)
+    (bank,) = make_banks((1,), own, weights, numbers)
+    sent, partner = merge_sent(1, own, theirs, bank)
+    theirs = trade(sent, 2)
+    own = merge_kept(1, own, partner, bank)
+    bank, part = bank_and_part(2, own, weights, numbers)
+    sent, partner = merge_sent(2, part, theirs, bank, True)
+    theirs = trade(sent, 3)
+    own = merge_kept(2, own, partner, bank)
+    parts = own_parts(3, own, bank_last)
+    return merge_last(parts, theirs, bank_last)
 
 
 def solution(mesh):

time: 47.4 us -> 46.8 us (0.987)
  the two profiles are of different devices: /device:TPU:28 before, /device:TPU:20 now
where the time goes in v4:
time: 46.8 us; the launch traced here: 46.5 us
  starting transfers between devices  27.8 us (59%)
  Pallas kernels  13.5 us (29%)
  waiting for transfers between devices  3.49 us (7%)
  other arithmetic  0.89 us (2%)
  local copies, waits for them, and re-layouts  0.67 us (1%)
    ppermute x4, starting transfers between devices, trade(): lax.ppermute(message, 'aperture', [(i, i ^ 1 << level) for i in range(blo...  20 us
    ppermute x1, starting transfers between devices, body(): lax.ppermute(within_late, 'range', [(i ^ 1, i) for i in range(count) if n...  4.69 us
    ppermute x4, waiting for transfers between devices, trade(): lax.ppermute(message, 'aperture', [(i, i ^ 1 << level) for i in range(blo...  3.49 us
    pallas_call x3, Pallas kernels, merge_kept(): pl.pallas_call(functools.partial(merge_kept_kernel, trim_of(level), RIMS[...  2.79 us
    ppermute x1, starting transfers between devices, body(): odd = lax.ppermute(between, 'range', pairs + [(j, i) for i, j in pairs])  2.44 us
    pallas_call x1, Pallas kernels, prepare(): pl.pallas_call(prepare_kernel, out_shape=(jax.ShapeDtypeStruct((2 * LANES...  2.4 us
    pallas_call x3, Pallas kernels, merge_sent(): pl.pallas_call(functools.partial(kernel, trim_of(level), RIMS[level + 1])...  2.26 us
    pallas_call x1, Pallas kernels, merge_last(): pl.pallas_call(merge_last_kernel, out_shape=jax.ShapeDtypeStruct((2, ROWS...  1.7 us
  transfers between devices with their start and end apart: 7, of which 4 were waited for; matrix products, arithmetic and copies ran while one was open for 0% of the time, Pallas kernels for 20%

profile of v4, /device:TPU:20, one launch (start us, length us, event | category | flops | bytes accessed | tf_op | source)
XLA Modules:
  0.0 46.5 jit_solution(1165346860390462442)
XLA Ops:
  0.0 0.9 %broadcast_select_fusion = (bf16[2,32,384]{2,1,0:T(8,128)(2,1)S(1)}, bf16[2,32,384]{2,1,0:T(8,128)(2,1)S(1)}, bf16[2,32,384]{2,1,0:T(8,128)(2,1)S(1)}) fusion(pred[]{:T(512)S(6)} %eq.11, bf16[2,32,1024]{2,1,0:T(8,128)(2,1)} %echoes.3, pred[]{:T(512)S(6)} %eq.10, pred[]{:T(512)S(6)} %ne.14), kind=kLoop, calls=%fused_computation | loop fusion | flops 73728 | bytes 245763 | tf_op jit(solution)/shard_map/jit(_where)/select_n | solution.py:390
  0.9 0.0 copy-start.3
  0.9 0.7 %collective-permute-start.2 = (bf16[2,32,384]{2,1,0:T(8,128)(2,1)S(1)}, bf16[2,32,384]{2,1,0:T(8,128)(2,1)S(1)}, u32[]{:S(2)}, u32[]{:S(2)}) collective-permute-start(bf16[2,32,384]{2,1,0:T(8,128)(2,1)S(1)} %get-tuple-element.31), channel_id=1, source_target_pairs={{5,4},{13,12},{21,20},{29,28},{37,36},{45,44},{53,52},{61,60},{69,... | collective-permute-start | bytes 147464 | tf_op jit(solution)/shard_map/ppermute | solution.py:393
  1.6 0.0 copy-start.5
  1.6 2.4 %collective-permute-start = (bf16[2,32,384]{2,1,0:T(8,128)(2,1)S(1)}, bf16[2,32,384]{2,1,0:T(8,128)(2,1)S(1)}, u32[]{:S(2)}, u32[]{:S(2)}) collective-permute-start(bf16[2,32,384]{2,1,0:T(8,128)(2,1)S(1)} %get-tuple-element.32), channel_id=1, source_target_pairs={{1,2},{3,4},{5,6},{2,1},{4,3},{6,5},{9,10},{11,12},{13,14},{10,9},... | collective-permute-start | bytes 147464 | tf_op jit(solution)/shard_map/ppermute | solution.py:394
  4.0 4.7 %collective-permute-start.1 = (bf16[2,32,384]{2,1,0:T(8,128)(2,1)S(1)}, bf16[2,32,384]{2,1,0:T(8,128)(2,1)S(1)}, u32[]{:S(2)}, u32[]{:S(2)}) collective-permute-start(bf16[2,32,384]{2,1,0:T(8,128)(2,1)S(1)} %get-tuple-element.33), channel_id=1, source_target_pairs={{1,0},{0,1},{3,2},{2,3},{4,5},{7,6},{6,7},{9,8},{8,9},{11,10},{10,... | collective-permute-start | bytes 147464 | tf_op jit(solution)/shard_map/ppermute | solution.py:395
  8.8 0.0 copy-start.2
  8.8 0.6 %copy-done.2 = bf16[2,512]{1,0:T(2,128)(2,1)S(1)} copy-done((bf16[2,512]{1,0:T(2,128)(2,1)S(1)}, bf16[2,512]{1,0:T(2,128)(2,1)}, u32[]{:S(2)}) %copy-start.2) | copy-done | bytes 2072
  9.4 2.4 %prepare.1 = (bf16[256,1280]{1,0:T(8,128)(2,1)S(1)}, bf16[512,768]{1,0:T(8,128)(2,1)S(1)}, bf16[512,768]{1,0:T(8,128)(2,1)S(1)}, f32[32,256]{1,0:T(8,128)S(1)}, f32[32,128]{1,0:T(8,128)S(1)}) custom-call(bf16[2,512]{1,0:T(2,128)(2,1)S(1)} %copy-done.2, f32[4,64,32]{2,1,0:T(8,128)S(1)} %bitcast.6, s32[4,5,32]{2,1,0:T(8,128)S(1)} %pad_add_fusion.numbers_in), custom_call_target="tpu_custom_call" | custom-call | flops 1000000000 | bytes 2000000 | tf_op jit(solution)/shard_map/prepare/pallas_call | solution.py:274
  11.8 0.0 collective-permute-done.2.early
  11.9 0.0 collective-permute-done.odd
  11.9 0.0 collective-permute-done.1.late
  11.9 0.4 compress_sent.1
  12.3 1.9 %collective-permute-start.3 = (bf16[32,1280]{1,0:T(8,128)(2,1)S(1)}, bf16[32,1280]{1,0:T(8,128)(2,1)S(1)}, u32[]{:S(2)}, u32[]{:S(2)}) collective-permute-start(bf16[32,1280]{1,0:T(8,128)(2,1)S(1)} %compress_sent.1), channel_id=1, source_target_pairs={{0,8},{8,0},{16,24},{24,16},{32,40},{40,32},{48,56},{56,48},{64,72... | collective-permute-start | bytes 245768 | tf_op jit(solution)/shard_map/ppermute | solution.py:403
  14.2 0.6 %compress_kept.1.own = bf16[192,1280]{1,0:T(8,128)(2,1)S(1)} custom-call(bf16[2,32,1024]{2,1,0:T(8,128)(2,1)S(1)} %copy-done, bf16[2,32,384]{2,1,0:T(8,128)(2,1)S(1)} %collective-permute-done.odd, bf16[2,32,384]{2,1,0:T(8,128)(2,1)S(1)} %collective-permute-done.1.late, bf16[2,32,384]{2,1,0:T(8,128)(2,1)S(1)} %collective-permute-done.2.early, ...), custom_call_target="tpu_custom_call" | custom-call | flops 200000000 | bytes 1000000 | tf_op jit(solution)/shard_map/compress_kept/pallas_call | solution.py:336
  14.8 0.7 %collective-permute-done.3.theirs = bf16[32,1280]{1,0:T(8,128)(2,1)S(1)} collective-permute-done((bf16[32,1280]{1,0:T(8,128)(2,1)S(1)}, bf16[32,1280]{1,0:T(8,128)(2,1)S(1)}, u32[]{:S(2)}, u32[]{:S(2)}) %collective-permute-start.3) | collective-permute-done | bytes 81952 | tf_op jit(solution)/shard_map/ppermute | solution.py:403
  15.4 0.8 %merge_0_sent.1 = (bf16[32,1280]{1,0:T(8,128)(2,1)S(1)}, bf16[192,1280]{1,0:T(8,128)(2,1)S(1)}) custom-call(bf16[192,1280]{1,0:T(8,128)(2,1)S(1)} %compress_kept.1.own, bf16[32,1280]{1,0:T(8,128)(2,1)S(1)} %collective-permute-done.3.theirs, bf16[512,768]{1,0:T(8,128)(2,1)S(1)} %get-tuple-element.19.bank), custom_call_target="tpu_custom_call" | custom-call | tf_op jit(solution)/shard_map/merge_0_sent/pallas_call | solution.py:350
  16.3 4.3 %collective-permute-start.4 = (bf16[32,1280]{1,0:T(8,128)(2,1)S(1)}, bf16[32,1280]{1,0:T(8,128)(2,1)S(1)}, u32[]{:S(2)}, u32[]{:S(2)}) collective-permute-start(bf16[32,1280]{1,0:T(8,128)(2,1)S(1)} %get-tuple-element.21), channel_id=1, source_target_pairs={{0,16},{8,24},{16,0},{24,8},{32,48},{40,56},{48,32},{56,40},{64,80... | collective-permute-start | bytes 245768 | tf_op jit(solution)/shard_map/ppermute | solution.py:403
  20.5 1.0 %merge_0_kept.1.after.own = bf16[192,1280]{1,0:T(8,128)(2,1)S(1)} custom-call(bf16[192,1280]{1,0:T(8,128)(2,1)S(1)} %compress_kept.1.own, bf16[192,1280]{1,0:T(8,128)(2,1)S(1)} %get-tuple-element.20.partner, bf16[512,768]{1,0:T(8,128)(2,1)S(1)} %get-tuple-element.19.bank), custom_call_target="tpu_custom_call" | custom-call | flops 1000 | bytes 1000 | tf_op jit(solution)/shard_map/merge_0_kept/pallas_call | solution.py:361
  21.5 1.0 %bank_1.1.bank = bf16[512,768]{1,0:T(8,128)(2,1)S(1)} custom-call(bf16[192,1280]{1,0:T(8,128)(2,1)S(1)} %merge_0_kept.1.after.own, f32[32,256]{1,0:T(8,128)S(1)} %get-tuple-element.22.weights, f32[32,128]{1,0:T(8,128)S(1)} %get-tuple-element.23.numbers), custom_call_target="tpu_custom_call" | custom-call | flops 1000 | bytes 1000 | tf_op jit(solution)/shard_map/bank_1/pallas_call | solution.py:293
  22.5 0.7 %collective-permute-done.4.theirs = bf16[32,1280]{1,0:T(8,128)(2,1)S(1)} collective-permute-done((bf16[32,1280]{1,0:T(8,128)(2,1)S(1)}, bf16[32,1280]{1,0:T(8,128)(2,1)S(1)}, u32[]{:S(2)}, u32[]{:S(2)}) %collective-permute-start.4) | collective-permute-done | bytes 81952 | tf_op jit(solution)/shard_map/ppermute | solution.py:403
  23.3 0.8 %merge_1_sent.1 = (bf16[32,1152]{1,0:T(8,128)(2,1)S(1)}, bf16[192,1280]{1,0:T(8,128)(2,1)S(1)}) custom-call(bf16[192,1280]{1,0:T(8,128)(2,1)S(1)} %merge_0_kept.1.after.own, bf16[32,1280]{1,0:T(8,128)(2,1)S(1)} %collective-permute-done.4.theirs, bf16[512,768]{1,0:T(8,128)(2,1)S(1)} %bank_1.1.bank), custom_call_target="tpu_custom_call" | custom-call | tf_op jit(solution)/shard_map/merge_1_sent/pallas_call | solution.py:350
  24.1 6.1 %collective-permute-start.5 = (bf16[32,1152]{1,0:T(8,128)(2,1)S(1)}, bf16[32,1152]{1,0:T(8,128)(2,1)S(1)}, u32[]{:S(2)}, u32[]{:S(2)}) collective-permute-start(bf16[32,1152]{1,0:T(8,128)(2,1)S(1)} %get-tuple-element.26), channel_id=1, source_target_pairs={{0,32},{8,40},{16,48},{24,56},{32,0},{40,8},{48,16},{56,24},{64,96... | collective-permute-start | bytes 221192 | tf_op jit(solution)/shard_map/ppermute | solution.py:403
  30.2 1.0 %merge_1_kept.1.own = bf16[192,1152]{1,0:T(8,128)(2,1)S(1)} custom-call(bf16[192,1280]{1,0:T(8,128)(2,1)S(1)} %merge_0_kept.1.after.own, bf16[192,1280]{1,0:T(8,128)(2,1)S(1)} %get-tuple-element.24.partner, bf16[512,768]{1,0:T(8,128)(2,1)S(1)} %bank_1.1.bank), custom_call_target="tpu_custom_call" | custom-call | flops 1000 | bytes 1000 | tf_op jit(solution)/shard_map/merge_1_kept/pallas_call | solution.py:361
  31.2 1.4 %bank_and_part_2.1 = (bf16[512,768]{1,0:T(8,128)(2,1)S(1)}, f32[32,1152]{1,0:T(8,128)S(1)}) custom-call(bf16[192,1152]{1,0:T(8,128)(2,1)S(1)} %merge_1_kept.1.own, f32[32,256]{1,0:T(8,128)S(1)} %get-tuple-element.22.weights, f32[32,128]{1,0:T(8,128)S(1)} %get-tuple-element.23.numbers), custom_call_target="tpu_custom_call" | custom-call | flops 1000 | bytes 1000 | tf_op jit(solution)/shard_map/bank_and_part_2/pallas_call | solution.py:305
  32.6 1.3 %collective-permute-done.5.theirs = bf16[32,1152]{1,0:T(8,128)(2,1)S(1)} collective-permute-done((bf16[32,1152]{1,0:T(8,128)(2,1)S(1)}, bf16[32,1152]{1,0:T(8,128)(2,1)S(1)}, u32[]{:S(2)}, u32[]{:S(2)}) %collective-permute-start.5) | collective-permute-done | bytes 73760 | tf_op jit(solution)/shard_map/ppermute | solution.py:403
  33.9 0.6 %merge_2_sent.1 = (bf16[32,1152]{1,0:T(8,128)(2,1)S(1)}, bf16[192,1152]{1,0:T(8,128)(2,1)S(1)}) custom-call(f32[32,1152]{1,0:T(8,128)S(1)} %get-tuple-element.25.part, bf16[32,1152]{1,0:T(8,128)(2,1)S(1)} %collective-permute-done.5.theirs, bf16[512,768]{1,0:T(8,128)(2,1)S(1)} %get-tuple-element.27.bank), custom_call_target="tpu_custom_call" | custom-call | tf_op jit(solution)/shard_map/merge_2_sent/pallas_call | solution.py:350
  34.6 7.7 %collective-permute-start.6 = (bf16[32,1152]{1,0:T(8,128)(2,1)S(1)}, bf16[32,1152]{1,0:T(8,128)(2,1)S(1)}, u32[]{:S(2)}, u32[]{:S(2)}) collective-permute-start(bf16[32,1152]{1,0:T(8,128)(2,1)S(1)} %get-tuple-element.30), channel_id=1, source_target_pairs={{0,64},{8,72},{16,80},{24,88},{32,96},{40,104},{48,112},{56,120},{... | collective-permute-start | bytes 221192 | tf_op jit(solution)/shard_map/ppermute | solution.py:403
  42.2 0.9 %merge_2_kept.1.own = bf16[192,1152]{1,0:T(8,128)(2,1)S(1)} custom-call(bf16[192,1152]{1,0:T(8,128)(2,1)S(1)} %merge_1_kept.1.own, bf16[192,1152]{1,0:T(8,128)(2,1)S(1)} %get-tuple-element.28.partner, bf16[512,768]{1,0:T(8,128)(2,1)S(1)} %get-tuple-element.27.bank), custom_call_target="tpu_custom_call" | custom-call | flops 1000 | bytes 1000 | tf_op jit(solution)/shard_map/merge_2_kept/pallas_call | solution.py:361
  43.1 0.9 %own_parts_3.1.parts = f32[2,32,1152]{2,1,0:T(8,128)S(1)} custom-call(bf16[192,1152]{1,0:T(8,128)(2,1)S(1)} %merge_2_kept.1.own, bf16[512,768]{1,0:T(8,128)(2,1)S(1)} %get-tuple-element.29.bank), custom_call_target="tpu_custom_call" | custom-call | flops 1000 | bytes 1000 | tf_op jit(solution)/shard_map/own_parts_3/pallas_call | solution.py:317
  44.1 0.8 %collective-permute-done.6.theirs = bf16[32,1152]{1,0:T(8,128)(2,1)S(1)} collective-permute-done((bf16[32,1152]{1,0:T(8,128)(2,1)S(1)}, bf16[32,1152]{1,0:T(8,128)(2,1)S(1)}, u32[]{:S(2)}, u32[]{:S(2)}) %collective-permute-start.6) | collective-permute-done | bytes 73760 | tf_op jit(solution)/shard_map/ppermute | solution.py:403
  44.8 1.7 %merge_last.1 = bf16[2,32,1024]{2,1,0:T(8,128)(2,1)} custom-call(f32[2,32,1152]{2,1,0:T(8,128)S(1)} %own_parts_3.1.parts, bf16[32,1152]{1,0:T(8,128)(2,1)S(1)} %collective-permute-done.6.theirs, bf16[512,768]{1,0:T(8,128)(2,1)S(1)} %get-tuple-element.29.bank), custom_call_target="tpu_custom_call" | custom-call | tf_op jit(solution)/shard_map/merge_last/pallas_call | solution.py:373
  (9 shorter events, 0.0 us)
Async XLA Ops:
  0.0 8.7 %copy-start.4 = (s32[4,2,32]{2,1,0:T(2,128)S(1)}, s32[4,2,32]{2,1,0:T(2,128)}, u32[]{:S(2)}) copy-start(s32[4,2,32]{2,1,0:T(2,128)} %param.9) | copy-start | bytes 3076
  0.0 8.8 %copy-start.1 = (f32[4,2,2,32,16]{3,4,2,1,0:T(8,128)S(1)}, f32[4,2,2,32,16]{3,4,2,1,0:T(8,128)}, u32[]{:S(2)}) copy-start(f32[4,2,2,32,16]{3,4,2,1,0:T(8,128)} %param.8) | copy-start | bytes 98308
  0.9 7.9 %copy-start.3 = (s32[4,2,32]{2,1,0:T(2,128)S(1)}, s32[4,2,32]{2,1,0:T(2,128)}, u32[]{:S(2)}) copy-start(s32[4,2,32]{2,1,0:T(2,128)} %param.10) | copy-start | bytes 3076
  0.9 11.0 %collective-permute-start.2 = (bf16[2,32,384]{2,1,0:T(8,128)(2,1)S(1)}, bf16[2,32,384]{2,1,0:T(8,128)(2,1)S(1)}, u32[]{:S(2)}, u32[]{:S(2)}) collective-permute-start(bf16[2,32,384]{2,1,0:T(8,128)(2,1)S(1)} %get-tuple-element.31), channel_id=1, source_target_pairs={{5,4},{13,12},{21,20},{29,28},{37,36},{45,44},{53,52},{61,60},{69,... | collective-permute-start | bytes 147464 | tf_op jit(solution)/shard_map/ppermute | solution.py:393
  1.6 7.2 %copy-start.5 = (s32[4,32]{1,0:T(4,128)S(1)}, s32[4,32]{1,0:T(4,128)}, u32[]{:S(2)}) copy-start(s32[4,32]{1,0:T(4,128)} %param.11) | copy-start | bytes 1540
  1.6 10.3 %collective-permute-start = (bf16[2,32,384]{2,1,0:T(8,128)(2,1)S(1)}, bf16[2,32,384]{2,1,0:T(8,128)(2,1)S(1)}, u32[]{:S(2)}, u32[]{:S(2)}) collective-permute-start(bf16[2,32,384]{2,1,0:T(8,128)(2,1)S(1)} %get-tuple-element.32), channel_id=1, source_target_pairs={{1,2},{3,4},{5,6},{2,1},{4,3},{6,5},{9,10},{11,12},{13,14},{10,9},... | collective-permute-start | bytes 147464 | tf_op jit(solution)/shard_map/ppermute | solution.py:394
  4.0 7.8 %collective-permute-start.1 = (bf16[2,32,384]{2,1,0:T(8,128)(2,1)S(1)}, bf16[2,32,384]{2,1,0:T(8,128)(2,1)S(1)}, u32[]{:S(2)}, u32[]{:S(2)}) collective-permute-start(bf16[2,32,384]{2,1,0:T(8,128)(2,1)S(1)} %get-tuple-element.33), channel_id=1, source_target_pairs={{1,0},{0,1},{3,2},{2,3},{4,5},{7,6},{6,7},{9,8},{8,9},{11,10},{10,... | collective-permute-start | bytes 147464 | tf_op jit(solution)/shard_map/ppermute | solution.py:395
  8.8 0.7 %copy-start.2 = (bf16[2,512]{1,0:T(2,128)(2,1)S(1)}, bf16[2,512]{1,0:T(2,128)(2,1)}, u32[]{:S(2)}) copy-start(bf16[2,512]{1,0:T(2,128)(2,1)} %chirp.1) | copy-start | bytes 6148
  9.4 2.4 %copy-start = (bf16[2,32,1024]{2,1,0:T(8,128)(2,1)S(1)}, bf16[2,32,1024]{2,1,0:T(8,128)(2,1)}, u32[]{:S(2)}) copy-start(bf16[2,32,1024]{2,1,0:T(8,128)(2,1)} %echoes.3) | copy-start | bytes 393220
  12.3 3.2 %collective-permute-start.3 = (bf16[32,1280]{1,0:T(8,128)(2,1)S(1)}, bf16[32,1280]{1,0:T(8,128)(2,1)S(1)}, u32[]{:S(2)}, u32[]{:S(2)}) collective-permute-start(bf16[32,1280]{1,0:T(8,128)(2,1)S(1)} %compress_sent.1), channel_id=1, source_target_pairs={{0,8},{8,0},{16,24},{24,16},{32,40},{40,32},{48,56},{56,48},{64,72... | collective-permute-start | bytes 245768 | tf_op jit(solution)/shard_map/ppermute | solution.py:403
  16.3 7.0 %collective-permute-start.4 = (bf16[32,1280]{1,0:T(8,128)(2,1)S(1)}, bf16[32,1280]{1,0:T(8,128)(2,1)S(1)}, u32[]{:S(2)}, u32[]{:S(2)}) collective-permute-start(bf16[32,1280]{1,0:T(8,128)(2,1)S(1)} %get-tuple-element.21), channel_id=1, source_target_pairs={{0,16},{8,24},{16,0},{24,8},{32,48},{40,56},{48,32},{56,40},{64,80... | collective-permute-start | bytes 245768 | tf_op jit(solution)/shard_map/ppermute | solution.py:403
  24.1 9.8 %collective-permute-start.5 = (bf16[32,1152]{1,0:T(8,128)(2,1)S(1)}, bf16[32,1152]{1,0:T(8,128)(2,1)S(1)}, u32[]{:S(2)}, u32[]{:S(2)}) collective-permute-start(bf16[32,1152]{1,0:T(8,128)(2,1)S(1)} %get-tuple-element.26), channel_id=1, source_target_pairs={{0,32},{8,40},{16,48},{24,56},{32,0},{40,8},{48,16},{56,24},{64,96... | collective-permute-start | bytes 221192 | tf_op jit(solution)/shard_map/ppermute | solution.py:403
  34.6 10.3 %collective-permute-start.6 = (bf16[32,1152]{1,0:T(8,128)(2,1)S(1)}, bf16[32,1152]{1,0:T(8,128)(2,1)S(1)}, u32[]{:S(2)}, u32[]{:S(2)}) collective-permute-start(bf16[32,1152]{1,0:T(8,128)(2,1)S(1)} %get-tuple-element.30), channel_id=1, source_target_pairs={{0,64},{8,72},{16,80},{24,88},{32,96},{40,104},{48,112},{56,120},{... | collective-permute-start | bytes 221192 | tf_op jit(solution)/shard_map/ppermute | solution.py:403

commit v5 on v4

--- a/solution.py
+++ b/solution.py
@@ -125,12 +125,12 @@
         table[16 + level : 17 + level, 0:ROWS] = own[4:5]
     numbers[:, 0:ROWS] = table[...].T[0:ROWS]
     build_level(bank, weights, numbers, 0)
-    build_level(bank_last, weights, numbers, LEVELS - 1)
-
-
-def banks_kernel(levels, after, weights, numbers, *banks):
-    for level, bank in zip(levels, banks):
-        build_level(bank, weights, numbers, level)
+    build_bank(bank_last, *level_params(weights, numbers, LEVELS - 1, slice(0, HALF)))
+
+
+def banks_kernel(after, weights, numbers, bank, bank_last):
+    build_level(bank, weights, numbers, 1)
+    build_bank(bank_last, *level_params(weights, numbers, LEVELS - 1, slice(HALF, ROWS)))
 
 
 def bank_and_part_kernel(level, trim, own, weights, numbers, bank, part):
@@ -138,8 +138,15 @@
     part[...] = fine_sum(child_product(bank.at[OUTS : 2 * OUTS], 0, own), trim)
 
 
-def parts_kernel(trim, own, bank, parts):
-    product = child_product(bank, 0, own)
+def last_product(low, high, t, stack):
+    at = slice(t * COLS, (t + 1) * COLS)
+    bank = jnp.concatenate([low[:, at], high[:, at]], axis=0)
+    rows = jnp.concatenate(child_rows_of(stack), axis=0)
+    return jnp.dot(bank, rows, preferred_element_type=F32)
+
+
+def parts_kernel(trim, own, low, high, parts):
+    product = last_product(low, high, 0, own)
     for half in range(2):
         parts[half] = fine_sum(product[half * OUTS : (half + 1) * OUTS], trim)
 
@@ -241,9 +248,9 @@
     fill_stack(after, rounded(fine_sum(product, trim), rim))
 
 
-def merge_last_kernel(parts, theirs, bank, out, partner):
+def merge_last_kernel(parts, theirs, low, high, out, partner):
     fill_stack(partner, theirs[...])
-    product = child_product(bank, 1, partner)
+    product = last_product(low, high, 1, partner)
     for half in range(2):
         total = parts[half] + fine_sum(product[half * OUTS : (half + 1) * OUTS], RIM_LATE)
         total = total[:, 0:BINS].astype(BF16)
@@ -254,6 +261,7 @@
 WHOLE = pl.BlockSpec(memory_space=pltpu.VMEM)
 PARAMS = pltpu.CompilerParams(vmem_limit_bytes=VMEM)
 BANK = jax.ShapeDtypeStruct((2 * OUTS, 2 * COLS), BF16)
+HALF_BANK = jax.ShapeDtypeStruct((OUTS, 2 * COLS), BF16)
 FRAMES = (FRAME, FRAME, FRAME_LATE, FRAME_LATE)
 RIMS = (RIM, RIM, RIM_LATE, RIM_LATE)
 
@@ -276,7 +284,7 @@
         out_shape=(
             jax.ShapeDtypeStruct((2 * LANES, 2 * SPAN), BF16),
             BANK,
-            BANK,
+            HALF_BANK,
             jax.ShapeDtypeStruct((ROWS, 4 * PART), F32),
             jax.ShapeDtypeStruct((ROWS, LANES), F32),
         ),
@@ -289,15 +297,15 @@
     )(chirp, taps, numbers)
 
 
-def make_banks(levels, after, weights, numbers):
-    return pl.pallas_call(
-        functools.partial(banks_kernel, levels),
-        out_shape=(BANK,) * len(levels),
+def make_banks(after, weights, numbers):
+    return pl.pallas_call(
+        banks_kernel,
+        out_shape=(BANK, HALF_BANK),
         in_specs=[pl.BlockSpec(memory_space=pl.ANY), WHOLE, WHOLE],
-        out_specs=(WHOLE,) * len(levels),
+        out_specs=(WHOLE, WHOLE),
         compiler_params=PARAMS,
         cost_estimate=small_cost(),
-        name="bank_" + "_".join(map(str, levels)),
+        name="banks",
     )(after, weights, numbers)
 
 
@@ -313,16 +321,16 @@
     )(own, weights, numbers)
 
 
-def own_parts(level, own, bank):
+def own_parts(level, own, low, high):
     return pl.pallas_call(
         functools.partial(parts_kernel, trim_of(level)),
         out_shape=jax.ShapeDtypeStruct((2, 2 * HALF, FRAMES[level]), F32),
-        in_specs=[WHOLE] * 2,
+        in_specs=[WHOLE] * 3,
         out_specs=WHOLE,
         compiler_params=PARAMS,
         cost_estimate=small_cost(),
         name=f"own_parts_{level}",
-    )(own, bank)
+    )(own, low, high)
 
 
 def trim_of(level):
@@ -369,16 +377,16 @@
     )(own, partner, bank)
 
 
-def merge_last(parts, theirs, bank):
+def merge_last(parts, theirs, low, high):
     return pl.pallas_call(
         merge_last_kernel,
         out_shape=jax.ShapeDtypeStruct((2, ROWS, BINS), BF16),
-        in_specs=[WHOLE] * 3,
+        in_specs=[WHOLE] * 4,
         out_specs=WHOLE,
         scratch_shapes=[pltpu.VMEM((COLS // 2, FRAMES[LEVELS - 1]), BF16)],
         compiler_params=PARAMS,
         name="merge_last",
-    )(parts, theirs, bank)
+    )(parts, theirs, low, high)
 
 
 def body(echoes, transmit_chirp, band_weights, band_offsets, band_widths, child_rows):
@@ -395,7 +403,7 @@
     late = lax.ppermute(within_late, "range", [(i ^ 1, i) for i in range(count) if not takes_early(i)])
     taps = jnp.swapaxes(band_weights, 3, 4).reshape(LEVELS, PART, ROWS)
     numbers = jnp.concatenate([band_offsets, band_widths, child_rows[:, None]], axis=1)
-    toeplitz, bank, bank_last, weights, numbers = prepare(transmit_chirp, taps, numbers)
+    toeplitz, bank, low, weights, numbers = prepare(transmit_chirp, taps, numbers)
     sent = compress(True, echoes, odd, late, early, toeplitz)
     blocks = lax.axis_size("aperture")
 
@@ -407,7 +415,7 @@
     sent, partner = merge_sent(0, own, theirs, bank)
     theirs = trade(sent, 1)
     own = merge_kept(0, own, partner, bank)
-    (bank,) = make_banks((1,), own, weights, numbers)
+    bank, high = make_banks(own, weights, numbers)
     sent, partner = merge_sent(1, own, theirs, bank)
     theirs = trade(sent, 2)
     own = merge_kept(1, own, partner, bank)
@@ -415,8 +423,8 @@
     sent, partner = merge_sent(2, part, theirs, bank, True)
     theirs = trade(sent, 3)
     own = merge_kept(2, own, partner, bank)
-    parts = own_parts(3, own, bank_last)
-    return merge_last(parts, theirs, bank_last)
+    parts = own_parts(3, own, low, high)
+    return merge_last(parts, theirs, low, high)
 
 
 def solution(mesh):

time: 46.8 us -> 46.7 us (level)
  the two profiles are of different devices: /device:TPU:20 before, /device:TPU:28 now
where the time goes in v5:
time: 46.7 us; the launch traced here: 46.4 us
  starting transfers between devices  26.8 us (57%)
  Pallas kernels  13.4 us (29%)
  waiting for transfers between devices  4.44 us (10%)
  other arithmetic  0.89 us (2%)
  local copies, waits for them, and re-layouts  0.67 us (1%)
    ppermute x4, starting transfers between devices, trade(): lax.ppermute(message, 'aperture', [(i, i ^ 1 << level) for i in range(blo...  20 us
    ppermute x1, starting transfers between devices, body(): odd = lax.ppermute(between, 'range', pairs + [(j, i) for i, j in pairs])  4.22 us
    ppermute x4, waiting for transfers between devices, trade(): lax.ppermute(message, 'aperture', [(i, i ^ 1 << level) for i in range(blo...  2.94 us
    pallas_call x3, Pallas kernels, merge_kept(): pl.pallas_call(functools.partial(merge_kept_kernel, trim_of(level), RIMS[...  2.79 us
    pallas_call x3, Pallas kernels, merge_sent(): pl.pallas_call(functools.partial(kernel, trim_of(level), RIMS[level + 1])...  2.25 us
    ppermute x1, starting transfers between devices, body(): lax.ppermute(within_late, 'range', [(i ^ 1, i) for i in range(count) if n...  1.92 us
    pallas_call x1, Pallas kernels, prepare(): pl.pallas_call(prepare_kernel, out_shape=(jax.ShapeDtypeStruct((2 * LANES...  1.82 us
    pallas_call x1, Pallas kernels, merge_last(): pl.pallas_call(merge_last_kernel, out_shape=jax.ShapeDtypeStruct((2, ROWS...  1.69 us
  transfers between devices with their start and end apart: 7, of which 5 were waited for; matrix products, arithmetic and copies ran while one was open for 0% of the time, Pallas kernels for 20%

profile of v5, /device:TPU:28, one launch (start us, length us, event | category | flops | bytes accessed | tf_op | source)
XLA Modules:
  0.0 46.4 jit_solution(7084467668185701536)
XLA Ops:
  0.0 0.9 %broadcast_select_fusion = (bf16[2,32,384]{2,1,0:T(8,128)(2,1)S(1)}, bf16[2,32,384]{2,1,0:T(8,128)(2,1)S(1)}, bf16[2,32,384]{2,1,0:T(8,128)(2,1)S(1)}) fusion(pred[]{:T(512)S(6)} %eq.11, bf16[2,32,1024]{2,1,0:T(8,128)(2,1)} %echoes.3, pred[]{:T(512)S(6)} %eq.10, pred[]{:T(512)S(6)} %ne.14), kind=kLoop, calls=%fused_computation | loop fusion | flops 73728 | bytes 245763 | tf_op jit(solution)/shard_map/jit(_where)/select_n | solution.py:398
  0.9 0.0 copy-start.3
  0.9 0.7 %collective-permute-start.2 = (bf16[2,32,384]{2,1,0:T(8,128)(2,1)S(1)}, bf16[2,32,384]{2,1,0:T(8,128)(2,1)S(1)}, u32[]{:S(2)}, u32[]{:S(2)}) collective-permute-start(bf16[2,32,384]{2,1,0:T(8,128)(2,1)S(1)} %get-tuple-element.35), channel_id=1, source_target_pairs={{5,4},{13,12},{21,20},{29,28},{37,36},{45,44},{53,52},{61,60},{69,... | collective-permute-start | bytes 147464 | tf_op jit(solution)/shard_map/ppermute | solution.py:401
  1.6 0.0 copy-start.5
  1.6 4.2 %collective-permute-start = (bf16[2,32,384]{2,1,0:T(8,128)(2,1)S(1)}, bf16[2,32,384]{2,1,0:T(8,128)(2,1)S(1)}, u32[]{:S(2)}, u32[]{:S(2)}) collective-permute-start(bf16[2,32,384]{2,1,0:T(8,128)(2,1)S(1)} %get-tuple-element.36), channel_id=1, source_target_pairs={{1,2},{3,4},{5,6},{2,1},{4,3},{6,5},{9,10},{11,12},{13,14},{10,9},... | collective-permute-start | bytes 147464 | tf_op jit(solution)/shard_map/ppermute | solution.py:402
  5.8 1.9 %collective-permute-start.1 = (bf16[2,32,384]{2,1,0:T(8,128)(2,1)S(1)}, bf16[2,32,384]{2,1,0:T(8,128)(2,1)S(1)}, u32[]{:S(2)}, u32[]{:S(2)}) collective-permute-start(bf16[2,32,384]{2,1,0:T(8,128)(2,1)S(1)} %get-tuple-element.37), channel_id=1, source_target_pairs={{1,0},{0,1},{3,2},{2,3},{4,5},{7,6},{6,7},{9,8},{8,9},{11,10},{10,... | collective-permute-start | bytes 147464 | tf_op jit(solution)/shard_map/ppermute | solution.py:403
  7.8 0.0 copy-start.2
  7.8 0.6 %copy-done.2 = bf16[2,512]{1,0:T(2,128)(2,1)S(1)} copy-done((bf16[2,512]{1,0:T(2,128)(2,1)S(1)}, bf16[2,512]{1,0:T(2,128)(2,1)}, u32[]{:S(2)}) %copy-start.2) | copy-done | bytes 2072
  8.5 1.8 %prepare.1 = (bf16[256,1280]{1,0:T(8,128)(2,1)S(1)}, bf16[512,768]{1,0:T(8,128)(2,1)S(1)}, bf16[256,768]{1,0:T(8,128)(2,1)S(1)}, f32[32,256]{1,0:T(8,128)S(1)}, f32[32,128]{1,0:T(8,128)S(1)}) custom-call(bf16[2,512]{1,0:T(2,128)(2,1)S(1)} %copy-done.2, f32[4,64,32]{2,1,0:T(8,128)S(1)} %bitcast.6, s32[4,5,32]{2,1,0:T(8,128)S(1)} %pad_add_fusion.numbers_in), custom_call_target="tpu_custom_call" | custom-call | flops 1000000000 | bytes 2000000 | tf_op jit(solution)/shard_map/prepare/pallas_call | solution.py:282
  10.3 0.0 collective-permute-done.2.early
  10.3 0.0 collective-permute-done.odd
  10.3 1.5 %collective-permute-done.1.late = bf16[2,32,384]{2,1,0:T(8,128)(2,1)S(1)} collective-permute-done((bf16[2,32,384]{2,1,0:T(8,128)(2,1)S(1)}, bf16[2,32,384]{2,1,0:T(8,128)(2,1)S(1)}, u32[]{:S(2)}, u32[]{:S(2)}) %collective-permute-start.1) | collective-permute-done | bytes 49184 | tf_op jit(solution)/shard_map/ppermute | solution.py:403
  11.8 0.4 compress_sent.1
  12.2 1.9 %collective-permute-start.3 = (bf16[32,1280]{1,0:T(8,128)(2,1)S(1)}, bf16[32,1280]{1,0:T(8,128)(2,1)S(1)}, u32[]{:S(2)}, u32[]{:S(2)}) collective-permute-start(bf16[32,1280]{1,0:T(8,128)(2,1)S(1)} %compress_sent.1), channel_id=1, source_target_pairs={{0,8},{8,0},{16,24},{24,16},{32,40},{40,32},{48,56},{56,48},{64,72... | collective-permute-start | bytes 245768 | tf_op jit(solution)/shard_map/ppermute | solution.py:411
  14.1 0.6 %compress_kept.1.own = bf16[192,1280]{1,0:T(8,128)(2,1)S(1)} custom-call(bf16[2,32,1024]{2,1,0:T(8,128)(2,1)S(1)} %copy-done, bf16[2,32,384]{2,1,0:T(8,128)(2,1)S(1)} %collective-permute-done.odd, bf16[2,32,384]{2,1,0:T(8,128)(2,1)S(1)} %collective-permute-done.1.late, bf16[2,32,384]{2,1,0:T(8,128)(2,1)S(1)} %collective-permute-done.2.early, ...), custom_call_target="tpu_custom_call" | custom-call | flops 200000000 | bytes 1000000 | tf_op jit(solution)/shard_map/compress_kept/pallas_call | solution.py:344
  14.7 0.7 %collective-permute-done.3.theirs = bf16[32,1280]{1,0:T(8,128)(2,1)S(1)} collective-permute-done((bf16[32,1280]{1,0:T(8,128)(2,1)S(1)}, bf16[32,1280]{1,0:T(8,128)(2,1)S(1)}, u32[]{:S(2)}, u32[]{:S(2)}) %collective-permute-start.3) | collective-permute-done | bytes 81952 | tf_op jit(solution)/shard_map/ppermute | solution.py:411
  15.4 0.8 %merge_0_sent.1 = (bf16[32,1280]{1,0:T(8,128)(2,1)S(1)}, bf16[192,1280]{1,0:T(8,128)(2,1)S(1)}) custom-call(bf16[192,1280]{1,0:T(8,128)(2,1)S(1)} %compress_kept.1.own, bf16[32,1280]{1,0:T(8,128)(2,1)S(1)} %collective-permute-done.3.theirs, bf16[512,768]{1,0:T(8,128)(2,1)S(1)} %get-tuple-element.21.bank), custom_call_target="tpu_custom_call" | custom-call | tf_op jit(solution)/shard_map/merge_0_sent/pallas_call | solution.py:358
  16.2 4.3 %collective-permute-start.4 = (bf16[32,1280]{1,0:T(8,128)(2,1)S(1)}, bf16[32,1280]{1,0:T(8,128)(2,1)S(1)}, u32[]{:S(2)}, u32[]{:S(2)}) collective-permute-start(bf16[32,1280]{1,0:T(8,128)(2,1)S(1)} %get-tuple-element.23), channel_id=1, source_target_pairs={{0,16},{8,24},{16,0},{24,8},{32,48},{40,56},{48,32},{56,40},{64,80... | collective-permute-start | bytes 245768 | tf_op jit(solution)/shard_map/ppermute | solution.py:411
  20.4 1.0 %merge_0_kept.1.after.own = bf16[192,1280]{1,0:T(8,128)(2,1)S(1)} custom-call(bf16[192,1280]{1,0:T(8,128)(2,1)S(1)} %compress_kept.1.own, bf16[192,1280]{1,0:T(8,128)(2,1)S(1)} %get-tuple-element.22.partner, bf16[512,768]{1,0:T(8,128)(2,1)S(1)} %get-tuple-element.21.bank), custom_call_target="tpu_custom_call" | custom-call | flops 1000 | bytes 1000 | tf_op jit(solution)/shard_map/merge_0_kept/pallas_call | solution.py:369
  21.4 1.6 %banks.1 = (bf16[512,768]{1,0:T(8,128)(2,1)S(1)}, bf16[256,768]{1,0:T(8,128)(2,1)S(1)}) custom-call(bf16[192,1280]{1,0:T(8,128)(2,1)S(1)} %merge_0_kept.1.after.own, f32[32,256]{1,0:T(8,128)S(1)} %get-tuple-element.24.weights, f32[32,128]{1,0:T(8,128)S(1)} %get-tuple-element.25.numbers), custom_call_target="tpu_custom_call" | custom-call | flops 1000 | bytes 1000 | tf_op jit(solution)/shard_map/banks/pallas_call | solution.py:301
  23.0 0.2 collective-permute-done.4.theirs
  23.2 0.8 %merge_1_sent.1 = (bf16[32,1152]{1,0:T(8,128)(2,1)S(1)}, bf16[192,1280]{1,0:T(8,128)(2,1)S(1)}) custom-call(bf16[192,1280]{1,0:T(8,128)(2,1)S(1)} %merge_0_kept.1.after.own, bf16[32,1280]{1,0:T(8,128)(2,1)S(1)} %collective-permute-done.4.theirs, bf16[512,768]{1,0:T(8,128)(2,1)S(1)} %get-tuple-element.26.bank), custom_call_target="tpu_custom_call" | custom-call | tf_op jit(solution)/shard_map/merge_1_sent/pallas_call | solution.py:358
  24.0 6.1 %collective-permute-start.5 = (bf16[32,1152]{1,0:T(8,128)(2,1)S(1)}, bf16[32,1152]{1,0:T(8,128)(2,1)S(1)}, u32[]{:S(2)}, u32[]{:S(2)}) collective-permute-start(bf16[32,1152]{1,0:T(8,128)(2,1)S(1)} %get-tuple-element.29), channel_id=1, source_target_pairs={{0,32},{8,40},{16,48},{24,56},{32,0},{40,8},{48,16},{56,24},{64,96... | collective-permute-start | bytes 221192 | tf_op jit(solution)/shard_map/ppermute | solution.py:411
  30.1 1.0 %merge_1_kept.1.own = bf16[192,1152]{1,0:T(8,128)(2,1)S(1)} custom-call(bf16[192,1280]{1,0:T(8,128)(2,1)S(1)} %merge_0_kept.1.after.own, bf16[192,1280]{1,0:T(8,128)(2,1)S(1)} %get-tuple-element.27.partner, bf16[512,768]{1,0:T(8,128)(2,1)S(1)} %get-tuple-element.26.bank), custom_call_target="tpu_custom_call" | custom-call | flops 1000 | bytes 1000 | tf_op jit(solution)/shard_map/merge_1_kept/pallas_call | solution.py:369
  31.1 1.4 %bank_and_part_2.1 = (bf16[512,768]{1,0:T(8,128)(2,1)S(1)}, f32[32,1152]{1,0:T(8,128)S(1)}) custom-call(bf16[192,1152]{1,0:T(8,128)(2,1)S(1)} %merge_1_kept.1.own, f32[32,256]{1,0:T(8,128)S(1)} %get-tuple-element.24.weights, f32[32,128]{1,0:T(8,128)S(1)} %get-tuple-element.25.numbers), custom_call_target="tpu_custom_call" | custom-call | flops 1000 | bytes 1000 | tf_op jit(solution)/shard_map/bank_and_part_2/pallas_call | solution.py:313
  32.5 1.3 %collective-permute-done.5.theirs = bf16[32,1152]{1,0:T(8,128)(2,1)S(1)} collective-permute-done((bf16[32,1152]{1,0:T(8,128)(2,1)S(1)}, bf16[32,1152]{1,0:T(8,128)(2,1)S(1)}, u32[]{:S(2)}, u32[]{:S(2)}) %collective-permute-start.5) | collective-permute-done | bytes 73760 | tf_op jit(solution)/shard_map/ppermute | solution.py:411
  33.8 0.6 %merge_2_sent.1 = (bf16[32,1152]{1,0:T(8,128)(2,1)S(1)}, bf16[192,1152]{1,0:T(8,128)(2,1)S(1)}) custom-call(f32[32,1152]{1,0:T(8,128)S(1)} %get-tuple-element.28.part, bf16[32,1152]{1,0:T(8,128)(2,1)S(1)} %collective-permute-done.5.theirs, bf16[512,768]{1,0:T(8,128)(2,1)S(1)} %get-tuple-element.30.bank), custom_call_target="tpu_custom_call" | custom-call | tf_op jit(solution)/shard_map/merge_2_sent/pallas_call | solution.py:358
  34.5 7.7 %collective-permute-start.6 = (bf16[32,1152]{1,0:T(8,128)(2,1)S(1)}, bf16[32,1152]{1,0:T(8,128)(2,1)S(1)}, u32[]{:S(2)}, u32[]{:S(2)}) collective-permute-start(bf16[32,1152]{1,0:T(8,128)(2,1)S(1)} %get-tuple-element.34), channel_id=1, source_target_pairs={{0,64},{8,72},{16,80},{24,88},{32,96},{40,104},{48,112},{56,120},{... | collective-permute-start | bytes 221192 | tf_op jit(solution)/shard_map/ppermute | solution.py:411
  42.2 0.9 %merge_2_kept.1.own = bf16[192,1152]{1,0:T(8,128)(2,1)S(1)} custom-call(bf16[192,1152]{1,0:T(8,128)(2,1)S(1)} %merge_1_kept.1.own, bf16[192,1152]{1,0:T(8,128)(2,1)S(1)} %get-tuple-element.31.partner, bf16[512,768]{1,0:T(8,128)(2,1)S(1)} %get-tuple-element.30.bank), custom_call_target="tpu_custom_call" | custom-call | flops 1000 | bytes 1000 | tf_op jit(solution)/shard_map/merge_2_kept/pallas_call | solution.py:369
  43.0 0.9 %own_parts_3.1.parts = f32[2,32,1152]{2,1,0:T(8,128)S(1)} custom-call(bf16[192,1152]{1,0:T(8,128)(2,1)S(1)} %merge_2_kept.1.own, bf16[256,768]{1,0:T(8,128)(2,1)S(1)} %get-tuple-element.32.low, bf16[256,768]{1,0:T(8,128)(2,1)S(1)} %get-tuple-element.33.high), custom_call_target="tpu_custom_call" | custom-call | flops 1000 | bytes 1000 | tf_op jit(solution)/shard_map/own_parts_3/pallas_call | solution.py:325
  44.0 0.8 %collective-permute-done.6.theirs = bf16[32,1152]{1,0:T(8,128)(2,1)S(1)} collective-permute-done((bf16[32,1152]{1,0:T(8,128)(2,1)S(1)}, bf16[32,1152]{1,0:T(8,128)(2,1)S(1)}, u32[]{:S(2)}, u32[]{:S(2)}) %collective-permute-start.6) | collective-permute-done | bytes 73760 | tf_op jit(solution)/shard_map/ppermute | solution.py:411
  44.7 1.7 %merge_last.1 = bf16[2,32,1024]{2,1,0:T(8,128)(2,1)} custom-call(f32[2,32,1152]{2,1,0:T(8,128)S(1)} %own_parts_3.1.parts, bf16[32,1152]{1,0:T(8,128)(2,1)S(1)} %collective-permute-done.6.theirs, bf16[256,768]{1,0:T(8,128)(2,1)S(1)} %get-tuple-element.32.low, bf16[256,768]{1,0:T(8,128)(2,1)S(1)} %get-tuple-element.33.high), custom_call_target="tpu_custom_call" | custom-call | tf_op jit(solution)/shard_map/merge_last/pallas_call | solution.py:381
  (9 shorter events, 0.0 us)
Async XLA Ops:
  0.0 7.7 %copy-start.4 = (s32[4,2,32]{2,1,0:T(2,128)S(1)}, s32[4,2,32]{2,1,0:T(2,128)}, u32[]{:S(2)}) copy-start(s32[4,2,32]{2,1,0:T(2,128)} %param.9) | copy-start | bytes 3076
  0.0 7.8 %copy-start.1 = (f32[4,2,2,32,16]{3,4,2,1,0:T(8,128)S(1)}, f32[4,2,2,32,16]{3,4,2,1,0:T(8,128)}, u32[]{:S(2)}) copy-start(f32[4,2,2,32,16]{3,4,2,1,0:T(8,128)} %param.8) | copy-start | bytes 98308
  0.9 6.9 %copy-start.3 = (s32[4,2,32]{2,1,0:T(2,128)S(1)}, s32[4,2,32]{2,1,0:T(2,128)}, u32[]{:S(2)}) copy-start(s32[4,2,32]{2,1,0:T(2,128)} %param.10) | copy-start | bytes 3076
  0.9 9.4 %collective-permute-start.2 = (bf16[2,32,384]{2,1,0:T(8,128)(2,1)S(1)}, bf16[2,32,384]{2,1,0:T(8,128)(2,1)S(1)}, u32[]{:S(2)}, u32[]{:S(2)}) collective-permute-start(bf16[2,32,384]{2,1,0:T(8,128)(2,1)S(1)} %get-tuple-element.35), channel_id=1, source_target_pairs={{5,4},{13,12},{21,20},{29,28},{37,36},{45,44},{53,52},{61,60},{69,... | collective-permute-start | bytes 147464 | tf_op jit(solution)/shard_map/ppermute | solution.py:401
  1.6 6.2 %copy-start.5 = (s32[4,32]{1,0:T(4,128)S(1)}, s32[4,32]{1,0:T(4,128)}, u32[]{:S(2)}) copy-start(s32[4,32]{1,0:T(4,128)} %param.11) | copy-start | bytes 1540
  1.6 8.7 %collective-permute-start = (bf16[2,32,384]{2,1,0:T(8,128)(2,1)S(1)}, bf16[2,32,384]{2,1,0:T(8,128)(2,1)S(1)}, u32[]{:S(2)}, u32[]{:S(2)}) collective-permute-start(bf16[2,32,384]{2,1,0:T(8,128)(2,1)S(1)} %get-tuple-element.36), channel_id=1, source_target_pairs={{1,2},{3,4},{5,6},{2,1},{4,3},{6,5},{9,10},{11,12},{13,14},{10,9},... | collective-permute-start | bytes 147464 | tf_op jit(solution)/shard_map/ppermute | solution.py:402
  5.8 6.0 %collective-permute-start.1 = (bf16[2,32,384]{2,1,0:T(8,128)(2,1)S(1)}, bf16[2,32,384]{2,1,0:T(8,128)(2,1)S(1)}, u32[]{:S(2)}, u32[]{:S(2)}) collective-permute-start(bf16[2,32,384]{2,1,0:T(8,128)(2,1)S(1)} %get-tuple-element.37), channel_id=1, source_target_pairs={{1,0},{0,1},{3,2},{2,3},{4,5},{7,6},{6,7},{9,8},{8,9},{11,10},{10,... | collective-permute-start | bytes 147464 | tf_op jit(solution)/shard_map/ppermute | solution.py:403
  7.8 0.7 %copy-start.2 = (bf16[2,512]{1,0:T(2,128)(2,1)S(1)}, bf16[2,512]{1,0:T(2,128)(2,1)}, u32[]{:S(2)}) copy-start(bf16[2,512]{1,0:T(2,128)(2,1)} %chirp.1) | copy-start | bytes 6148
  8.5 3.3 %copy-start = (bf16[2,32,1024]{2,1,0:T(8,128)(2,1)S(1)}, bf16[2,32,1024]{2,1,0:T(8,128)(2,1)}, u32[]{:S(2)}) copy-start(bf16[2,32,1024]{2,1,0:T(8,128)(2,1)} %echoes.3) | copy-start | bytes 393220
  12.2 3.2 %collective-permute-start.3 = (bf16[32,1280]{1,0:T(8,128)(2,1)S(1)}, bf16[32,1280]{1,0:T(8,128)(2,1)S(1)}, u32[]{:S(2)}, u32[]{:S(2)}) collective-permute-start(bf16[32,1280]{1,0:T(8,128)(2,1)S(1)} %compress_sent.1), channel_id=1, source_target_pairs={{0,8},{8,0},{16,24},{24,16},{32,40},{40,32},{48,56},{56,48},{64,72... | collective-permute-start | bytes 245768 | tf_op jit(solution)/shard_map/ppermute | solution.py:411
  16.2 7.0 %collective-permute-start.4 = (bf16[32,1280]{1,0:T(8,128)(2,1)S(1)}, bf16[32,1280]{1,0:T(8,128)(2,1)S(1)}, u32[]{:S(2)}, u32[]{:S(2)}) collective-permute-start(bf16[32,1280]{1,0:T(8,128)(2,1)S(1)} %get-tuple-element.23), channel_id=1, source_target_pairs={{0,16},{8,24},{16,0},{24,8},{32,48},{40,56},{48,32},{56,40},{64,80... | collective-permute-start | bytes 245768 | tf_op jit(solution)/shard_map/ppermute | solution.py:411
  24.0 9.8 %collective-permute-start.5 = (bf16[32,1152]{1,0:T(8,128)(2,1)S(1)}, bf16[32,1152]{1,0:T(8,128)(2,1)S(1)}, u32[]{:S(2)}, u32[]{:S(2)}) collective-permute-start(bf16[32,1152]{1,0:T(8,128)(2,1)S(1)} %get-tuple-element.29), channel_id=1, source_target_pairs={{0,32},{8,40},{16,48},{24,56},{32,0},{40,8},{48,16},{56,24},{64,96... | collective-permute-start | bytes 221192 | tf_op jit(solution)/shard_map/ppermute | solution.py:411
  34.5 10.3 %collective-permute-start.6 = (bf16[32,1152]{1,0:T(8,128)(2,1)S(1)}, bf16[32,1152]{1,0:T(8,128)(2,1)S(1)}, u32[]{:S(2)}, u32[]{:S(2)}) collective-permute-start(bf16[32,1152]{1,0:T(8,128)(2,1)S(1)} %get-tuple-element.34), channel_id=1, source_target_pairs={{0,64},{8,72},{16,80},{24,88},{32,96},{40,104},{48,112},{56,120},{... | collective-permute-start | bytes 221192 | tf_op jit(solution)/shard_map/ppermute | solution.py:411

commit v6 on v5

--- a/solution.py
+++ b/solution.py
@@ -248,14 +248,22 @@
     fill_stack(after, rounded(fine_sum(product, trim), rim))
 
 
-def merge_last_kernel(parts, theirs, low, high, out, partner):
+def merge_last_kernel(parts, theirs, low, high, out, partner, held, sems):
     fill_stack(partner, theirs[...])
     product = last_product(low, high, 1, partner)
+    copies = []
     for half in range(2):
         total = parts[half] + fine_sum(product[half * OUTS : (half + 1) * OUTS], RIM_LATE)
         total = total[:, 0:BINS].astype(BF16)
+        rows = slice(half * HALF, (half + 1) * HALF)
         for part in range(2):
-            out[part, half * HALF : (half + 1) * HALF] = total[part * HALF : (part + 1) * HALF]
+            held[part, rows] = total[part * HALF : (part + 1) * HALF]
+        copies.append(
+            pltpu.make_async_copy(held.at[:, rows], out.at[:, rows], sems.at[half])
+        )
+        copies[half].start()
+    for copy in copies:
+        copy.wait()
 
 
 WHOLE = pl.BlockSpec(memory_space=pltpu.VMEM)
@@ -382,8 +390,12 @@
         merge_last_kernel,
         out_shape=jax.ShapeDtypeStruct((2, ROWS, BINS), BF16),
         in_specs=[WHOLE] * 4,
-        out_specs=WHOLE,
-        scratch_shapes=[pltpu.VMEM((COLS // 2, FRAMES[LEVELS - 1]), BF16)],
+        out_specs=pl.BlockSpec(memory_space=pl.ANY),
+        scratch_shapes=[
+            pltpu.VMEM((COLS // 2, FRAMES[LEVELS - 1]), BF16),
+            pltpu.VMEM((2, ROWS, BINS), BF16),
+            pltpu.SemaphoreType.DMA((2,)),
+        ],
         compiler_params=PARAMS,
         name="merge_last",
     )(parts, theirs, low, high)

time: 46.7 us -> 46.7 us (level)
  no operation moved by 1% of the time
where the time goes in v6:
time: 46.7 us; the launch traced here: 46.4 us
  starting transfers between devices  26.8 us (57%)
  Pallas kernels  13.4 us (29%)
  waiting for transfers between devices  4.44 us (10%)
  other arithmetic  0.89 us (2%)
  local copies, waits for them, and re-layouts  0.67 us (1%)
    ppermute x4, starting transfers between devices, trade(): lax.ppermute(message, 'aperture', [(i, i ^ 1 << level) for i in range(blo...  20 us
    ppermute x1, starting transfers between devices, body(): odd = lax.ppermute(between, 'range', pairs + [(j, i) for i, j in pairs])  4.22 us
    ppermute x4, waiting for transfers between devices, trade(): lax.ppermute(message, 'aperture', [(i, i ^ 1 << level) for i in range(blo...  2.94 us
    pallas_call x3, Pallas kernels, merge_kept(): pl.pallas_call(functools.partial(merge_kept_kernel, trim_of(level), RIMS[...  2.79 us
    pallas_call x3, Pallas kernels, merge_sent(): pl.pallas_call(functools.partial(kernel, trim_of(level), RIMS[level + 1])...  2.25 us
    ppermute x1, starting transfers between devices, body(): lax.ppermute(within_late, 'range', [(i ^ 1, i) for i in range(count) if n...  1.92 us
    pallas_call x1, Pallas kernels, prepare(): pl.pallas_call(prepare_kernel, out_shape=(jax.ShapeDtypeStruct((2 * LANES...  1.82 us
    pallas_call x1, Pallas kernels, merge_last(): pl.pallas_call(merge_last_kernel, out_shape=jax.ShapeDtypeStruct((2, ROWS...  1.68 us
  transfers between devices with their start and end apart: 7, of which 5 were waited for; matrix products, arithmetic and copies ran while one was open for 0% of the time, Pallas kernels for 20%

profile of v6, /device:TPU:28, one launch (start us, length us, event | category | flops | bytes accessed | tf_op | source)
XLA Modules:
  0.0 46.4 jit_solution(811298455675621124)
XLA Ops:
  0.0 0.9 %broadcast_select_fusion = (bf16[2,32,384]{2,1,0:T(8,128)(2,1)S(1)}, bf16[2,32,384]{2,1,0:T(8,128)(2,1)S(1)}, bf16[2,32,384]{2,1,0:T(8,128)(2,1)S(1)}) fusion(pred[]{:T(512)S(6)} %eq.11, bf16[2,32,1024]{2,1,0:T(8,128)(2,1)} %echoes.3, pred[]{:T(512)S(6)} %eq.10, pred[]{:T(512)S(6)} %ne.14), kind=kLoop, calls=%fused_computation | loop fusion | flops 73728 | bytes 245763 | tf_op jit(solution)/shard_map/jit(_where)/select_n | solution.py:410
  0.9 0.0 copy-start.3
  0.9 0.7 %collective-permute-start.2 = (bf16[2,32,384]{2,1,0:T(8,128)(2,1)S(1)}, bf16[2,32,384]{2,1,0:T(8,128)(2,1)S(1)}, u32[]{:S(2)}, u32[]{:S(2)}) collective-permute-start(bf16[2,32,384]{2,1,0:T(8,128)(2,1)S(1)} %get-tuple-element.35), channel_id=1, source_target_pairs={{5,4},{13,12},{21,20},{29,28},{37,36},{45,44},{53,52},{61,60},{69,... | collective-permute-start | bytes 147464 | tf_op jit(solution)/shard_map/ppermute | solution.py:413
  1.6 0.0 copy-start.5
  1.6 4.2 %collective-permute-start = (bf16[2,32,384]{2,1,0:T(8,128)(2,1)S(1)}, bf16[2,32,384]{2,1,0:T(8,128)(2,1)S(1)}, u32[]{:S(2)}, u32[]{:S(2)}) collective-permute-start(bf16[2,32,384]{2,1,0:T(8,128)(2,1)S(1)} %get-tuple-element.36), channel_id=1, source_target_pairs={{1,2},{3,4},{5,6},{2,1},{4,3},{6,5},{9,10},{11,12},{13,14},{10,9},... | collective-permute-start | bytes 147464 | tf_op jit(solution)/shard_map/ppermute | solution.py:414
  5.8 1.9 %collective-permute-start.1 = (bf16[2,32,384]{2,1,0:T(8,128)(2,1)S(1)}, bf16[2,32,384]{2,1,0:T(8,128)(2,1)S(1)}, u32[]{:S(2)}, u32[]{:S(2)}) collective-permute-start(bf16[2,32,384]{2,1,0:T(8,128)(2,1)S(1)} %get-tuple-element.37), channel_id=1, source_target_pairs={{1,0},{0,1},{3,2},{2,3},{4,5},{7,6},{6,7},{9,8},{8,9},{11,10},{10,... | collective-permute-start | bytes 147464 | tf_op jit(solution)/shard_map/ppermute | solution.py:415
  7.8 0.0 copy-start.2
  7.8 0.6 %copy-done.2 = bf16[2,512]{1,0:T(2,128)(2,1)S(1)} copy-done((bf16[2,512]{1,0:T(2,128)(2,1)S(1)}, bf16[2,512]{1,0:T(2,128)(2,1)}, u32[]{:S(2)}) %copy-start.2) | copy-done | bytes 2072
  8.5 1.8 %prepare.1 = (bf16[256,1280]{1,0:T(8,128)(2,1)S(1)}, bf16[512,768]{1,0:T(8,128)(2,1)S(1)}, bf16[256,768]{1,0:T(8,128)(2,1)S(1)}, f32[32,256]{1,0:T(8,128)S(1)}, f32[32,128]{1,0:T(8,128)S(1)}) custom-call(bf16[2,512]{1,0:T(2,128)(2,1)S(1)} %copy-done.2, f32[4,64,32]{2,1,0:T(8,128)S(1)} %bitcast.6, s32[4,5,32]{2,1,0:T(8,128)S(1)} %pad_add_fusion.numbers_in), custom_call_target="tpu_custom_call" | custom-call | flops 1000000000 | bytes 2000000 | tf_op jit(solution)/shard_map/prepare/pallas_call | solution.py:290
  10.3 0.0 collective-permute-done.2.early
  10.3 0.0 collective-permute-done.odd
  10.3 1.5 %collective-permute-done.1.late = bf16[2,32,384]{2,1,0:T(8,128)(2,1)S(1)} collective-permute-done((bf16[2,32,384]{2,1,0:T(8,128)(2,1)S(1)}, bf16[2,32,384]{2,1,0:T(8,128)(2,1)S(1)}, u32[]{:S(2)}, u32[]{:S(2)}) %collective-permute-start.1) | collective-permute-done | bytes 49184 | tf_op jit(solution)/shard_map/ppermute | solution.py:415
  11.8 0.4 compress_sent.1
  12.2 1.9 %collective-permute-start.3 = (bf16[32,1280]{1,0:T(8,128)(2,1)S(1)}, bf16[32,1280]{1,0:T(8,128)(2,1)S(1)}, u32[]{:S(2)}, u32[]{:S(2)}) collective-permute-start(bf16[32,1280]{1,0:T(8,128)(2,1)S(1)} %compress_sent.1), channel_id=1, source_target_pairs={{0,8},{8,0},{16,24},{24,16},{32,40},{40,32},{48,56},{56,48},{64,72... | collective-permute-start | bytes 245768 | tf_op jit(solution)/shard_map/ppermute | solution.py:423
  14.1 0.6 %compress_kept.1.own = bf16[192,1280]{1,0:T(8,128)(2,1)S(1)} custom-call(bf16[2,32,1024]{2,1,0:T(8,128)(2,1)S(1)} %copy-done, bf16[2,32,384]{2,1,0:T(8,128)(2,1)S(1)} %collective-permute-done.odd, bf16[2,32,384]{2,1,0:T(8,128)(2,1)S(1)} %collective-permute-done.1.late, bf16[2,32,384]{2,1,0:T(8,128)(2,1)S(1)} %collective-permute-done.2.early, ...), custom_call_target="tpu_custom_call" | custom-call | flops 200000000 | bytes 1000000 | tf_op jit(solution)/shard_map/compress_kept/pallas_call | solution.py:352
  14.7 0.7 %collective-permute-done.3.theirs = bf16[32,1280]{1,0:T(8,128)(2,1)S(1)} collective-permute-done((bf16[32,1280]{1,0:T(8,128)(2,1)S(1)}, bf16[32,1280]{1,0:T(8,128)(2,1)S(1)}, u32[]{:S(2)}, u32[]{:S(2)}) %collective-permute-start.3) | collective-permute-done | bytes 81952 | tf_op jit(solution)/shard_map/ppermute | solution.py:423
  15.4 0.8 %merge_0_sent.1 = (bf16[32,1280]{1,0:T(8,128)(2,1)S(1)}, bf16[192,1280]{1,0:T(8,128)(2,1)S(1)}) custom-call(bf16[192,1280]{1,0:T(8,128)(2,1)S(1)} %compress_kept.1.own, bf16[32,1280]{1,0:T(8,128)(2,1)S(1)} %collective-permute-done.3.theirs, bf16[512,768]{1,0:T(8,128)(2,1)S(1)} %get-tuple-element.21.bank), custom_call_target="tpu_custom_call" | custom-call | tf_op jit(solution)/shard_map/merge_0_sent/pallas_call | solution.py:366
  16.2 4.3 %collective-permute-start.4 = (bf16[32,1280]{1,0:T(8,128)(2,1)S(1)}, bf16[32,1280]{1,0:T(8,128)(2,1)S(1)}, u32[]{:S(2)}, u32[]{:S(2)}) collective-permute-start(bf16[32,1280]{1,0:T(8,128)(2,1)S(1)} %get-tuple-element.23), channel_id=1, source_target_pairs={{0,16},{8,24},{16,0},{24,8},{32,48},{40,56},{48,32},{56,40},{64,80... | collective-permute-start | bytes 245768 | tf_op jit(solution)/shard_map/ppermute | solution.py:423
  20.4 1.0 %merge_0_kept.1.after.own = bf16[192,1280]{1,0:T(8,128)(2,1)S(1)} custom-call(bf16[192,1280]{1,0:T(8,128)(2,1)S(1)} %compress_kept.1.own, bf16[192,1280]{1,0:T(8,128)(2,1)S(1)} %get-tuple-element.22.partner, bf16[512,768]{1,0:T(8,128)(2,1)S(1)} %get-tuple-element.21.bank), custom_call_target="tpu_custom_call" | custom-call | flops 1000 | bytes 1000 | tf_op jit(solution)/shard_map/merge_0_kept/pallas_call | solution.py:377
  21.4 1.6 %banks.1 = (bf16[512,768]{1,0:T(8,128)(2,1)S(1)}, bf16[256,768]{1,0:T(8,128)(2,1)S(1)}) custom-call(bf16[192,1280]{1,0:T(8,128)(2,1)S(1)} %merge_0_kept.1.after.own, f32[32,256]{1,0:T(8,128)S(1)} %get-tuple-element.24.weights, f32[32,128]{1,0:T(8,128)S(1)} %get-tuple-element.25.numbers), custom_call_target="tpu_custom_call" | custom-call | flops 1000 | bytes 1000 | tf_op jit(solution)/shard_map/banks/pallas_call | solution.py:309
  23.0 0.2 collective-permute-done.4.theirs
  23.2 0.8 %merge_1_sent.1 = (bf16[32,1152]{1,0:T(8,128)(2,1)S(1)}, bf16[192,1280]{1,0:T(8,128)(2,1)S(1)}) custom-call(bf16[192,1280]{1,0:T(8,128)(2,1)S(1)} %merge_0_kept.1.after.own, bf16[32,1280]{1,0:T(8,128)(2,1)S(1)} %collective-permute-done.4.theirs, bf16[512,768]{1,0:T(8,128)(2,1)S(1)} %get-tuple-element.26.bank), custom_call_target="tpu_custom_call" | custom-call | tf_op jit(solution)/shard_map/merge_1_sent/pallas_call | solution.py:366
  24.0 6.1 %collective-permute-start.5 = (bf16[32,1152]{1,0:T(8,128)(2,1)S(1)}, bf16[32,1152]{1,0:T(8,128)(2,1)S(1)}, u32[]{:S(2)}, u32[]{:S(2)}) collective-permute-start(bf16[32,1152]{1,0:T(8,128)(2,1)S(1)} %get-tuple-element.29), channel_id=1, source_target_pairs={{0,32},{8,40},{16,48},{24,56},{32,0},{40,8},{48,16},{56,24},{64,96... | collective-permute-start | bytes 221192 | tf_op jit(solution)/shard_map/ppermute | solution.py:423
  30.1 1.0 %merge_1_kept.1.own = bf16[192,1152]{1,0:T(8,128)(2,1)S(1)} custom-call(bf16[192,1280]{1,0:T(8,128)(2,1)S(1)} %merge_0_kept.1.after.own, bf16[192,1280]{1,0:T(8,128)(2,1)S(1)} %get-tuple-element.27.partner, bf16[512,768]{1,0:T(8,128)(2,1)S(1)} %get-tuple-element.26.bank), custom_call_target="tpu_custom_call" | custom-call | flops 1000 | bytes 1000 | tf_op jit(solution)/shard_map/merge_1_kept/pallas_call | solution.py:377
  31.1 1.4 %bank_and_part_2.1 = (bf16[512,768]{1,0:T(8,128)(2,1)S(1)}, f32[32,1152]{1,0:T(8,128)S(1)}) custom-call(bf16[192,1152]{1,0:T(8,128)(2,1)S(1)} %merge_1_kept.1.own, f32[32,256]{1,0:T(8,128)S(1)} %get-tuple-element.24.weights, f32[32,128]{1,0:T(8,128)S(1)} %get-tuple-element.25.numbers), custom_call_target="tpu_custom_call" | custom-call | flops 1000 | bytes 1000 | tf_op jit(solution)/shard_map/bank_and_part_2/pallas_call | solution.py:321
  32.5 1.3 %collective-permute-done.5.theirs = bf16[32,1152]{1,0:T(8,128)(2,1)S(1)} collective-permute-done((bf16[32,1152]{1,0:T(8,128)(2,1)S(1)}, bf16[32,1152]{1,0:T(8,128)(2,1)S(1)}, u32[]{:S(2)}, u32[]{:S(2)}) %collective-permute-start.5) | collective-permute-done | bytes 73760 | tf_op jit(solution)/shard_map/ppermute | solution.py:423
  33.8 0.6 %merge_2_sent.1 = (bf16[32,1152]{1,0:T(8,128)(2,1)S(1)}, bf16[192,1152]{1,0:T(8,128)(2,1)S(1)}) custom-call(f32[32,1152]{1,0:T(8,128)S(1)} %get-tuple-element.28.part, bf16[32,1152]{1,0:T(8,128)(2,1)S(1)} %collective-permute-done.5.theirs, bf16[512,768]{1,0:T(8,128)(2,1)S(1)} %get-tuple-element.30.bank), custom_call_target="tpu_custom_call" | custom-call | tf_op jit(solution)/shard_map/merge_2_sent/pallas_call | solution.py:366
  34.5 7.7 %collective-permute-start.6 = (bf16[32,1152]{1,0:T(8,128)(2,1)S(1)}, bf16[32,1152]{1,0:T(8,128)(2,1)S(1)}, u32[]{:S(2)}, u32[]{:S(2)}) collective-permute-start(bf16[32,1152]{1,0:T(8,128)(2,1)S(1)} %get-tuple-element.34), channel_id=1, source_target_pairs={{0,64},{8,72},{16,80},{24,88},{32,96},{40,104},{48,112},{56,120},{... | collective-permute-start | bytes 221192 | tf_op jit(solution)/shard_map/ppermute | solution.py:423
  42.2 0.9 %merge_2_kept.1.own = bf16[192,1152]{1,0:T(8,128)(2,1)S(1)} custom-call(bf16[192,1152]{1,0:T(8,128)(2,1)S(1)} %merge_1_kept.1.own, bf16[192,1152]{1,0:T(8,128)(2,1)S(1)} %get-tuple-element.31.partner, bf16[512,768]{1,0:T(8,128)(2,1)S(1)} %get-tuple-element.30.bank), custom_call_target="tpu_custom_call" | custom-call | flops 1000 | bytes 1000 | tf_op jit(solution)/shard_map/merge_2_kept/pallas_call | solution.py:377
  43.0 0.9 %own_parts_3.1.parts = f32[2,32,1152]{2,1,0:T(8,128)S(1)} custom-call(bf16[192,1152]{1,0:T(8,128)(2,1)S(1)} %merge_2_kept.1.own, bf16[256,768]{1,0:T(8,128)(2,1)S(1)} %get-tuple-element.32.low, bf16[256,768]{1,0:T(8,128)(2,1)S(1)} %get-tuple-element.33.high), custom_call_target="tpu_custom_call" | custom-call | flops 1000 | bytes 1000 | tf_op jit(solution)/shard_map/own_parts_3/pallas_call | solution.py:333
  44.0 0.8 %collective-permute-done.6.theirs = bf16[32,1152]{1,0:T(8,128)(2,1)S(1)} collective-permute-done((bf16[32,1152]{1,0:T(8,128)(2,1)S(1)}, bf16[32,1152]{1,0:T(8,128)(2,1)S(1)}, u32[]{:S(2)}, u32[]{:S(2)}) %collective-permute-start.6) | collective-permute-done | bytes 73760 | tf_op jit(solution)/shard_map/ppermute | solution.py:423
  44.7 1.7 %merge_last.1 = bf16[2,32,1024]{2,1,0:T(8,128)(2,1)} custom-call(f32[2,32,1152]{2,1,0:T(8,128)S(1)} %own_parts_3.1.parts, bf16[32,1152]{1,0:T(8,128)(2,1)S(1)} %collective-permute-done.6.theirs, bf16[256,768]{1,0:T(8,128)(2,1)S(1)} %get-tuple-element.32.low, bf16[256,768]{1,0:T(8,128)(2,1)S(1)} %get-tuple-element.33.high), custom_call_target="tpu_custom_call" | custom-call | tf_op jit(solution)/shard_map/merge_last/pallas_call | solution.py:389
  (9 shorter events, 0.0 us)
Async XLA Ops:
  0.0 7.7 %copy-start.4 = (s32[4,2,32]{2,1,0:T(2,128)S(1)}, s32[4,2,32]{2,1,0:T(2,128)}, u32[]{:S(2)}) copy-start(s32[4,2,32]{2,1,0:T(2,128)} %param.9) | copy-start | bytes 3076
  0.0 7.8 %copy-start.1 = (f32[4,2,2,32,16]{3,4,2,1,0:T(8,128)S(1)}, f32[4,2,2,32,16]{3,4,2,1,0:T(8,128)}, u32[]{:S(2)}) copy-start(f32[4,2,2,32,16]{3,4,2,1,0:T(8,128)} %param.8) | copy-start | bytes 98308
  0.9 6.9 %copy-start.3 = (s32[4,2,32]{2,1,0:T(2,128)S(1)}, s32[4,2,32]{2,1,0:T(2,128)}, u32[]{:S(2)}) copy-start(s32[4,2,32]{2,1,0:T(2,128)} %param.10) | copy-start | bytes 3076
  0.9 9.4 %collective-permute-start.2 = (bf16[2,32,384]{2,1,0:T(8,128)(2,1)S(1)}, bf16[2,32,384]{2,1,0:T(8,128)(2,1)S(1)}, u32[]{:S(2)}, u32[]{:S(2)}) collective-permute-start(bf16[2,32,384]{2,1,0:T(8,128)(2,1)S(1)} %get-tuple-element.35), channel_id=1, source_target_pairs={{5,4},{13,12},{21,20},{29,28},{37,36},{45,44},{53,52},{61,60},{69,... | collective-permute-start | bytes 147464 | tf_op jit(solution)/shard_map/ppermute | solution.py:413
  1.6 6.2 %copy-start.5 = (s32[4,32]{1,0:T(4,128)S(1)}, s32[4,32]{1,0:T(4,128)}, u32[]{:S(2)}) copy-start(s32[4,32]{1,0:T(4,128)} %param.11) | copy-start | bytes 1540
  1.6 8.7 %collective-permute-start = (bf16[2,32,384]{2,1,0:T(8,128)(2,1)S(1)}, bf16[2,32,384]{2,1,0:T(8,128)(2,1)S(1)}, u32[]{:S(2)}, u32[]{:S(2)}) collective-permute-start(bf16[2,32,384]{2,1,0:T(8,128)(2,1)S(1)} %get-tuple-element.36), channel_id=1, source_target_pairs={{1,2},{3,4},{5,6},{2,1},{4,3},{6,5},{9,10},{11,12},{13,14},{10,9},... | collective-permute-start | bytes 147464 | tf_op jit(solution)/shard_map/ppermute | solution.py:414
  5.8 6.0 %collective-permute-start.1 = (bf16[2,32,384]{2,1,0:T(8,128)(2,1)S(1)}, bf16[2,32,384]{2,1,0:T(8,128)(2,1)S(1)}, u32[]{:S(2)}, u32[]{:S(2)}) collective-permute-start(bf16[2,32,384]{2,1,0:T(8,128)(2,1)S(1)} %get-tuple-element.37), channel_id=1, source_target_pairs={{1,0},{0,1},{3,2},{2,3},{4,5},{7,6},{6,7},{9,8},{8,9},{11,10},{10,... | collective-permute-start | bytes 147464 | tf_op jit(solution)/shard_map/ppermute | solution.py:415
  7.8 0.7 %copy-start.2 = (bf16[2,512]{1,0:T(2,128)(2,1)S(1)}, bf16[2,512]{1,0:T(2,128)(2,1)}, u32[]{:S(2)}) copy-start(bf16[2,512]{1,0:T(2,128)(2,1)} %chirp.1) | copy-start | bytes 6148
  8.5 3.3 %copy-start = (bf16[2,32,1024]{2,1,0:T(8,128)(2,1)S(1)}, bf16[2,32,1024]{2,1,0:T(8,128)(2,1)}, u32[]{:S(2)}) copy-start(bf16[2,32,1024]{2,1,0:T(8,128)(2,1)} %echoes.3) | copy-start | bytes 393220
  12.2 3.2 %collective-permute-start.3 = (bf16[32,1280]{1,0:T(8,128)(2,1)S(1)}, bf16[32,1280]{1,0:T(8,128)(2,1)S(1)}, u32[]{:S(2)}, u32[]{:S(2)}) collective-permute-start(bf16[32,1280]{1,0:T(8,128)(2,1)S(1)} %compress_sent.1), channel_id=1, source_target_pairs={{0,8},{8,0},{16,24},{24,16},{32,40},{40,32},{48,56},{56,48},{64,72... | collective-permute-start | bytes 245768 | tf_op jit(solution)/shard_map/ppermute | solution.py:423
  16.2 7.0 %collective-permute-start.4 = (bf16[32,1280]{1,0:T(8,128)(2,1)S(1)}, bf16[32,1280]{1,0:T(8,128)(2,1)S(1)}, u32[]{:S(2)}, u32[]{:S(2)}) collective-permute-start(bf16[32,1280]{1,0:T(8,128)(2,1)S(1)} %get-tuple-element.23), channel_id=1, source_target_pairs={{0,16},{8,24},{16,0},{24,8},{32,48},{40,56},{48,32},{56,40},{64,80... | collective-permute-start | bytes 245768 | tf_op jit(solution)/shard_map/ppermute | solution.py:423
  24.0 9.8 %collective-permute-start.5 = (bf16[32,1152]{1,0:T(8,128)(2,1)S(1)}, bf16[32,1152]{1,0:T(8,128)(2,1)S(1)}, u32[]{:S(2)}, u32[]{:S(2)}) collective-permute-start(bf16[32,1152]{1,0:T(8,128)(2,1)S(1)} %get-tuple-element.29), channel_id=1, source_target_pairs={{0,32},{8,40},{16,48},{24,56},{32,0},{40,8},{48,16},{56,24},{64,96... | collective-permute-start | bytes 221192 | tf_op jit(solution)/shard_map/ppermute | solution.py:423
  34.5 10.3 %collective-permute-start.6 = (bf16[32,1152]{1,0:T(8,128)(2,1)S(1)}, bf16[32,1152]{1,0:T(8,128)(2,1)S(1)}, u32[]{:S(2)}, u32[]{:S(2)}) collective-permute-start(bf16[32,1152]{1,0:T(8,128)(2,1)S(1)} %get-tuple-element.34), channel_id=1, source_target_pairs={{0,64},{8,72},{16,80},{24,88},{32,96},{40,104},{48,112},{56,120},{... | collective-permute-start | bytes 221192 | tf_op jit(solution)/shard_map/ppermute | solution.py:423
